TPU v7x, 512 devices: a whole 4x8x8 slice. The times are simulated.
512 devices in a mesh: dp: 64 (over z, y_hi, core), feat: 8 (over y_lo, x).
Axes of the slice: x: 4, y: 8 (y_hi: 4, y_lo: 2; y = y_hi * 2 + y_lo), z: 8, core: 2. Of those that a mesh axis runs over, the one named last changes fastest.
Arguments:
- views: float32 [8192, 1536], P('dp', 'feat'), may hold values from -0.2 to 0.2
- partner: int32 [8192], P('dp'), may hold values from 0 to 8191, as said below
Outputs:
- loss: float32 [], replicated
- grad_views: float32 [8192, 1536], P('dp', 'feat')
Inputs may be any that keep to these rules, and one draw needn't show every extreme that they name: partner pairs the views: partner[partner[i]] == i and partner[i] != i.
All inputs are finite; a program needn't handle non-finite values.
Results may differ from a plain program's by a relative error of at most 0.0003.
Values sent between devices are 32-bit elements; how exact they have to be, the bound alone decides.
No kernel may reach another device: no remote copies, remote signals or barrier semaphores. Data moves between devices by JAX's collectives and lax.ppermute only.
A program may use at most 64 MiB of HBM per device.

v0:
```python
import jax
import jax.numpy as jnp
from jax import lax
from jax.sharding import PartitionSpec as P


def per_device(views, partner):
    inv_tau = 10.0
    rows_here = views.shape[0]
    norms_sq = lax.psum(jnp.sum(views * views, axis=1), "feat")
    scale = lax.rsqrt(norms_sq + 1e-06)
    units = views * scale[:, None]
    rows = lax.axis_index("dp") * rows_here + jnp.arange(rows_here, dtype=jnp.int32)
    total_rows = rows_here * lax.axis_size("dp")
    every = lax.all_gather(units, "dp", axis=0, tiled=True)
    partial_value = jnp.dot(units, every.T, precision=lax.Precision.HIGHEST)
    scores = lax.psum(partial_value, "feat") * inv_tau
    cols = jnp.arange(total_rows, dtype=jnp.int32)
    diag = cols[None, :] == rows[:, None]
    lse = jnp.log(jnp.sum(jnp.where(diag, 0.0, jnp.exp(scores)), axis=1))
    hit = cols[None, :] == partner[:, None]
    pos = jnp.sum(jnp.where(hit, scores, 0.0), axis=1)
    lse_all = lax.all_gather(lse, "dp", axis=0, tiled=True)
    both = jnp.exp(scores - lse[:, None]) + jnp.exp(scores - lse_all[None, :])
    weights = jnp.where(diag, 0.0, both) - 2.0 * hit.astype(jnp.float32)
    grad_units = jnp.dot(weights, every, precision=lax.Precision.HIGHEST) * inv_tau
    proj = lax.psum(jnp.sum(units * grad_units, axis=1), "feat")
    grad_views = (grad_units - units * proj[:, None]) * scale[:, None]
    loss = lax.psum(jnp.sum(lse - pos), "dp") / total_rows
    return (loss, grad_views)


def solution(mesh):
    return jax.shard_map(
        per_device,
        mesh=mesh,
        in_specs=(P("dp", "feat"), P("dp")),
        out_specs=(P(), P("dp", "feat")),
        check_vma=False,
    )
```

profile of v0, /device:TPU:1, one launch (start us, length us, event | category | flops | bytes accessed | tf_op | source)
XLA Modules:
  0.0 510.0 jit_solution(17717270864826665138)
XLA Ops:
  7.2 0.0 all-gather.3.cloned.1.call-start
  7.2 0.9 multiply_reduce_fusion.1
  8.1 16.8 %psum.28 = f32[128]{0:T(128)S(1)} all-reduce(f32[128]{0:T(128)S(1)} %multiply_reduce_fusion.1), channel_id=1, replica_groups=mesh['dp'=64,'feat'=8] {'feat'}, use_global_device_ids=true, to_apply=%region_1.0 | all-reduce | flops 128 | bytes 1024 | tf_op jit(solution)/shard_map/psum | solution.py:10
  24.9 1.5 broadcast_multiply_fusion
  26.5 0.0 all-gather.3.cloned.1.call-update
  26.5 0.0 all-reduce.2.cloned.1.call-start
  26.6 101.4 %all-gather.3.cloned.1.call-done = f32[8192,192]{0,1:T(8,128)} async-done(((f32[128,192]{0,1:T(8,128)}), f32[8192,192]{0,1:T(8,128)}) %all-gather.3.cloned.1.call-update) | async-done | bytes 6291472 | tf_op jit(solution)/shard_map/all_gather | solution.py:15
  127.9 8.9 %fusion.24 = f32[128,8192]{1,0:T(8,128)} fusion(f32[128,192]{0,1:T(8,128)} %broadcast_multiply_fusion, f32[8192,192]{0,1:T(8,128)} %all-gather.3.cloned.1.call-done), kind=kOutput, calls=%fused_computation.34 | convolution fusion | flops 2415919104 | bytes 10584064 | tf_op jit(solution)/shard_map/dot_general | solution.py:16
  136.8 0.0 copy-start.3
  136.8 0.0 copy-start.1
  136.9 0.0 all-reduce.2.cloned.1.call-update
  136.9 110.7 %all-reduce.2.cloned.1.call-done = f32[128,8192]{1,0:T(8,128)} async-done(((f32[128,8192]{1,0:T(8,128)}), f32[128,8192]{1,0:T(8,128)}) %all-reduce.2.cloned.1.call-update) | async-done | bytes 4194320 | tf_op jit(solution)/shard_map/psum | solution.py:17
  247.5 0.0 copy-done.3
  247.5 0.0 copy-start
  247.6 4.1 select_reduce_fusion.1
  251.7 0.6 fusion.23
  252.3 82.5 %all-gather = f32[64,1,128]{2,1,0:T(1,128)S(1)} all-gather(f32[1,1,128]{2,1,0:T(1,128)S(1)} %get-tuple-element.6), channel_id=1, replica_groups=mesh['dp'=64,'feat'=8] {'dp'}, dimensions={0}, use_global_device_ids=true | all-gather | bytes 33280 | tf_op jit(solution)/shard_map/all_gather | solution.py:23
  334.8 0.0 copy-done.1
  334.8 0.0 copy-done
  334.9 0.0 copy-start.2
  334.9 9.8 %multiply_reduce_fusion = (f32[128]{0:T(128)S(1)}, f32[128,192]{0,1:T(8,128)S(1)}) fusion(f32[128,192]{0,1:T(8,128)S(1)} %copy-done.1, f32[8192,192]{0,1:T(8,128)} %all-gather.3.cloned.1.call-done, f32[128,8192]{1,0:T(8,128)S(1)} %copy-done, f32[8192]{0:T(1024)S(1)} %bitcast.6, f32[128]{0:T(128)S(1)} %get-tuple-element.4, s32[128]{0:T(128)S(1)} %copy-done.3, ...), kind=kOutput, calls=%fused_computation.23 | convolution fusion | flops 2425430016 | bytes 10717184 | tf_op jit(solution)/shard_map/dot_general | solution.py:26
  344.7 13.7 %psum.31 = f32[128]{0:T(128)S(1)} all-reduce(f32[128]{0:T(128)S(1)} %get-tuple-element.7), channel_id=1, replica_groups=mesh['dp'=64,'feat'=8] {'feat'}, use_global_device_ids=true, to_apply=%region_8.9 | all-reduce | flops 128 | bytes 1024 | tf_op jit(solution)/shard_map/psum | solution.py:27
  358.4 142.4 %psum.30 = f32[]{:T(128)} all-reduce(f32[]{:T(128)} %get-tuple-element.5), channel_id=1, replica_groups=mesh['dp'=64,'feat'=8] {'dp'}, use_global_device_ids=true, to_apply=%region_6.7 | all-reduce | flops 1 | bytes 8 | tf_op jit(solution)/shard_map/psum | solution.py:29
  500.7 0.0 copy-done.2
  500.7 0.7 subtract_multiply_fusion
  (2 shorter events, 0.0 us)
Async XLA Ops:
  7.2 120.8 %all-gather.3.cloned.1.call-start = ((), (), s32[]{:S(2)}) async-start(), calls=%async_computation | async-start | bytes 6389760 | tf_op jit(solution)/shard_map/all_gather | solution.py:15
  26.5 221.0 %all-reduce.2.cloned.1.call-start = ((), (), s32[]{:S(2)}) async-start(), calls=%async_computation.1 | async-start | bytes 8388608 | tf_op jit(solution)/shard_map/psum | solution.py:17
  136.8 110.7 %copy-start.3 = (s32[128]{0:T(128)S(1)}, s32[128]{0:T(128)}, u32[]{:S(2)}) copy-start(s32[128]{0:T(128)} %param.3) | copy-start | bytes 1540
  136.8 198.0 %copy-start.1 = (f32[128,192]{0,1:T(8,128)S(1)}, f32[128,192]{0,1:T(8,128)}, u32[]{:S(2)}) copy-start(f32[128,192]{0,1:T(8,128)} %broadcast_multiply_fusion) | copy-start | bytes 294916
  247.5 87.3 %copy-start = (f32[128,8192]{1,0:T(8,128)S(1)}, f32[128,8192]{1,0:T(8,128)}, u32[]{:S(2)}) copy-start(f32[128,8192]{1,0:T(8,128)} %all-reduce.2.cloned.1.call-done) | copy-start | bytes 12582916
  334.9 165.9 %copy-start.2 = (f32[128,192]{0,1:T(8,128)S(1)}, f32[128,192]{0,1:T(8,128)}, u32[]{:S(2)}) copy-start(f32[128,192]{0,1:T(8,128)} %param.2) | copy-start | bytes 294916
Sparse Core Ops, SparseCore 0:
  26.6 101.2 all-gather.2
  137.0 110.5 all-reduce.1
where the time goes:
time: 510 us
  blocking collectives  255 us (50%)
  waiting for transfers between devices  212 us (42%)
  matrix products  18.8 us (4%)
  between operations  15.8 us (3%)
  other arithmetic  7.9 us (2%)
    psum x1, blocking collectives, per_device(): loss = lax.psum(jnp.sum(lse - pos), 'dp') / total_rows  142 us
    psum x1, waiting for transfers between devices, per_device(): scores = lax.psum(partial_value, 'feat') * inv_tau  111 us
    all_gather x1, waiting for transfers between devices, per_device(): every = lax.all_gather(units, 'dp', axis=0, tiled=True)  101 us
    all_gather x1, blocking collectives, per_device(): lse_all = lax.all_gather(lse, 'dp', axis=0, tiled=True)  82.5 us
    psum x1, blocking collectives, per_device(): norms_sq = lax.psum(jnp.sum(views * views, axis=1), 'feat')  16.8 us
    psum x1, blocking collectives, per_device(): proj = lax.psum(jnp.sum(units * grad_units, axis=1), 'feat')  13.7 us
  transfers between devices with their start and end apart: 2, of which 2 were waited for; matrix products, arithmetic and copies ran while one was open for 0% of the time, Pallas kernels for 0%

commit v1 on v0

v1 whole, which is shorter than its diff:
```python
import jax
import jax.numpy as jnp
from jax import lax
from jax.experimental import pallas as pl
from jax.experimental.pallas import tpu as pltpu
from jax.sharding import Mesh, PartitionSpec as P

NZ, NYH, NC, NYL, NX = 8, 4, 2, 2, 4
NF = NYL * NX
ROWS = 128
FEAT = 192
WIDE = NF * FEAT
CHUNK = ROWS // NF
NCOL = NZ * NYH * CHUNK
PIECE = FEAT + 8
TOTAL = 8192
INV_TAU = 10.0
VMEM = pl.BlockSpec(memory_space=pltpu.VMEM)
SMEM = pl.BlockSpec(memory_space=pltpu.SMEM)
PARAMS = pltpu.CompilerParams(vmem_limit_bytes=48 * 1024 * 1024)


def f32(*shape):
    return jax.ShapeDtypeStruct(shape, jnp.float32)


def split(x):
    hi = x.astype(jnp.bfloat16)
    lo = (x - hi.astype(jnp.float32)).astype(jnp.bfloat16)
    return hi, lo


def dot3(a, b, dims):
    def one(x, y):
        return lax.dot_general(x, y, (dims, ((), ())), preferred_element_type=jnp.float32)
    return one(a[0], b[0]) + (one(a[0], b[1]) + one(a[1], b[0]))


def column(x):
    return jnp.broadcast_to(x, (ROWS, ROWS)).T[:, :1]


def pack(x):
    half = CHUNK // 2
    return jnp.concatenate([x[:, :ROWS], jnp.concatenate([x[:half, ROWS:], x[half:, ROWS:]], axis=1)], axis=0)


def unpack(x):
    tail = x[CHUNK:, :]
    rest = FEAT - ROWS
    return jnp.concatenate([x[:CHUNK, :], jnp.concatenate([tail[:, :rest], tail[:, rest:]], axis=0)], axis=1)


def chunk_kernel(view_ref, out_ref):
    x = view_ref[...].T
    for f in range(NF):
        piece = pack(x[f * CHUNK:(f + 1) * CHUNK, :])
        for y in range(NYH):
            out_ref[y * NF + f] = piece


def column_kernel(piece_ref, view_ref, unit_ref, copies_ref):
    for y in range(NYH):
        x = jnp.concatenate([unpack(piece_ref[y * NF + f]) for f in range(NF)], axis=1)
        scale = lax.rsqrt(jnp.sum(x * x, axis=1, keepdims=True) + 1e-06)
        unit_ref[y * CHUNK:(y + 1) * CHUNK, :] = x * scale
    for f in range(NF):
        copies_ref[f] = view_ref[...]


def norm_kernel(piece_ref, unit_ref, scale_ref):
    x = piece_ref[...].reshape(WIDE, ROWS)
    scale = lax.rsqrt(jnp.sum(x * x, axis=0, keepdims=True) + 1e-06)
    scale_ref[...] = scale
    unit_ref[...] = (x * scale).T


def tile_masks(pos_ref, half, part):
    zy, core, me = pos_ref[0], pos_ref[1], pos_ref[2]
    lane = lax.broadcasted_iota(jnp.int32, (1, NCOL), 1)
    col = ((lane // CHUNK) * NC + core) * ROWS + me * CHUNK + lane % CHUNK
    row = (zy * NC + half) * ROWS + lax.broadcasted_iota(jnp.int32, (ROWS, 1), 0)
    return col == row, col == part


def score_kernel(pos_ref, own_ref, oth_ref, cols_ref, ownp_ref, othp_ref, s_ref, row_ref, col_ref, hi, lo):
    core = pos_ref[1]
    for j, ref in enumerate((own_ref, oth_ref)):
        hi[j], lo[j] = split(ref[...])
    rows = (hi[...].reshape(NC * ROWS, WIDE), lo[...].reshape(NC * ROWS, WIDE))
    step = 256
    for c in range(0, NCOL, step):
        s_ref[:, c:c + step] = INV_TAU * dot3(rows, split(cols_ref[c:c + step, :]), ((1,), (1,)))
    colsum = jnp.zeros((1, NCOL), jnp.float32)
    pos = jnp.zeros((1, ROWS), jnp.float32)
    sums = []
    for j, part in enumerate((ownp_ref, othp_ref)):
        s = s_ref[j * ROWS:(j + 1) * ROWS, :]
        diag, hit = tile_masks(pos_ref, core ^ j, part[...])
        e = jnp.where(diag, 0.0, jnp.exp(s))
        colsum = colsum + jnp.sum(e, axis=0, keepdims=True)
        lanes = e[:, :ROWS]
        hits = jnp.sum(jnp.where(hit, s, 0.0), axis=0, keepdims=True)
        for c in range(NCOL // ROWS):
            pos = pos + hits[:, c * ROWS:(c + 1) * ROWS]
            if c:
                lanes = lanes + e[:, c * ROWS:(c + 1) * ROWS]
        sums.append(jnp.sum(lanes.T, axis=0, keepdims=True))
    first = core == 0
    row = jnp.concatenate([jnp.where(first, sums[0], sums[1]), jnp.where(first, sums[1], sums[0]),
                           jnp.zeros((8 - NC, ROWS), jnp.float32)], axis=0)
    nrow = NCOL // ROWS
    col = jnp.concatenate([colsum[:, c * ROWS:(c + 1) * ROWS] for c in range(nrow)]
                          + [pos, jnp.zeros((7 - nrow, ROWS), jnp.float32)], axis=0)
    for k in range(NC * NF):
        row_ref[k] = row
    for k in range(NZ * NYH):
        col_ref[k] = col


def grad_kernel(pos_ref, s_ref, own_ref, oth_ref, cols_ref, ownp_ref, othp_ref, rows_ref, cols_l_ref, mine_ref, theirs_ref, w_hi, w_lo):
    core = pos_ref[1]
    row_l = jnp.sum(rows_ref[...], axis=0)
    col_l = jnp.sum(cols_l_ref[...], axis=0)
    nrow = NCOL // ROWS
    col_inv = jnp.concatenate([1.0 / col_l[c:c + 1, :] for c in range(nrow)], axis=1)
    loss = jnp.sum(jnp.log(col_l[:nrow, :]), axis=0, keepdims=True) - col_l[nrow:nrow + 1, :]
    projs = []
    for j, part in enumerate((ownp_ref, othp_ref)):
        s = s_ref[j * ROWS:(j + 1) * ROWS, :]
        half = core ^ j
        diag, hit = tile_masks(pos_ref, half, part[...])
        inv = column(1.0 / jnp.where(half == 0, row_l[0:1, :], row_l[1:2, :]))
        w = jnp.where(diag, 0.0, jnp.exp(s) * (inv + col_inv)) - jnp.where(hit, 2.0, 0.0)
        projs.append(jnp.sum(w * s, axis=1, keepdims=True))
        w_hi[j], w_lo[j] = split(w)
    weights = (w_hi[...].reshape(NC * ROWS, NCOL), w_lo[...].reshape(NC * ROWS, NCOL))
    step = 2 * FEAT
    tail = jnp.concatenate([loss, jnp.zeros((7, ROWS), jnp.float32)], axis=0)
    for c in range(WIDE // step):
        at = slice(c * step, (c + 1) * step)
        g = INV_TAU * dot3(weights, split(cols_ref[:, at]), ((1,), (0,)))
        for j, (units, out) in enumerate(((own_ref, mine_ref), (oth_ref, theirs_ref))):
            t = (g[j * ROWS:(j + 1) * ROWS, :] - units[:, at] * projs[j]).T
            for p in range(2):
                out[2 * c + p, :FEAT, :] = t[p * FEAT:(p + 1) * FEAT, :]
                out[2 * c + p, FEAT:, :] = tail


def last_kernel(piece_ref, scale_ref, loss_ref, grad_ref):
    total = jnp.sum(piece_ref[...], axis=0)
    loss_ref[...] = jnp.sum(total[FEAT:FEAT + 1, :], axis=1, keepdims=True) / TOTAL
    grad_ref[...] = total[:FEAT, :] * scale_ref[...]


def swap(x, axes, size, k):
    return lax.ppermute(x, axes, [(i, i ^ k) for i in range(size)])


def trade(x, axes):
    return lax.all_to_all(x, axes, 0, 0, tiled=True)


def call(body, name, outs, args, scratch=()):
    return pl.pallas_call(
        body,
        out_shape=outs,
        in_specs=[SMEM if a.shape == (3,) else VMEM for a in args],
        out_specs=[VMEM] * len(outs),
        scratch_shapes=list(scratch),
        compiler_params=PARAMS,
        name=name,
    )(*args)


def per_device(views, partner):
    zy = lax.axis_index(("z", "yh"))
    core = lax.axis_index("core")
    me = lax.axis_index(("yl", "x"))
    pos = jnp.stack([zy, core, me]).astype(jnp.int32)
    feat = ("yl", "x")

    own_p = partner.reshape(ROWS, 1)
    oth_p = swap(partner, "core", NC, 1).reshape(ROWS, 1)
    packed = CHUNK * FEAT // ROWS
    chunks, = call(chunk_kernel, "chunks", [f32(NYH * NF, packed, ROWS)], [views.T])
    chunks = trade(chunks, ("yh", "yl", "x"))
    chunk, copies = call(column_kernel, "columns", [f32(NYH * CHUNK, WIDE), f32(NF, FEAT, ROWS)], [chunks, views.T])
    cols = lax.all_gather(chunk, "z", axis=0, tiled=True)
    own, scale = call(norm_kernel, "norm", [f32(ROWS, WIDE), f32(1, ROWS)], [trade(copies, feat)])
    oth = swap(own, "core", NC, 1)
    s, row, col = call(
        score_kernel, "scores",
        [f32(NC * ROWS, NCOL), f32(NC * NF, 8, ROWS), f32(NZ * NYH, 8, ROWS)],
        [pos, own, oth, cols, own_p, oth_p],
        [pltpu.VMEM((NC, ROWS, WIDE), jnp.bfloat16)] * 2,
    )
    rows_l = trade(row, ("core", "yl", "x"))
    cols_l = trade(col, ("z", "yh"))
    mine, theirs = call(
        grad_kernel, "gradient",
        [f32(NF, PIECE, ROWS)] * 2,
        [pos, s, own, oth, cols, own_p, oth_p, rows_l, cols_l],
        [pltpu.VMEM((NC, ROWS, NCOL), jnp.bfloat16)] * 2,
    )
    pieces = trade(mine + swap(theirs, "core", NC, 1), feat)
    loss, grad = call(last_kernel, "finish", [f32(1, 1), f32(FEAT, ROWS)], [pieces, scale])
    return loss.reshape(()), grad.T


def solution(mesh):
    fine = Mesh(mesh.devices.reshape(NZ, NYH, NC, NYL, NX), ("z", "yh", "core", "yl", "x"))
    rows = ("z", "yh", "core")
    return jax.shard_map(
        per_device,
        mesh=fine,
        in_specs=(P(rows, ("yl", "x")), P(rows)),
        out_specs=(P(), P(rows, ("yl", "x"))),
        check_vma=False,
    )
```

time: 510 us -> 151 us (0.30)
  waiting for transfers between devices: 212 us -> 29.8 us
  blocking collectives: 255 us -> 83.3 us
  matrix products: 18.8 us -> 0 us
  starting transfers between devices: 0.08 us -> 11.8 us
  Pallas kernels: 0 us -> 8.87 us
  other arithmetic: 7.9 us -> 0.16 us
    psum x3 -> x0, blocking collectives: 173 us -> none  [the longest x1 142 us: per_device(): loss = lax.psum(jnp.sum(lse - pos), 'dp') / total_rows]
    psum x1 -> x0, waiting for transfers between devices: 111 us -> none  [per_device(): scores = lax.psum(partial_value, 'feat') * inv_tau]
    all_to_all x0 -> x5, blocking collectives: none -> 83.3 us  [trade(): return lax.all_to_all(x, axes, 0, 0, tiled=True)]
    all_gather x1 -> x0, blocking collectives: 82.5 us -> none  [per_device(): lse_all = lax.all_gather(lse, 'dp', axis=0, tiled=True)]
    all_gather x1, waiting for transfers between devices: 101 us -> 27 us  [per_device(): cols = lax.all_gather(chunk, 'z', axis=0, tiled=True)]
    dot_general x2 -> x0, matrix products: 18.8 us -> none  [the longest x1 9.83 us: per_device(): jnp.dot(weights, every, precision=lax.Precision.HIGHEST) * inv_tau]
    ppermute x0 -> x3, starting transfers between devices: none -> 11.7 us  [swap(): return lax.ppermute(x, axes, [(i, i ^ k) for i in range(size)])]
    pallas_call x0 -> x6, Pallas kernels: none -> 8.87 us  [call(): pl.pallas_call(body, out_shape=outs, in_specs=[SMEM if a.shape == (3,) el...]
  transfers between devices with their start and end apart: 2 -> 4, of which waited for: 2 -> 3; matrix products, arithmetic and copies ran while one was open for 0% -> 0% of each run, Pallas kernels for 0% -> 0%
where the time goes in v1:
time: 151 us
  blocking collectives  83.3 us (55%)
  waiting for transfers between devices  29.8 us (20%)
  between operations  14.1 us (9%)
  starting transfers between devices  11.8 us (8%)
  Pallas kernels  8.87 us (6%)
  local copies, waits for them, and re-layouts  3 us (2%)
    all_to_all x5, blocking collectives, trade(): return lax.all_to_all(x, axes, 0, 0, tiled=True)  83.3 us
    all_gather x1, waiting for transfers between devices, per_device(): cols = lax.all_gather(chunk, 'z', axis=0, tiled=True)  27 us
    ppermute x3, starting transfers between devices, swap(): return lax.ppermute(x, axes, [(i, i ^ k) for i in range(size)])  11.7 us
    pallas_call x6, Pallas kernels, call(): pl.pallas_call(body, out_shape=outs, in_specs=[SMEM if a.shape == (3,) el...  8.87 us
  transfers between devices with their start and end apart: 4, of which 3 were waited for; matrix products, arithmetic and copies ran while one was open for 0% of the time, Pallas kernels for 0%

profile of v1, /device:TPU:1, one launch (start us, length us, event | category | flops | bytes accessed | tf_op | source)
XLA Modules:
  0.0 151.0 jit_solution(2088030485339338765)
XLA Ops:
  7.2 0.0 copy-start.2
  7.2 0.0 all-gather.2.cloned.1.call-start
  7.2 0.0 copy-start.1
  7.2 0.9 copy-done.1
  8.1 0.2 chunks.1
  8.3 24.1 %all_to_all.25.piece_ref = f32[32,24,128]{2,1,0:T(8,128)S(1)} all-to-all(f32[32,24,128]{2,1,0:T(8,128)S(1)} %chunks.1), channel_id=1, replica_groups=mesh['z'=8,'yh'=4,'core'=2,'yl'=2,'x'=4] {'yh','yl','x'}, dimensions={0} | all-to-all | bytes 786432 | tf_op jit(solution)/shard_map/all_to_all | solution.py:161
  32.4 1.1 columns.1
  33.4 0.0 all-gather.2.cloned.1.call-update
  33.5 12.9 %all_to_all.26.piece_ref = f32[8,192,128]{2,1,0:T(8,128)S(1)} all-to-all(f32[8,192,128]{2,1,0:T(8,128)S(1)} %get-tuple-element.13), channel_id=1, replica_groups=mesh['z'=8,'yh'=4,'core'=2,'yl'=2,'x'=4] {'yl','x'}, dimensions={0} | all-to-all | bytes 1572864 | tf_op jit(solution)/shard_map/all_to_all | solution.py:161
  46.3 0.5 norm.1
  46.8 5.9 %collective-permute-start = (f32[128,1536]{1,0:T(8,128)S(1)}, f32[128,1536]{1,0:T(8,128)S(1)}, u32[]{:S(2)}, u32[]{:S(2)}) collective-permute-start(f32[128,1536]{1,0:T(8,128)S(1)} %get-tuple-element.14.own_ref), channel_id=1, source_target_pairs={{0,8},{8,0},{1,9},{9,1},{2,10},{10,2},{3,11},{11,3},{4,12},{12,4},... | collective-permute-start | bytes 2359304 | tf_op jit(solution)/shard_map/ppermute | solution.py:157
  52.7 0.0 copy-done.2
  52.7 1.9 %collective-permute-start.1 = (s32[128]{0:T(128)S(1)}, s32[128]{0:T(128)S(1)}, u32[]{:S(2)}, u32[]{:S(2)}) collective-permute-start(s32[128]{0:T(128)S(1)} %copy-done.2), channel_id=1, source_target_pairs={{0,8},{8,0},{1,9},{9,1},{2,10},{10,2},{3,11},{11,3},{4,12},{12,4},... | collective-permute-start | bytes 1544 | tf_op jit(solution)/shard_map/ppermute | solution.py:157
  54.7 0.1 pad_add_fusion.pos_ref
  54.8 0.1 copy.4.ownp_ref
  54.9 0.9 collective-permute-done.1
  55.8 0.1 copy.5.othp_ref
  55.9 0.0 collective-permute-done.oth_ref
  55.9 27.0 %all-gather.2.cloned.1.call-done.cols_ref = f32[512,1536]{1,0:T(8,128)} async-done(((f32[64,1536]{1,0:T(8,128)}), f32[512,1536]{1,0:T(8,128)}) %all-gather.2.cloned.1.call-update) | async-done | bytes 3145744 | tf_op jit(solution)/shard_map/all_gather | solution.py:189
  82.8 0.0 copy-start
  82.8 1.9 %copy-done = f32[512,1536]{1,0:T(8,128)S(1)} copy-done((f32[512,1536]{1,0:T(8,128)S(1)}, f32[512,1536]{1,0:T(8,128)}, u32[]{:S(2)}) %copy-start) | copy-done | bytes 3145752
  84.7 2.3 %scores.1 = (f32[256,512]{1,0:T(8,128)S(1)}, f32[16,8,128]{2,1,0:T(8,128)S(1)}, f32[32,8,128]{2,1,0:T(8,128)S(1)}) custom-call(s32[3]{0:T(128)S(1)} %pad_add_fusion.pos_ref, f32[128,1536]{1,0:T(8,128)S(1)} %get-tuple-element.14.own_ref, f32[128,1536]{1,0:T(8,128)S(1)} %collective-permute-done.oth_ref, f32[512,1536]{1,0:T(8,128)S(1)} %copy-done, ...), custom_call_target="tpu_custom_call" | custom-call | tf_op jit(solution)/shard_map/scores/pallas_call | solution.py:165
  87.1 11.5 %all_to_all.27.rows_ref = f32[16,8,128]{2,1,0:T(8,128)S(1)} all-to-all(f32[16,8,128]{2,1,0:T(8,128)S(1)} %get-tuple-element.17), channel_id=1, replica_groups=mesh['z'=8,'yh'=4,'core'=2,'yl'=2,'x'=4] {'core','yl','x'}, dimensions={0} | all-to-all | bytes 131072 | tf_op jit(solution)/shard_map/all_to_all | solution.py:161
  98.6 19.3 %all_to_all.28.cols_l_ref = f32[32,8,128]{2,1,0:T(8,128)S(1)} all-to-all(f32[32,8,128]{2,1,0:T(8,128)S(1)} %get-tuple-element.18), channel_id=1, replica_groups=mesh['z'=8,'yh'=4,'core'=2,'yl'=2,'x'=4] {'z','yh'}, dimensions={0} | all-to-all | bytes 262144 | tf_op jit(solution)/shard_map/all_to_all | solution.py:161
  117.9 4.2 %gradient.1 = (f32[8,200,128]{2,1,0:T(8,128)S(1)}, f32[8,200,128]{2,1,0:T(8,128)S(1)}) custom-call(s32[3]{0:T(128)S(1)} %pad_add_fusion.pos_ref, f32[256,512]{1,0:T(8,128)S(1)} %get-tuple-element.16.s_ref, f32[128,1536]{1,0:T(8,128)S(1)} %get-tuple-element.14.own_ref, f32[128,1536]{1,0:T(8,128)S(1)} %collective-permute-done.oth_ref, ...), custom_call_target="tpu_custom_call" | custom-call | tf_op jit(solution)/shard_map/gradient/pallas_call | solution.py:165
  122.0 3.9 %collective-permute-start.2 = (f32[8,200,128]{2,1,0:T(8,128)S(1)}, f32[8,200,128]{2,1,0:T(8,128)S(1)}, u32[]{:S(2)}, u32[]{:S(2)}) collective-permute-start(f32[8,200,128]{2,1,0:T(8,128)S(1)} %get-tuple-element.20), channel_id=1, source_target_pairs={{0,8},{8,0},{1,9},{9,1},{2,10},{10,2},{3,11},{11,3},{4,12},{12,4},... | collective-permute-start | bytes 2457608 | tf_op jit(solution)/shard_map/ppermute | solution.py:157
  126.0 1.9 %collective-permute-done.2 = f32[8,200,128]{2,1,0:T(8,128)S(1)} collective-permute-done((f32[8,200,128]{2,1,0:T(8,128)S(1)}, f32[8,200,128]{2,1,0:T(8,128)S(1)}, u32[]{:S(2)}, u32[]{:S(2)}) %collective-permute-start.2) | collective-permute-done | bytes 819232 | tf_op jit(solution)/shard_map/ppermute | solution.py:157
  127.9 0.1 add.11
  128.0 15.5 %all_to_all.29.piece_ref = f32[8,200,128]{2,1,0:T(8,128)S(1)} all-to-all(f32[8,200,128]{2,1,0:T(8,128)S(1)} %add.11), channel_id=1, replica_groups=mesh['z'=8,'yh'=4,'core'=2,'yl'=2,'x'=4] {'yl','x'}, dimensions={0} | all-to-all | bytes 1638400 | tf_op jit(solution)/shard_map/all_to_all | solution.py:161
  143.5 0.7 finish.1
Async XLA Ops:
  7.2 45.6 %copy-start.2 = (s32[128]{0:T(128)S(1)}, s32[128]{0:T(128)}, u32[]{:S(2)}) copy-start(s32[128]{0:T(128)} %param.3) | copy-start | bytes 1540
  7.2 75.7 %all-gather.2.cloned.1.call-start = ((), (), s32[]{:S(2)}) async-start(), calls=%async_computation.5 | async-start | bytes 3538944 | tf_op jit(solution)/shard_map/all_gather | solution.py:189
  7.2 0.9 copy-start.1
  46.8 9.1 %collective-permute-start = (f32[128,1536]{1,0:T(8,128)S(1)}, f32[128,1536]{1,0:T(8,128)S(1)}, u32[]{:S(2)}, u32[]{:S(2)}) collective-permute-start(f32[128,1536]{1,0:T(8,128)S(1)} %get-tuple-element.14.own_ref), channel_id=1, source_target_pairs={{0,8},{8,0},{1,9},{9,1},{2,10},{10,2},{3,11},{11,3},{4,12},{12,4},... | collective-permute-start | bytes 2359304 | tf_op jit(solution)/shard_map/ppermute | solution.py:157
  52.7 3.0 %collective-permute-start.1 = (s32[128]{0:T(128)S(1)}, s32[128]{0:T(128)S(1)}, u32[]{:S(2)}, u32[]{:S(2)}) collective-permute-start(s32[128]{0:T(128)S(1)} %copy-done.2), channel_id=1, source_target_pairs={{0,8},{8,0},{1,9},{9,1},{2,10},{10,2},{3,11},{11,3},{4,12},{12,4},... | collective-permute-start | bytes 1544 | tf_op jit(solution)/shard_map/ppermute | solution.py:157
  82.8 1.9 %copy-start = (f32[512,1536]{1,0:T(8,128)S(1)}, f32[512,1536]{1,0:T(8,128)}, u32[]{:S(2)}) copy-start(f32[512,1536]{1,0:T(8,128)} %all-gather.2.cloned.1.call-done.cols_ref) | copy-start | bytes 9437188
  122.0 5.9 %collective-permute-start.2 = (f32[8,200,128]{2,1,0:T(8,128)S(1)}, f32[8,200,128]{2,1,0:T(8,128)S(1)}, u32[]{:S(2)}, u32[]{:S(2)}) collective-permute-start(f32[8,200,128]{2,1,0:T(8,128)S(1)} %get-tuple-element.20), channel_id=1, source_target_pairs={{0,8},{8,0},{1,9},{9,1},{2,10},{10,2},{3,11},{11,3},{4,12},{12,4},... | collective-permute-start | bytes 2457608 | tf_op jit(solution)/shard_map/ppermute | solution.py:157
Sparse Core Ops, SparseCore 0:
  33.6 49.2 all-gather.1

commit v2 on v1

--- a/solution.py
+++ b/solution.py
@@ -13,11 +13,13 @@
 CHUNK = ROWS // NF
 NCOL = NZ * NYH * CHUNK
 PIECE = FEAT + 8
+PACKED = CHUNK * FEAT // ROWS
 TOTAL = 8192
 INV_TAU = 10.0
 VMEM = pl.BlockSpec(memory_space=pltpu.VMEM)
 SMEM = pl.BlockSpec(memory_space=pltpu.SMEM)
-PARAMS = pltpu.CompilerParams(vmem_limit_bytes=48 * 1024 * 1024)
+HBM = pl.BlockSpec(memory_space=pltpu.HBM)
+PARAMS = pltpu.CompilerParams(vmem_limit_bytes=20 * 1024 * 1024)
 
 
 def f32(*shape):
@@ -54,14 +56,21 @@
 def chunk_kernel(view_ref, out_ref):
     x = view_ref[...].T
     for f in range(NF):
-        piece = pack(x[f * CHUNK:(f + 1) * CHUNK, :])
+        low, across = f // NX, f % NX
+        out_ref[across, low * PACKED:(low + 1) * PACKED, :] = pack(x[f * CHUNK:(f + 1) * CHUNK, :])
+
+
+def half_kernel(piece_ref, out_ref):
+    for low in range(NYL):
+        at = slice(low * PACKED, (low + 1) * PACKED)
+        x = jnp.concatenate([unpack(piece_ref[k, at, :]) for k in range(NX)], axis=1)
         for y in range(NYH):
-            out_ref[y * NF + f] = piece
+            out_ref[y * NYL + low] = x
 
 
 def column_kernel(piece_ref, view_ref, unit_ref, copies_ref):
     for y in range(NYH):
-        x = jnp.concatenate([unpack(piece_ref[y * NF + f]) for f in range(NF)], axis=1)
+        x = jnp.concatenate([piece_ref[y * NYL + low] for low in range(NYL)], axis=1)
         scale = lax.rsqrt(jnp.sum(x * x, axis=1, keepdims=True) + 1e-06)
         unit_ref[y * CHUNK:(y + 1) * CHUNK, :] = x * scale
     for f in range(NF):
@@ -83,14 +92,24 @@
     return col == row, col == part
 
 
-def score_kernel(pos_ref, own_ref, oth_ref, cols_ref, ownp_ref, othp_ref, s_ref, row_ref, col_ref, hi, lo):
+def score_kernel(pos_ref, own_ref, oth_ref, cols_hbm, ownp_ref, othp_ref, s_ref, row_ref, col_ref, chi_ref, clo_ref, hi, lo, cols, sems):
     core = pos_ref[1]
+    step = 256
+    copies = []
+    for i in range(NCOL // step):
+        at = pl.ds(i * step, step)
+        copies.append(pltpu.make_async_copy(cols_hbm.at[at, :], cols.at[at, :], sems.at[i]))
+        copies[-1].start()
     for j, ref in enumerate((own_ref, oth_ref)):
         hi[j], lo[j] = split(ref[...])
     rows = (hi[...].reshape(NC * ROWS, WIDE), lo[...].reshape(NC * ROWS, WIDE))
-    step = 256
-    for c in range(0, NCOL, step):
-        s_ref[:, c:c + step] = INV_TAU * dot3(rows, split(cols_ref[c:c + step, :]), ((1,), (1,)))
+    for i, copy in enumerate(copies):
+        at = slice(i * step, (i + 1) * step)
+        copy.wait()
+        h, l = split(cols[at, :])
+        chi_ref[at, :] = h
+        clo_ref[at, :] = l
+        s_ref[:, at] = INV_TAU * dot3(rows, (h, l), ((1,), (1,)))
     colsum = jnp.zeros((1, NCOL), jnp.float32)
     pos = jnp.zeros((1, ROWS), jnp.float32)
     sums = []
@@ -112,13 +131,22 @@
     nrow = NCOL // ROWS
     col = jnp.concatenate([colsum[:, c * ROWS:(c + 1) * ROWS] for c in range(nrow)]
                           + [pos, jnp.zeros((7 - nrow, ROWS), jnp.float32)], axis=0)
-    for k in range(NC * NF):
+    for k in range(NC * NYL):
         row_ref[k] = row
-    for k in range(NZ * NYH):
+    for k in range(NYH):
         col_ref[k] = col
 
 
-def grad_kernel(pos_ref, s_ref, own_ref, oth_ref, cols_ref, ownp_ref, othp_ref, rows_ref, cols_l_ref, mine_ref, theirs_ref, w_hi, w_lo):
+def relay_kernel(rows_ref, cols_ref, row_ref, col_ref):
+    row = jnp.sum(rows_ref[...], axis=0)
+    col = jnp.sum(cols_ref[...], axis=0)
+    for k in range(NX):
+        row_ref[k] = row
+    for k in range(NZ):
+        col_ref[k] = col
+
+
+def grad_kernel(pos_ref, s_ref, own_ref, oth_ref, chi_ref, clo_ref, ownp_ref, othp_ref, rows_ref, cols_l_ref, mine_ref, theirs_ref, w_hi, w_lo):
     core = pos_ref[1]
     row_l = jnp.sum(rows_ref[...], axis=0)
     col_l = jnp.sum(cols_l_ref[...], axis=0)
@@ -139,7 +167,7 @@
     tail = jnp.concatenate([loss, jnp.zeros((7, ROWS), jnp.float32)], axis=0)
     for c in range(WIDE // step):
         at = slice(c * step, (c + 1) * step)
-        g = INV_TAU * dot3(weights, split(cols_ref[:, at]), ((1,), (0,)))
+        g = INV_TAU * dot3(weights, (chi_ref[:, at], clo_ref[:, at]), ((1,), (0,)))
         for j, (units, out) in enumerate(((own_ref, mine_ref), (oth_ref, theirs_ref))):
             t = (g[j * ROWS:(j + 1) * ROWS, :] - units[:, at] * projs[j]).T
             for p in range(2):
@@ -161,11 +189,11 @@
     return lax.all_to_all(x, axes, 0, 0, tiled=True)
 
 
-def call(body, name, outs, args, scratch=()):
+def call(body, name, outs, args, scratch=(), far=()):
     return pl.pallas_call(
         body,
         out_shape=outs,
-        in_specs=[SMEM if a.shape == (3,) else VMEM for a in args],
+        in_specs=[SMEM if a.shape == (3,) else HBM if i in far else VMEM for i, a in enumerate(args)],
         out_specs=[VMEM] * len(outs),
         scratch_shapes=list(scratch),
         compiler_params=PARAMS,
@@ -182,25 +210,28 @@
 
     own_p = partner.reshape(ROWS, 1)
     oth_p = swap(partner, "core", NC, 1).reshape(ROWS, 1)
-    packed = CHUNK * FEAT // ROWS
-    chunks, = call(chunk_kernel, "chunks", [f32(NYH * NF, packed, ROWS)], [views.T])
-    chunks = trade(chunks, ("yh", "yl", "x"))
-    chunk, copies = call(column_kernel, "columns", [f32(NYH * CHUNK, WIDE), f32(NF, FEAT, ROWS)], [chunks, views.T])
+    chunks, = call(chunk_kernel, "chunks", [f32(NX, NYL * PACKED, ROWS)], [views.T])
+    halves, = call(half_kernel, "halves", [f32(NYH * NYL, CHUNK, WIDE // NYL)], [trade(chunks, "x")])
+    chunk, copies = call(column_kernel, "columns", [f32(NYH * CHUNK, WIDE), f32(NF, FEAT, ROWS)],
+                         [trade(halves, ("yh", "yl")), views.T])
     cols = lax.all_gather(chunk, "z", axis=0, tiled=True)
     own, scale = call(norm_kernel, "norm", [f32(ROWS, WIDE), f32(1, ROWS)], [trade(copies, feat)])
     oth = swap(own, "core", NC, 1)
-    s, row, col = call(
+    bf16 = jax.ShapeDtypeStruct((NCOL, WIDE), jnp.bfloat16)
+    s, row, col, chi, clo = call(
         score_kernel, "scores",
-        [f32(NC * ROWS, NCOL), f32(NC * NF, 8, ROWS), f32(NZ * NYH, 8, ROWS)],
+        [f32(NC * ROWS, NCOL), f32(NC * NYL, 8, ROWS), f32(NYH, 8, ROWS), bf16, bf16],
         [pos, own, oth, cols, own_p, oth_p],
-        [pltpu.VMEM((NC, ROWS, WIDE), jnp.bfloat16)] * 2,
+        [pltpu.VMEM((NC, ROWS, WIDE), jnp.bfloat16)] * 2
+        + [pltpu.VMEM((NCOL, WIDE), jnp.float32), pltpu.SemaphoreType.DMA((NCOL // 256,))],
+        far=(3,),
     )
-    rows_l = trade(row, ("core", "yl", "x"))
-    cols_l = trade(col, ("z", "yh"))
+    row, col = call(relay_kernel, "relay", [f32(NX, 8, ROWS), f32(NZ, 8, ROWS)],
+                    [trade(row, ("core", "yl")), trade(col, "yh")])
     mine, theirs = call(
         grad_kernel, "gradient",
         [f32(NF, PIECE, ROWS)] * 2,
-        [pos, s, own, oth, cols, own_p, oth_p, rows_l, cols_l],
+        [pos, s, own, oth, chi, clo, own_p, oth_p, trade(row, "x"), trade(col, "z")],
         [pltpu.VMEM((NC, ROWS, NCOL), jnp.bfloat16)] * 2,
     )
     pieces = trade(mine + swap(theirs, "core", NC, 1), feat)

time: 151 us -> 165 us (1.093)
  blocking collectives: 83.3 us -> 91.8 us
  starting transfers between devices: 11.8 us -> 16 us
    all_to_all x5 -> x8, blocking collectives: 83.3 us -> 91.8 us  [trade(): return lax.all_to_all(x, axes, 0, 0, tiled=True)]
    ppermute x3, starting transfers between devices: 11.7 us -> 16 us  [swap(): return lax.ppermute(x, axes, [(i, i ^ k) for i in range(size)])]
    pallas_call x6 -> x8, Pallas kernels: 8.87 us -> 9.11 us  [call(): pl.pallas_call(body, out_shape=outs, in_specs=[SMEM if a.shape == (3,) el...]
where the time goes in v2:
time: 165 us; the launch traced here: 164 us
  blocking collectives  91.8 us (56%)
  waiting for transfers between devices  30.3 us (18%)
  starting transfers between devices  16 us (10%)
  between operations  14.1 us (9%)
  Pallas kernels  9.11 us (6%)
  local copies, waits for them, and re-layouts  3.01 us (2%)
    all_to_all x8, blocking collectives, trade(): return lax.all_to_all(x, axes, 0, 0, tiled=True)  91.8 us
    all_gather x1, waiting for transfers between devices, per_device(): cols = lax.all_gather(chunk, 'z', axis=0, tiled=True)  27.4 us
    ppermute x3, starting transfers between devices, swap(): return lax.ppermute(x, axes, [(i, i ^ k) for i in range(size)])  16 us
    pallas_call x8, Pallas kernels, call(): pl.pallas_call(body, out_shape=outs, in_specs=[SMEM if a.shape == (3,) el...  9.11 us
  transfers between devices with their start and end apart: 4, of which 3 were waited for; matrix products, arithmetic and copies ran while one was open for 0% of the time, Pallas kernels for 0%

profile of v2, /device:TPU:1, one launch (start us, length us, event | category | flops | bytes accessed | tf_op | source)
XLA Modules:
  0.0 164.5 jit_solution(10292855144002748429)
XLA Ops:
  7.2 0.0 all-gather.2.cloned.1.call-start
  7.2 0.0 copy-start.1
  7.2 0.9 copy-done.1
  8.1 0.0 copy-start.2
  8.1 0.2 chunks.1
  8.3 9.3 %all_to_all.40.piece_ref = f32[4,48,128]{2,1,0:T(8,128)S(1)} all-to-all(f32[4,48,128]{2,1,0:T(8,128)S(1)} %chunks.1), channel_id=1, replica_groups=mesh['z'=8,'yh'=4,'core'=2,'yl'=2,'x'=4] {'x'}, dimensions={0} | all-to-all | bytes 196608 | tf_op jit(solution)/shard_map/all_to_all | solution.py:189
  17.6 0.1 halves.1
  17.7 18.2 %all_to_all.41.piece_ref = f32[8,16,768]{2,1,0:T(8,128)S(1)} all-to-all(f32[8,16,768]{2,1,0:T(8,128)S(1)} %halves.1), channel_id=1, replica_groups=mesh['z'=8,'yh'=4,'core'=2,'yl'=2,'x'=4] {'yh','yl'}, dimensions={0} | all-to-all | bytes 786432 | tf_op jit(solution)/shard_map/all_to_all | solution.py:189
  35.9 0.0 copy-done.2
  35.9 0.0 copy-start.3
  35.9 0.9 columns.1
  36.7 0.0 all-gather.2.cloned.1.call-update
  36.8 11.3 %all_to_all.42.piece_ref = f32[8,192,128]{2,1,0:T(8,128)S(1)} all-to-all(f32[8,192,128]{2,1,0:T(8,128)S(1)} %get-tuple-element.17), channel_id=1, replica_groups=mesh['z'=8,'yh'=4,'core'=2,'yl'=2,'x'=4] {'yl','x'}, dimensions={0} | all-to-all | bytes 1572864 | tf_op jit(solution)/shard_map/all_to_all | solution.py:189
  48.1 0.5 norm.1
  48.5 7.2 %collective-permute-start = (f32[128,1536]{1,0:T(8,128)S(1)}, f32[128,1536]{1,0:T(8,128)S(1)}, u32[]{:S(2)}, u32[]{:S(2)}) collective-permute-start(f32[128,1536]{1,0:T(8,128)S(1)} %get-tuple-element.18.own_ref), channel_id=1, source_target_pairs={{0,8},{8,0},{1,9},{9,1},{2,10},{10,2},{3,11},{11,3},{4,12},{12,4},... | collective-permute-start | bytes 2359304 | tf_op jit(solution)/shard_map/ppermute | solution.py:185
  55.7 0.0 copy-done.3
  55.7 1.9 %collective-permute-start.1 = (s32[128]{0:T(128)S(1)}, s32[128]{0:T(128)S(1)}, u32[]{:S(2)}, u32[]{:S(2)}) collective-permute-start(s32[128]{0:T(128)S(1)} %copy-done.3), channel_id=1, source_target_pairs={{0,8},{8,0},{1,9},{9,1},{2,10},{10,2},{3,11},{11,3},{4,12},{12,4},... | collective-permute-start | bytes 1544 | tf_op jit(solution)/shard_map/ppermute | solution.py:185
  57.6 0.1 pad_add_fusion.pos_ref
  57.7 0.1 copy.4.ownp_ref
  57.8 0.9 collective-permute-done.1
  58.7 0.1 copy.5.othp_ref
  58.8 0.0 collective-permute-done.oth_ref
  58.8 27.4 %all-gather.2.cloned.1.call-done.cols_hbm = f32[512,1536]{1,0:T(8,128)} async-done(((f32[64,1536]{1,0:T(8,128)}), f32[512,1536]{1,0:T(8,128)}) %all-gather.2.cloned.1.call-update) | async-done | bytes 3145744 | tf_op jit(solution)/shard_map/all_gather | solution.py:217
  86.3 0.0 copy-start
  86.3 1.9 %copy-done = f32[512,1536]{1,0:T(8,128)S(1)} copy-done((f32[512,1536]{1,0:T(8,128)S(1)}, f32[512,1536]{1,0:T(8,128)}, u32[]{:S(2)}) %copy-start) | copy-done | bytes 3145752
  88.1 4.0 %scores.1 = (f32[256,512]{1,0:T(8,128)S(1)}, f32[4,8,128]{2,1,0:T(8,128)S(1)}, f32[4,8,128]{2,1,0:T(8,128)S(1)}, bf16[512,1536]{1,0:T(8,128)(2,1)S(1)}, bf16[512,1536]{1,0:T(8,128)(2,1)S(1)}) custom-call(s32[3]{0:T(128)S(1)} %pad_add_fusion.pos_ref, f32[128,1536]{1,0:T(8,128)S(1)} %get-tuple-element.18.own_ref, ...), custom_call_target="tpu_custom_call" | custom-call | tf_op jit(solution)/shard_map/scores/pallas_call | solution.py:193
  92.1 6.4 %all_to_all.43.rows_ref = f32[4,8,128]{2,1,0:T(8,128)S(1)} all-to-all(f32[4,8,128]{2,1,0:T(8,128)S(1)} %get-tuple-element.23), channel_id=1, replica_groups=mesh['z'=8,'yh'=4,'core'=2,'yl'=2,'x'=4] {'core','yl'}, dimensions={0} | all-to-all | bytes 32768 | tf_op jit(solution)/shard_map/all_to_all | solution.py:189
  98.5 12.7 %all_to_all.44.cols_ref = f32[4,8,128]{2,1,0:T(8,128)S(1)} all-to-all(f32[4,8,128]{2,1,0:T(8,128)S(1)} %get-tuple-element.24), channel_id=1, replica_groups=mesh['z'=8,'yh'=4,'core'=2,'yl'=2,'x'=4] {'yh'}, dimensions={0} | all-to-all | bytes 32768 | tf_op jit(solution)/shard_map/all_to_all | solution.py:189
  111.2 8.0 %all_to_all.45.rows_ref = f32[4,8,128]{2,1,0:T(8,128)S(1)} all-to-all(f32[4,8,128]{2,1,0:T(8,128)S(1)} %get-tuple-element.25), channel_id=1, replica_groups=mesh['z'=8,'yh'=4,'core'=2,'yl'=2,'x'=4] {'x'}, dimensions={0} | all-to-all | bytes 32768 | tf_op jit(solution)/shard_map/all_to_all | solution.py:189
  119.2 10.5 %all_to_all.46.cols_l_ref = f32[8,8,128]{2,1,0:T(8,128)S(1)} all-to-all(f32[8,8,128]{2,1,0:T(8,128)S(1)} %get-tuple-element.26), channel_id=1, replica_groups=mesh['z'=8,'yh'=4,'core'=2,'yl'=2,'x'=4] {'z'}, dimensions={0} | all-to-all | bytes 65536 | tf_op jit(solution)/shard_map/all_to_all | solution.py:189
  129.7 2.8 %gradient.1 = (f32[8,200,128]{2,1,0:T(8,128)S(1)}, f32[8,200,128]{2,1,0:T(8,128)S(1)}) custom-call(s32[3]{0:T(128)S(1)} %pad_add_fusion.pos_ref, f32[256,512]{1,0:T(8,128)S(1)} %get-tuple-element.20.s_ref, f32[128,1536]{1,0:T(8,128)S(1)} %get-tuple-element.18.own_ref, f32[128,1536]{1,0:T(8,128)S(1)} %collective-permute-done.oth_ref, ...), custom_call_target="tpu_custom_call" | custom-call | tf_op jit(solution)/shard_map/gradient/pallas_call | solution.py:193
  132.5 6.9 %collective-permute-start.2 = (f32[8,200,128]{2,1,0:T(8,128)S(1)}, f32[8,200,128]{2,1,0:T(8,128)S(1)}, u32[]{:S(2)}, u32[]{:S(2)}) collective-permute-start(f32[8,200,128]{2,1,0:T(8,128)S(1)} %get-tuple-element.28), channel_id=1, source_target_pairs={{0,8},{8,0},{1,9},{9,1},{2,10},{10,2},{3,11},{11,3},{4,12},{12,4},... | collective-permute-start | bytes 2457608 | tf_op jit(solution)/shard_map/ppermute | solution.py:185
  139.4 1.9 %collective-permute-done.2 = f32[8,200,128]{2,1,0:T(8,128)S(1)} collective-permute-done((f32[8,200,128]{2,1,0:T(8,128)S(1)}, f32[8,200,128]{2,1,0:T(8,128)S(1)}, u32[]{:S(2)}, u32[]{:S(2)}) %collective-permute-start.2) | collective-permute-done | bytes 819232 | tf_op jit(solution)/shard_map/ppermute | solution.py:185
  141.4 0.1 add.11
  141.5 15.5 %all_to_all.47.piece_ref = f32[8,200,128]{2,1,0:T(8,128)S(1)} all-to-all(f32[8,200,128]{2,1,0:T(8,128)S(1)} %add.11), channel_id=1, replica_groups=mesh['z'=8,'yh'=4,'core'=2,'yl'=2,'x'=4] {'yl','x'}, dimensions={0} | all-to-all | bytes 1638400 | tf_op jit(solution)/shard_map/all_to_all | solution.py:189
  157.0 0.7 finish.1
  (1 shorter events, 0.0 us)
Async XLA Ops:
  7.2 79.1 %all-gather.2.cloned.1.call-start = ((), (), s32[]{:S(2)}) async-start(), calls=%async_computation.8 | async-start | bytes 3538944 | tf_op jit(solution)/shard_map/all_gather | solution.py:217
  7.2 0.9 copy-start.1
  8.1 27.8 %copy-start.2 = (f32[128,192]{0,1:T(8,128)S(1)}, f32[128,192]{0,1:T(8,128)}, u32[]{:S(2)}) copy-start(f32[128,192]{0,1:T(8,128)} %param.2) | copy-start | bytes 294916
  35.9 19.8 %copy-start.3 = (s32[128]{0:T(128)S(1)}, s32[128]{0:T(128)}, u32[]{:S(2)}) copy-start(s32[128]{0:T(128)} %param.3) | copy-start | bytes 1540
  48.5 10.3 %collective-permute-start = (f32[128,1536]{1,0:T(8,128)S(1)}, f32[128,1536]{1,0:T(8,128)S(1)}, u32[]{:S(2)}, u32[]{:S(2)}) collective-permute-start(f32[128,1536]{1,0:T(8,128)S(1)} %get-tuple-element.18.own_ref), channel_id=1, source_target_pairs={{0,8},{8,0},{1,9},{9,1},{2,10},{10,2},{3,11},{11,3},{4,12},{12,4},... | collective-permute-start | bytes 2359304 | tf_op jit(solution)/shard_map/ppermute | solution.py:185
  55.7 3.0 %collective-permute-start.1 = (s32[128]{0:T(128)S(1)}, s32[128]{0:T(128)S(1)}, u32[]{:S(2)}, u32[]{:S(2)}) collective-permute-start(s32[128]{0:T(128)S(1)} %copy-done.3), channel_id=1, source_target_pairs={{0,8},{8,0},{1,9},{9,1},{2,10},{10,2},{3,11},{11,3},{4,12},{12,4},... | collective-permute-start | bytes 1544 | tf_op jit(solution)/shard_map/ppermute | solution.py:185
  86.3 1.9 %copy-start = (f32[512,1536]{1,0:T(8,128)S(1)}, f32[512,1536]{1,0:T(8,128)}, u32[]{:S(2)}) copy-start(f32[512,1536]{1,0:T(8,128)} %all-gather.2.cloned.1.call-done.cols_hbm) | copy-start | bytes 9437188
  132.5 8.9 %collective-permute-start.2 = (f32[8,200,128]{2,1,0:T(8,128)S(1)}, f32[8,200,128]{2,1,0:T(8,128)S(1)}, u32[]{:S(2)}, u32[]{:S(2)}) collective-permute-start(f32[8,200,128]{2,1,0:T(8,128)S(1)} %get-tuple-element.28), channel_id=1, source_target_pairs={{0,8},{8,0},{1,9},{9,1},{2,10},{10,2},{3,11},{11,3},{4,12},{12,4},... | collective-permute-start | bytes 2457608 | tf_op jit(solution)/shard_map/ppermute | solution.py:185
Sparse Core Ops, SparseCore 0:
  36.9 49.3 all-gather.1

commit v3 on v1

--- a/solution.py
+++ b/solution.py
@@ -17,7 +17,8 @@
 INV_TAU = 10.0
 VMEM = pl.BlockSpec(memory_space=pltpu.VMEM)
 SMEM = pl.BlockSpec(memory_space=pltpu.SMEM)
-PARAMS = pltpu.CompilerParams(vmem_limit_bytes=48 * 1024 * 1024)
+HBM = pl.BlockSpec(memory_space=pltpu.HBM)
+MIB = 1024 * 1024
 
 
 def f32(*shape):
@@ -59,17 +60,15 @@
             out_ref[y * NF + f] = piece
 
 
-def column_kernel(piece_ref, view_ref, unit_ref, copies_ref):
+def column_kernel(piece_ref, unit_ref):
     for y in range(NYH):
         x = jnp.concatenate([unpack(piece_ref[y * NF + f]) for f in range(NF)], axis=1)
         scale = lax.rsqrt(jnp.sum(x * x, axis=1, keepdims=True) + 1e-06)
         unit_ref[y * CHUNK:(y + 1) * CHUNK, :] = x * scale
-    for f in range(NF):
-        copies_ref[f] = view_ref[...]
 
 
 def norm_kernel(piece_ref, unit_ref, scale_ref):
-    x = piece_ref[...].reshape(WIDE, ROWS)
+    x = piece_ref[...]
     scale = lax.rsqrt(jnp.sum(x * x, axis=0, keepdims=True) + 1e-06)
     scale_ref[...] = scale
     unit_ref[...] = (x * scale).T
@@ -83,14 +82,21 @@
     return col == row, col == part
 
 
-def score_kernel(pos_ref, own_ref, oth_ref, cols_ref, ownp_ref, othp_ref, s_ref, row_ref, col_ref, hi, lo):
+def score_kernel(pos_ref, own_ref, oth_ref, cols_hbm, ownp_ref, othp_ref, s_ref, row_ref, col_ref, hi, lo, cols, sems):
     core = pos_ref[1]
+    step = 256
+    copies = []
+    for i in range(NCOL // step):
+        at = pl.ds(i * step, step)
+        copies.append(pltpu.make_async_copy(cols_hbm.at[at, :], cols.at[at, :], sems.at[i]))
+        copies[-1].start()
     for j, ref in enumerate((own_ref, oth_ref)):
         hi[j], lo[j] = split(ref[...])
     rows = (hi[...].reshape(NC * ROWS, WIDE), lo[...].reshape(NC * ROWS, WIDE))
-    step = 256
-    for c in range(0, NCOL, step):
-        s_ref[:, c:c + step] = INV_TAU * dot3(rows, split(cols_ref[c:c + step, :]), ((1,), (1,)))
+    for i, copy in enumerate(copies):
+        at = slice(i * step, (i + 1) * step)
+        copy.wait()
+        s_ref[:, at] = INV_TAU * dot3(rows, split(cols[at, :]), ((1,), (1,)))
     colsum = jnp.zeros((1, NCOL), jnp.float32)
     pos = jnp.zeros((1, ROWS), jnp.float32)
     sums = []
@@ -112,8 +118,7 @@
     nrow = NCOL // ROWS
     col = jnp.concatenate([colsum[:, c * ROWS:(c + 1) * ROWS] for c in range(nrow)]
                           + [pos, jnp.zeros((7 - nrow, ROWS), jnp.float32)], axis=0)
-    for k in range(NC * NF):
-        row_ref[k] = row
+    row_ref[...] = row
     for k in range(NZ * NYH):
         col_ref[k] = col
 
@@ -161,14 +166,14 @@
     return lax.all_to_all(x, axes, 0, 0, tiled=True)
 
 
-def call(body, name, outs, args, scratch=()):
+def call(body, name, outs, args, scratch=(), far=(), limit=24):
     return pl.pallas_call(
         body,
         out_shape=outs,
-        in_specs=[SMEM if a.shape == (3,) else VMEM for a in args],
+        in_specs=[SMEM if a.shape == (3,) else HBM if i in far else VMEM for i, a in enumerate(args)],
         out_specs=[VMEM] * len(outs),
         scratch_shapes=list(scratch),
-        compiler_params=PARAMS,
+        compiler_params=pltpu.CompilerParams(vmem_limit_bytes=limit * MIB),
         name=name,
     )(*args)
 
@@ -183,19 +188,21 @@
     own_p = partner.reshape(ROWS, 1)
     oth_p = swap(partner, "core", NC, 1).reshape(ROWS, 1)
     packed = CHUNK * FEAT // ROWS
+    whole = lax.all_gather(views.T, feat, axis=0, tiled=True)
     chunks, = call(chunk_kernel, "chunks", [f32(NYH * NF, packed, ROWS)], [views.T])
-    chunks = trade(chunks, ("yh", "yl", "x"))
-    chunk, copies = call(column_kernel, "columns", [f32(NYH * CHUNK, WIDE), f32(NF, FEAT, ROWS)], [chunks, views.T])
+    chunk, = call(column_kernel, "columns", [f32(NYH * CHUNK, WIDE)], [trade(chunks, ("yh", "yl", "x"))])
     cols = lax.all_gather(chunk, "z", axis=0, tiled=True)
-    own, scale = call(norm_kernel, "norm", [f32(ROWS, WIDE), f32(1, ROWS)], [trade(copies, feat)])
+    own, scale = call(norm_kernel, "norm", [f32(ROWS, WIDE), f32(1, ROWS)], [whole])
     oth = swap(own, "core", NC, 1)
     s, row, col = call(
         score_kernel, "scores",
-        [f32(NC * ROWS, NCOL), f32(NC * NF, 8, ROWS), f32(NZ * NYH, 8, ROWS)],
+        [f32(NC * ROWS, NCOL), f32(8, ROWS), f32(NZ * NYH, 8, ROWS)],
         [pos, own, oth, cols, own_p, oth_p],
-        [pltpu.VMEM((NC, ROWS, WIDE), jnp.bfloat16)] * 2,
+        [pltpu.VMEM((NC, ROWS, WIDE), jnp.bfloat16)] * 2
+        + [pltpu.VMEM((NCOL, WIDE), jnp.float32), pltpu.SemaphoreType.DMA((NCOL // 256,))],
+        far=(3,), limit=48,
     )
-    rows_l = trade(row, ("core", "yl", "x"))
+    rows_l = lax.all_gather(row, ("core", "yl", "x"), axis=0, tiled=False)
     cols_l = trade(col, ("z", "yh"))
     mine, theirs = call(
         grad_kernel, "gradient",

time: 151 us -> 168 us (1.11)
  waiting for transfers between devices: 29.8 us -> 12.8 us
  blocking collectives: 83.3 us -> 96.9 us
  starting transfers between devices: 11.8 us -> 22.7 us
  local copies, waits for them, and re-layouts: 3 us -> 11.1 us
    all_gather x0 -> x2, blocking collectives: none -> 54.9 us  [the longest x1 30.2 us: per_device(): rows_l = lax.all_gather(row, ('core', 'yl', 'x'), axis=0, tiled=False)]
    all_to_all x5 -> x2, blocking collectives: 83.3 us -> 42.1 us  [trade(): return lax.all_to_all(x, axes, 0, 0, tiled=True)]
    all_gather x1, waiting for transfers between devices: 27 us -> 9.57 us  [per_device(): cols = lax.all_gather(chunk, 'z', axis=0, tiled=True)]
    all_to_all x0 -> x1, starting transfers between devices: none -> 9.09 us  [trade(): return lax.all_to_all(x, axes, 0, 0, tiled=True)]
    unnamed x6 -> x24, local copies, waits for them, and re-layouts: 2.78 us -> 10.9 us
    ppermute x3, starting transfers between devices: 11.7 us -> 13.6 us  [swap(): return lax.ppermute(x, axes, [(i, i ^ k) for i in range(size)])]
  transfers between devices with their start and end apart: 4 -> 5, of which waited for: 3 -> 3; matrix products, arithmetic and copies ran while one was open for 0% -> 0% of each run, Pallas kernels for 0% -> 0%
where the time goes in v3:
time: 168 us
  blocking collectives  96.9 us (58%)
  starting transfers between devices  22.7 us (14%)
  between operations  14.2 us (8%)
  waiting for transfers between devices  12.8 us (8%)
  local copies, waits for them, and re-layouts  11.1 us (7%)
  Pallas kernels  9.74 us (6%)
    all_to_all x2, blocking collectives, trade(): return lax.all_to_all(x, axes, 0, 0, tiled=True)  42.1 us
    all_gather x1, blocking collectives, per_device(): rows_l = lax.all_gather(row, ('core', 'yl', 'x'), axis=0, tiled=False)  30.2 us
    all_gather x1, blocking collectives, per_device(): whole = lax.all_gather(views.T, feat, axis=0, tiled=True)  24.6 us
    ppermute x3, starting transfers between devices, swap(): return lax.ppermute(x, axes, [(i, i ^ k) for i in range(size)])  13.6 us
    unnamed x24, local copies, waits for them, and re-layouts  10.9 us
    pallas_call x6, Pallas kernels, call(): pl.pallas_call(body, out_shape=outs, in_specs=[SMEM if a.shape == (3,) el...  9.74 us
    all_gather x1, waiting for transfers between devices, per_device(): cols = lax.all_gather(chunk, 'z', axis=0, tiled=True)  9.57 us
    all_to_all x1, starting transfers between devices, trade(): return lax.all_to_all(x, axes, 0, 0, tiled=True)  9.09 us
  transfers between devices with their start and end apart: 5, of which 3 were waited for; matrix products, arithmetic and copies ran while one was open for 0% of the time, Pallas kernels for 0%

profile of v3, /device:TPU:1, one launch (start us, length us, event | category | flops | bytes accessed | tf_op | source)
XLA Modules:
  0.0 167.6 jit_solution(7789013102671164272)
XLA Ops:
  7.2 0.0 copy-start.11
  7.2 0.0 all-gather.3.cloned.1.call-start
  7.2 0.0 copy-start.10
  7.2 0.9 copy-done.10
  8.1 0.2 chunks.1
  8.3 24.1 %all_to_all.15.piece_ref = f32[32,24,128]{2,1,0:T(8,128)S(1)} all-to-all(f32[32,24,128]{2,1,0:T(8,128)S(1)} %chunks.1), channel_id=1, replica_groups=mesh['z'=8,'yh'=4,'core'=2,'yl'=2,'x'=4] {'yh','yl','x'}, dimensions={0} | all-to-all | bytes 786432 | tf_op jit(solution)/shard_map/all_to_all | solution.py:166
  32.4 1.1 columns.1
  33.4 0.0 all-gather.3.cloned.1.call-update
  33.5 24.6 %all_gather.12.piece_ref = f32[1536,128]{1,0:T(8,128)S(1)} all-gather(f32[192,128]{1,0:T(8,128)} %bitcast.9), channel_id=1, replica_groups=mesh['z'=8,'yh'=4,'core'=2,'yl'=2,'x'=4] {'yl','x'}, dimensions={0}, use_global_device_ids=true | all-gather | bytes 884736 | tf_op jit(solution)/shard_map/all_gather | solution.py:191
  58.1 0.5 norm.1
  58.6 9.8 %collective-permute-start = (f32[128,1536]{1,0:T(8,128)S(1)}, f32[128,1536]{1,0:T(8,128)S(1)}, u32[]{:S(2)}, u32[]{:S(2)}) collective-permute-start(f32[128,1536]{1,0:T(8,128)S(1)} %get-tuple-element.11.own_ref), channel_id=1, source_target_pairs={{0,8},{8,0},{1,9},{9,1},{2,10},{10,2},{3,11},{11,3},{4,12},{12,4},... | collective-permute-start | bytes 2359304 | tf_op jit(solution)/shard_map/ppermute | solution.py:162
  68.4 0.0 copy-start.2
  68.4 0.9 copy-done.2
  69.3 0.0 copy-done.11
  69.3 1.9 %collective-permute-start.1 = (s32[128]{0:T(128)S(1)}, s32[128]{0:T(128)S(1)}, u32[]{:S(2)}, u32[]{:S(2)}) collective-permute-start(s32[128]{0:T(128)S(1)} %copy-done.11), channel_id=1, source_target_pairs={{0,8},{8,0},{1,9},{9,1},{2,10},{10,2},{3,11},{11,3},{4,12},{12,4},... | collective-permute-start | bytes 1544 | tf_op jit(solution)/shard_map/ppermute | solution.py:162
  71.2 0.1 pad_add_fusion.pos_ref
  71.3 0.1 copy.4.ownp_ref
  71.4 0.9 collective-permute-done.1
  72.3 0.1 copy.5.othp_ref
  72.4 0.0 collective-permute-done.oth_ref
  72.4 0.0 copy-start.5
  72.4 0.9 copy-done.5
  73.3 9.6 %all-gather.3.cloned.1.call-done.cols_hbm.cols_ref = f32[512,1536]{1,0:T(8,128)} async-done(((f32[64,1536]{1,0:T(8,128)}), f32[512,1536]{1,0:T(8,128)}) %all-gather.3.cloned.1.call-update) | async-done | bytes 3145744 | tf_op jit(solution)/shard_map/all_gather | solution.py:194
  82.8 0.0 copy-start
  82.8 1.9 %copy-done = f32[512,1536]{1,0:T(8,128)S(1)} copy-done((f32[512,1536]{1,0:T(8,128)S(1)}, f32[512,1536]{1,0:T(8,128)}, u32[]{:S(2)}) %copy-start) | copy-done | bytes 3145752
  84.7 0.0 copy-start.3
  84.7 1.1 copy-done.3
  85.9 0.0 copy-start.6
  85.9 1.1 copy-done.6
  87.0 0.0 copy-start.1
  87.0 4.6 %scores.1 = (f32[256,512]{1,0:T(8,128)S(1)}, f32[8,128]{1,0:T(8,128)S(1)}, f32[32,8,128]{2,1,0:T(8,128)}) custom-call(s32[3]{0:T(128)S(1)} %pad_add_fusion.pos_ref, f32[128,1536]{1,0:T(8,128)S(1)} %copy-done.3, f32[128,1536]{1,0:T(8,128)S(1)} %copy-done.6, f32[512,1536]{1,0:T(8,128)S(1)} %copy-done, s32[128,1]{1,0:T(8,128)S(1)} %copy.4.ownp_ref, ...), custom_call_target="tpu_custom_call" | custom-call | tf_op jit(solution)/shard_map/scores/pallas_call | solution.py:170
  91.6 0.0 copy-start.8
  91.6 0.8 copy-done.8
  92.4 9.1 %all-to-all-start.1 = ((f32[32,8,128]{2,1,0:T(8,128)}), f32[32,8,128]{2,1,0:T(8,128)S(1)}, u32[]{:S(2)}, u32[]{:S(2)}) async-start(f32[32,8,128]{2,1,0:T(8,128)} %get-tuple-element.14), calls=%async_computation.1 | async-start | bytes 262144 | tf_op jit(solution)/shard_map/all_to_all | solution.py:166
  101.5 30.2 %all-gather = f32[128,128]{1,0:T(8,128)S(1)} all-gather(f32[8,128]{1,0:T(8,128)S(1)} %get-tuple-element.13), channel_id=2, replica_groups=mesh['z'=8,'yh'=4,'core'=2,'yl'=2,'x'=4] {'core','yl','x'}, dimensions={0}, use_global_device_ids=true | all-gather | bytes 69632 | tf_op jit(solution)/shard_map/all_gather | solution.py:205
  131.7 0.0 all-to-all-done.1.cols_l_ref
  131.7 0.0 copy-done.1
  131.7 0.0 copy-start.4
  131.7 1.1 copy-done.4
  132.8 0.0 copy-start.7
  132.8 1.1 copy-done.7
  133.9 1.0 copy-done.9
  135.0 2.8 %gradient.1 = (f32[8,200,128]{2,1,0:T(8,128)S(1)}, f32[8,200,128]{2,1,0:T(8,128)S(1)}) custom-call(s32[3]{0:T(128)S(1)} %pad_add_fusion.pos_ref, f32[256,512]{1,0:T(8,128)S(1)} %copy-done.9, f32[128,1536]{1,0:T(8,128)S(1)} %copy-done.4, f32[128,1536]{1,0:T(8,128)S(1)} %copy-done.7, f32[512,1536]{1,0:T(8,128)S(1)} %copy-done.1, s32[128,1]{1,0:T(8,128)S(1)} %copy.4.ownp_ref, ...), custom_call_target="tpu_custom_call" | custom-call | tf_op jit(solution)/shard_map/gradient/pallas_call | solution.py:170
  137.8 1.9 %collective-permute-start.2 = (f32[8,200,128]{2,1,0:T(8,128)S(1)}, f32[8,200,128]{2,1,0:T(8,128)S(1)}, u32[]{:S(2)}, u32[]{:S(2)}) collective-permute-start(f32[8,200,128]{2,1,0:T(8,128)S(1)} %get-tuple-element.16), channel_id=1, source_target_pairs={{0,8},{8,0},{1,9},{9,1},{2,10},{10,2},{3,11},{11,3},{4,12},{12,4},... | collective-permute-start | bytes 2457608 | tf_op jit(solution)/shard_map/ppermute | solution.py:162
  139.7 2.3 %collective-permute-done.2 = f32[8,200,128]{2,1,0:T(8,128)S(1)} collective-permute-done((f32[8,200,128]{2,1,0:T(8,128)S(1)}, f32[8,200,128]{2,1,0:T(8,128)S(1)}, u32[]{:S(2)}, u32[]{:S(2)}) %collective-permute-start.2) | collective-permute-done | bytes 819232 | tf_op jit(solution)/shard_map/ppermute | solution.py:162
  142.0 0.1 add.11
  142.1 18.0 %all_to_all.16.piece_ref = f32[8,200,128]{2,1,0:T(8,128)S(1)} all-to-all(f32[8,200,128]{2,1,0:T(8,128)S(1)} %add.11), channel_id=1, replica_groups=mesh['z'=8,'yh'=4,'core'=2,'yl'=2,'x'=4] {'yl','x'}, dimensions={0} | all-to-all | bytes 1638400 | tf_op jit(solution)/shard_map/all_to_all | solution.py:166
  160.1 0.7 finish.1
  (1 shorter events, 0.0 us)
Async XLA Ops:
  7.2 62.1 %copy-start.11 = (s32[128]{0:T(128)S(1)}, s32[128]{0:T(128)}, u32[]{:S(2)}) copy-start(s32[128]{0:T(128)} %param.3) | copy-start | bytes 1540
  7.2 75.7 %all-gather.3.cloned.1.call-start = ((), (), s32[]{:S(2)}) async-start(), calls=%async_computation.3 | async-start | bytes 3538944 | tf_op jit(solution)/shard_map/all_gather | solution.py:194
  7.2 0.9 copy-start.10
  58.6 13.8 %collective-permute-start = (f32[128,1536]{1,0:T(8,128)S(1)}, f32[128,1536]{1,0:T(8,128)S(1)}, u32[]{:S(2)}, u32[]{:S(2)}) collective-permute-start(f32[128,1536]{1,0:T(8,128)S(1)} %get-tuple-element.11.own_ref), channel_id=1, source_target_pairs={{0,8},{8,0},{1,9},{9,1},{2,10},{10,2},{3,11},{11,3},{4,12},{12,4},... | collective-permute-start | bytes 2359304 | tf_op jit(solution)/shard_map/ppermute | solution.py:162
  68.4 0.9 copy-start.2
  69.3 3.0 %collective-permute-start.1 = (s32[128]{0:T(128)S(1)}, s32[128]{0:T(128)S(1)}, u32[]{:S(2)}, u32[]{:S(2)}) collective-permute-start(s32[128]{0:T(128)S(1)} %copy-done.11), channel_id=1, source_target_pairs={{0,8},{8,0},{1,9},{9,1},{2,10},{10,2},{3,11},{11,3},{4,12},{12,4},... | collective-permute-start | bytes 1544 | tf_op jit(solution)/shard_map/ppermute | solution.py:162
  72.4 0.9 copy-start.5
  82.8 1.9 %copy-start = (f32[512,1536]{1,0:T(8,128)S(1)}, f32[512,1536]{1,0:T(8,128)}, u32[]{:S(2)}) copy-start(f32[512,1536]{1,0:T(8,128)} %all-gather.3.cloned.1.call-done.cols_hbm.cols_ref) | copy-start | bytes 9437188
  84.7 1.1 copy-start.3
  85.9 1.1 copy-start.6
  87.0 44.7 %copy-start.1 = (f32[512,1536]{1,0:T(8,128)S(1)}, f32[512,1536]{1,0:T(8,128)}, u32[]{:S(2)}) copy-start(f32[512,1536]{1,0:T(8,128)} %all-gather.3.cloned.1.call-done.cols_hbm.cols_ref) | copy-start | bytes 9437188
  91.6 0.8 copy-start.8
  92.4 39.3 %all-to-all-start.1 = ((f32[32,8,128]{2,1,0:T(8,128)}), f32[32,8,128]{2,1,0:T(8,128)S(1)}, u32[]{:S(2)}, u32[]{:S(2)}) async-start(f32[32,8,128]{2,1,0:T(8,128)} %get-tuple-element.14), calls=%async_computation.1 | async-start | bytes 262144 | tf_op jit(solution)/shard_map/all_to_all | solution.py:166
  131.7 1.1 copy-start.4
  132.8 1.1 copy-start.7
  133.9 1.0 copy-start.9
  137.8 4.2 %collective-permute-start.2 = (f32[8,200,128]{2,1,0:T(8,128)S(1)}, f32[8,200,128]{2,1,0:T(8,128)S(1)}, u32[]{:S(2)}, u32[]{:S(2)}) collective-permute-start(f32[8,200,128]{2,1,0:T(8,128)S(1)} %get-tuple-element.16), channel_id=1, source_target_pairs={{0,8},{8,0},{1,9},{9,1},{2,10},{10,2},{3,11},{11,3},{4,12},{12,4},... | collective-permute-start | bytes 2457608 | tf_op jit(solution)/shard_map/ppermute | solution.py:162
Sparse Core Ops, SparseCore 0:
  33.6 49.2 all-gather.2

commit v4 on v1

--- a/solution.py
+++ b/solution.py
@@ -17,7 +17,7 @@
 INV_TAU = 10.0
 VMEM = pl.BlockSpec(memory_space=pltpu.VMEM)
 SMEM = pl.BlockSpec(memory_space=pltpu.SMEM)
-PARAMS = pltpu.CompilerParams(vmem_limit_bytes=48 * 1024 * 1024)
+PARAMS = pltpu.CompilerParams(vmem_limit_bytes=32 * 1024 * 1024)
 
 
 def f32(*shape):
@@ -112,15 +112,22 @@
     nrow = NCOL // ROWS
     col = jnp.concatenate([colsum[:, c * ROWS:(c + 1) * ROWS] for c in range(nrow)]
                           + [pos, jnp.zeros((7 - nrow, ROWS), jnp.float32)], axis=0)
-    for k in range(NC * NF):
-        row_ref[k] = row
+    row_ref[...] = row
     for k in range(NZ * NYH):
         col_ref[k] = col
 
 
-def grad_kernel(pos_ref, s_ref, own_ref, oth_ref, cols_ref, ownp_ref, othp_ref, rows_ref, cols_l_ref, mine_ref, theirs_ref, w_hi, w_lo):
+def split_kernel(cols_ref, row_ref, hi_ref, lo_ref):
+    step = 128
+    for c in range(0, NCOL, step):
+        h, l = split(cols_ref[c:c + step, :])
+        hi_ref[c:c + step, :] = h
+        lo_ref[c:c + step, :] = l
+
+
+def grad_kernel(pos_ref, s_ref, own_ref, oth_ref, chi_ref, clo_ref, ownp_ref, othp_ref, rows_ref, cols_l_ref, mine_ref, theirs_ref, w_hi, w_lo):
     core = pos_ref[1]
-    row_l = jnp.sum(rows_ref[...], axis=0)
+    row_l = rows_ref[...]
     col_l = jnp.sum(cols_l_ref[...], axis=0)
     nrow = NCOL // ROWS
     col_inv = jnp.concatenate([1.0 / col_l[c:c + 1, :] for c in range(nrow)], axis=1)
@@ -139,7 +146,7 @@
     tail = jnp.concatenate([loss, jnp.zeros((7, ROWS), jnp.float32)], axis=0)
     for c in range(WIDE // step):
         at = slice(c * step, (c + 1) * step)
-        g = INV_TAU * dot3(weights, split(cols_ref[:, at]), ((1,), (0,)))
+        g = INV_TAU * dot3(weights, (chi_ref[:, at], clo_ref[:, at]), ((1,), (0,)))
         for j, (units, out) in enumerate(((own_ref, mine_ref), (oth_ref, theirs_ref))):
             t = (g[j * ROWS:(j + 1) * ROWS, :] - units[:, at] * projs[j]).T
             for p in range(2):
@@ -191,16 +198,20 @@
     oth = swap(own, "core", NC, 1)
     s, row, col = call(
         score_kernel, "scores",
-        [f32(NC * ROWS, NCOL), f32(NC * NF, 8, ROWS), f32(NZ * NYH, 8, ROWS)],
+        [f32(NC * ROWS, NCOL), f32(8, ROWS), f32(NZ * NYH, 8, ROWS)],
         [pos, own, oth, cols, own_p, oth_p],
         [pltpu.VMEM((NC, ROWS, WIDE), jnp.bfloat16)] * 2,
     )
-    rows_l = trade(row, ("core", "yl", "x"))
     cols_l = trade(col, ("z", "yh"))
+    bf16 = jax.ShapeDtypeStruct((NCOL, WIDE), jnp.bfloat16)
+    chi, clo = call(split_kernel, "split", [bf16] * 2, [cols, row])
+    rows_l = row
+    for axis, size, k in (("core", NC, 1), ("x", NX, 1), ("x", NX, 2), ("yl", NYL, 1)):
+        rows_l = rows_l + swap(rows_l, axis, size, k)
     mine, theirs = call(
         grad_kernel, "gradient",
         [f32(NF, PIECE, ROWS)] * 2,
-        [pos, s, own, oth, cols, own_p, oth_p, rows_l, cols_l],
+        [pos, s, own, oth, chi, clo, own_p, oth_p, rows_l, cols_l],
         [pltpu.VMEM((NC, ROWS, NCOL), jnp.bfloat16)] * 2,
     )
     pieces = trade(mine + swap(theirs, "core", NC, 1), feat)

time: 151 us -> 161 us (1.066)
  blocking collectives: 83.3 us -> 54.2 us
  starting transfers between devices: 11.8 us -> 34.5 us
  local copies, waits for them, and re-layouts: 3 us -> 16.3 us
  waiting for transfers between devices: 29.8 us -> 31.6 us
    all_to_all x5 -> x3, blocking collectives: 83.3 us -> 54.2 us  [trade(): return lax.all_to_all(x, axes, 0, 0, tiled=True)]
    ppermute x3 -> x7, starting transfers between devices: 11.7 us -> 25.3 us  [swap(): return lax.ppermute(x, axes, [(i, i ^ k) for i in range(size)])]
    unnamed x6 -> x32, local copies, waits for them, and re-layouts: 2.78 us -> 16 us
    all_to_all x0 -> x1, starting transfers between devices: none -> 9.16 us  [trade(): return lax.all_to_all(x, axes, 0, 0, tiled=True)]
    ppermute x3 -> x7, waiting for transfers between devices: 2.83 us -> 6.42 us  [swap(): return lax.ppermute(x, axes, [(i, i ^ k) for i in range(size)])]
    all_gather x1, waiting for transfers between devices: 27 us -> 25.1 us  [per_device(): cols = lax.all_gather(chunk, 'z', axis=0, tiled=True)]
    pallas_call x6 -> x7, Pallas kernels: 8.87 us -> 8.54 us  [call(): pl.pallas_call(body, out_shape=outs, in_specs=[SMEM if a.shape == (3,) el...]
  transfers between devices with their start and end apart: 4 -> 9, of which waited for: 3 -> 6; matrix products, arithmetic and copies ran while one was open for 0% -> 0% of each run, Pallas kernels for 0% -> 1%
where the time goes in v4:
time: 161 us; the launch traced here: 160 us
  blocking collectives  54.2 us (34%)
  starting transfers between devices  34.5 us (21%)
  waiting for transfers between devices  31.6 us (20%)
  local copies, waits for them, and re-layouts  16.3 us (10%)
  between operations  14.2 us (9%)
  Pallas kernels  8.54 us (5%)
    all_to_all x3, blocking collectives, trade(): return lax.all_to_all(x, axes, 0, 0, tiled=True)  54.2 us
    ppermute x7, starting transfers between devices, swap(): return lax.ppermute(x, axes, [(i, i ^ k) for i in range(size)])  25.3 us
    all_gather x1, waiting for transfers between devices, per_device(): cols = lax.all_gather(chunk, 'z', axis=0, tiled=True)  25.1 us
    unnamed x32, local copies, waits for them, and re-layouts  16 us
    all_to_all x1, starting transfers between devices, trade(): return lax.all_to_all(x, axes, 0, 0, tiled=True)  9.16 us
    pallas_call x7, Pallas kernels, call(): pl.pallas_call(body, out_shape=outs, in_specs=[SMEM if a.shape == (3,) el...  8.54 us
    ppermute x7, waiting for transfers between devices, swap(): return lax.ppermute(x, axes, [(i, i ^ k) for i in range(size)])  6.42 us
  transfers between devices with their start and end apart: 9, of which 6 were waited for; matrix products, arithmetic and copies ran while one was open for 0% of the time, Pallas kernels for 1%

profile of v4, /device:TPU:1, one launch (start us, length us, event | category | flops | bytes accessed | tf_op | source)
XLA Modules:
  0.0 159.5 jit_solution(686425188421522537)
XLA Ops:
  7.2 0.0 all-gather.2.cloned.1.call-start
  7.2 0.9 copy-done.14
  8.1 0.2 chunks.1
  8.3 24.1 %all_to_all.20.piece_ref = f32[32,24,128]{2,1,0:T(8,128)S(1)} all-to-all(f32[32,24,128]{2,1,0:T(8,128)S(1)} %chunks.1), channel_id=1, replica_groups=mesh['z'=8,'yh'=4,'core'=2,'yl'=2,'x'=4] {'yh','yl','x'}, dimensions={0} | all-to-all | bytes 786432 | tf_op jit(solution)/shard_map/all_to_all | solution.py:168
  32.4 1.1 columns.1
  33.4 0.0 all-gather.2.cloned.1.call-update
  33.5 12.9 %all_to_all.21.piece_ref = f32[8,192,128]{2,1,0:T(8,128)S(1)} all-to-all(f32[8,192,128]{2,1,0:T(8,128)S(1)} %get-tuple-element.15), channel_id=1, replica_groups=mesh['z'=8,'yh'=4,'core'=2,'yl'=2,'x'=4] {'yl','x'}, dimensions={0} | all-to-all | bytes 1572864 | tf_op jit(solution)/shard_map/all_to_all | solution.py:168
  46.3 0.5 norm.1
  46.8 5.9 %collective-permute-start = (f32[128,1536]{1,0:T(8,128)S(1)}, f32[128,1536]{1,0:T(8,128)S(1)}, u32[]{:S(2)}, u32[]{:S(2)}) collective-permute-start(f32[128,1536]{1,0:T(8,128)S(1)} %get-tuple-element.16.own_ref), channel_id=1, source_target_pairs={{0,8},{8,0},{1,9},{9,1},{2,10},{10,2},{3,11},{11,3},{4,12},{12,4},... | collective-permute-start | bytes 2359304 | tf_op jit(solution)/shard_map/ppermute | solution.py:164
  52.7 0.9 copy-done.2
  53.6 0.0 copy-done.15
  53.6 1.9 %collective-permute-start.1 = (s32[128]{0:T(128)S(1)}, s32[128]{0:T(128)S(1)}, u32[]{:S(2)}, u32[]{:S(2)}) collective-permute-start(s32[128]{0:T(128)S(1)} %copy-done.15), channel_id=1, source_target_pairs={{0,8},{8,0},{1,9},{9,1},{2,10},{10,2},{3,11},{11,3},{4,12},{12,4},... | collective-permute-start | bytes 1544 | tf_op jit(solution)/shard_map/ppermute | solution.py:164
  55.5 0.1 pad_add_fusion.pos_ref
  55.6 0.1 copy.4.ownp_ref
  55.7 0.9 collective-permute-done.1
  56.6 0.1 copy.5.othp_ref
  56.7 0.0 collective-permute-done.oth_ref
  56.7 0.9 copy-done.5
  57.6 25.1 %all-gather.2.cloned.1.call-done.cols_ref = f32[512,1536]{1,0:T(8,128)} async-done(((f32[64,1536]{1,0:T(8,128)}), f32[512,1536]{1,0:T(8,128)}) %all-gather.2.cloned.1.call-update) | async-done | bytes 3145744 | tf_op jit(solution)/shard_map/all_gather | solution.py:196
  82.8 1.9 %copy-done = f32[512,1536]{1,0:T(8,128)S(1)} copy-done((f32[512,1536]{1,0:T(8,128)S(1)}, f32[512,1536]{1,0:T(8,128)}, u32[]{:S(2)}) %copy-start) | copy-done | bytes 3145752
  84.7 1.1 copy-done.3
  85.8 1.1 copy-done.6
  86.9 2.9 %scores.1 = (f32[256,512]{1,0:T(8,128)S(1)}, f32[8,128]{1,0:T(8,128)S(1)}, f32[32,8,128]{2,1,0:T(8,128)}) custom-call(s32[3]{0:T(128)S(1)} %pad_add_fusion.pos_ref, f32[128,1536]{1,0:T(8,128)S(1)} %copy-done.3, f32[128,1536]{1,0:T(8,128)S(1)} %copy-done.6, f32[512,1536]{1,0:T(8,128)S(1)} %copy-done, s32[128,1]{1,0:T(8,128)S(1)} %copy.4.ownp_ref, ...), custom_call_target="tpu_custom_call" | custom-call | tf_op jit(solution)/shard_map/scores/pallas_call | solution.py:172
  89.8 0.8 copy-done.12
  90.6 9.2 %all-to-all-start.2 = ((f32[32,8,128]{2,1,0:T(8,128)}), f32[32,8,128]{2,1,0:T(8,128)S(1)}, u32[]{:S(2)}, u32[]{:S(2)}) async-start(f32[32,8,128]{2,1,0:T(8,128)} %get-tuple-element.22), calls=%async_computation.2 | async-start | bytes 262144 | tf_op jit(solution)/shard_map/all_to_all | solution.py:168
  99.8 2.9 %collective-permute-start.2 = (f32[8,128]{1,0:T(8,128)S(1)}, f32[8,128]{1,0:T(8,128)S(1)}, u32[]{:S(2)}, u32[]{:S(2)}) collective-permute-start(f32[8,128]{1,0:T(8,128)S(1)} %get-tuple-element.19.row_ref), channel_id=1, source_target_pairs={{0,8},{8,0},{1,9},{9,1},{2,10},{10,2},{3,11},{11,3},{4,12},{12,4},... | collective-permute-start | bytes 12296 | tf_op jit(solution)/shard_map/ppermute | solution.py:164
  102.7 0.8 collective-permute-done.2
  103.5 3.1 %collective-permute-start.3 = (f32[8,128]{1,0:T(8,128)S(1)}, f32[8,128]{1,0:T(8,128)S(1)}, u32[]{:S(2)}, u32[]{:S(2)}) collective-permute-start(f32[8,128]{1,0:T(8,128)S(1)} %add.23), channel_id=1, source_target_pairs={{0,1},{1,0},{2,3},{3,2},{4,5},{5,4},{6,7},{7,6},{8,9},{9,8},{10,11... | collective-permute-start | bytes 12296 | tf_op jit(solution)/shard_map/ppermute | solution.py:164
  106.6 1.5 collective-permute-done.3
  108.2 4.6 %collective-permute-start.4 = (f32[8,128]{1,0:T(8,128)S(1)}, f32[8,128]{1,0:T(8,128)S(1)}, u32[]{:S(2)}, u32[]{:S(2)}) collective-permute-start(f32[8,128]{1,0:T(8,128)S(1)} %add.24), channel_id=1, source_target_pairs={{0,2},{1,3},{2,0},{3,1},{4,6},{5,7},{6,4},{7,5},{8,10},{9,11},{10,... | collective-permute-start | bytes 12296 | tf_op jit(solution)/shard_map/ppermute | solution.py:164
  112.8 1.2 collective-permute-done.4
  114.0 2.2 %collective-permute-start.5 = (f32[8,128]{1,0:T(8,128)S(1)}, f32[8,128]{1,0:T(8,128)S(1)}, u32[]{:S(2)}, u32[]{:S(2)}) collective-permute-start(f32[8,128]{1,0:T(8,128)S(1)} %add.25), channel_id=1, source_target_pairs={{0,4},{4,0},{1,5},{5,1},{2,6},{6,2},{3,7},{7,3},{8,12},{12,8},{9,1... | collective-permute-start | bytes 12296 | tf_op jit(solution)/shard_map/ppermute | solution.py:164
  116.2 0.5 split.1
  116.7 1.2 copy-done.8
  117.9 1.1 copy-done.10
  119.0 0.0 collective-permute-done.5
  119.0 0.0 all-to-all-done.2.cols_l_ref
  119.0 1.1 copy-done.4
  120.2 1.1 copy-done.7
  121.3 1.4 copy-done.9
  122.7 1.4 copy-done.11
  124.1 1.0 copy-done.13
  125.1 2.8 %gradient.1 = (f32[8,200,128]{2,1,0:T(8,128)S(1)}, f32[8,200,128]{2,1,0:T(8,128)S(1)}) custom-call(s32[3]{0:T(128)S(1)} %pad_add_fusion.pos_ref, f32[256,512]{1,0:T(8,128)S(1)} %copy-done.13, f32[128,1536]{1,0:T(8,128)S(1)} %copy-done.4, f32[128,1536]{1,0:T(8,128)S(1)} %copy-done.7, bf16[512,1536]{1,0:T(8,128)(2,1)S(1)} %copy-done.9, ...), custom_call_target="tpu_custom_call" | custom-call | tf_op jit(solution)/shard_map/gradient/pallas_call | solution.py:172
  128.0 4.7 %collective-permute-start.6 = (f32[8,200,128]{2,1,0:T(8,128)S(1)}, f32[8,200,128]{2,1,0:T(8,128)S(1)}, u32[]{:S(2)}, u32[]{:S(2)}) collective-permute-start(f32[8,200,128]{2,1,0:T(8,128)S(1)} %get-tuple-element.24), channel_id=1, source_target_pairs={{0,8},{8,0},{1,9},{9,1},{2,10},{10,2},{3,11},{11,3},{4,12},{12,4},... | collective-permute-start | bytes 2457608 | tf_op jit(solution)/shard_map/ppermute | solution.py:164
  132.7 1.9 %collective-permute-done.6 = f32[8,200,128]{2,1,0:T(8,128)S(1)} collective-permute-done((f32[8,200,128]{2,1,0:T(8,128)S(1)}, f32[8,200,128]{2,1,0:T(8,128)S(1)}, u32[]{:S(2)}, u32[]{:S(2)}) %collective-permute-start.6) | collective-permute-done | bytes 819232 | tf_op jit(solution)/shard_map/ppermute | solution.py:164
  134.6 0.1 add.27
  134.7 17.2 %all_to_all.22.piece_ref = f32[8,200,128]{2,1,0:T(8,128)S(1)} all-to-all(f32[8,200,128]{2,1,0:T(8,128)S(1)} %add.27), channel_id=1, replica_groups=mesh['z'=8,'yh'=4,'core'=2,'yl'=2,'x'=4] {'yl','x'}, dimensions={0} | all-to-all | bytes 1638400 | tf_op jit(solution)/shard_map/all_to_all | solution.py:168
  152.0 0.7 finish.1
  (21 shorter events, 0.0 us)
Async XLA Ops:
  7.2 75.6 %all-gather.2.cloned.1.call-start = ((), (), s32[]{:S(2)}) async-start(), calls=%async_computation.4 | async-start | bytes 3538944 | tf_op jit(solution)/shard_map/all_gather | solution.py:196
  7.2 0.9 copy-start.14
  32.4 21.2 %copy-start.15 = (s32[128]{0:T(128)S(1)}, s32[128]{0:T(128)}, u32[]{:S(2)}) copy-start(s32[128]{0:T(128)} %param.3) | copy-start | bytes 1540
  46.8 9.9 %collective-permute-start = (f32[128,1536]{1,0:T(8,128)S(1)}, f32[128,1536]{1,0:T(8,128)S(1)}, u32[]{:S(2)}, u32[]{:S(2)}) collective-permute-start(f32[128,1536]{1,0:T(8,128)S(1)} %get-tuple-element.16.own_ref), channel_id=1, source_target_pairs={{0,8},{8,0},{1,9},{9,1},{2,10},{10,2},{3,11},{11,3},{4,12},{12,4},... | collective-permute-start | bytes 2359304 | tf_op jit(solution)/shard_map/ppermute | solution.py:164
  52.7 0.9 copy-start.2
  53.6 3.0 %collective-permute-start.1 = (s32[128]{0:T(128)S(1)}, s32[128]{0:T(128)S(1)}, u32[]{:S(2)}, u32[]{:S(2)}) collective-permute-start(s32[128]{0:T(128)S(1)} %copy-done.15), channel_id=1, source_target_pairs={{0,8},{8,0},{1,9},{9,1},{2,10},{10,2},{3,11},{11,3},{4,12},{12,4},... | collective-permute-start | bytes 1544 | tf_op jit(solution)/shard_map/ppermute | solution.py:164
  56.7 0.9 copy-start.5
  82.8 1.9 %copy-start = (f32[512,1536]{1,0:T(8,128)S(1)}, f32[512,1536]{1,0:T(8,128)}, u32[]{:S(2)}) copy-start(f32[512,1536]{1,0:T(8,128)} %all-gather.2.cloned.1.call-done.cols_ref) | copy-start | bytes 9437188
  84.7 1.1 copy-start.3
  85.8 1.1 copy-start.6
  86.9 29.3 %copy-start.1 = (f32[512,1536]{1,0:T(8,128)S(1)}, f32[512,1536]{1,0:T(8,128)}, u32[]{:S(2)}) copy-start(f32[512,1536]{1,0:T(8,128)} %all-gather.2.cloned.1.call-done.cols_ref) | copy-start | bytes 9437188
  89.8 0.8 copy-start.12
  90.6 28.4 %all-to-all-start.2 = ((f32[32,8,128]{2,1,0:T(8,128)}), f32[32,8,128]{2,1,0:T(8,128)S(1)}, u32[]{:S(2)}, u32[]{:S(2)}) async-start(f32[32,8,128]{2,1,0:T(8,128)} %get-tuple-element.22), calls=%async_computation.2 | async-start | bytes 262144 | tf_op jit(solution)/shard_map/all_to_all | solution.py:168
  99.8 3.7 %collective-permute-start.2 = (f32[8,128]{1,0:T(8,128)S(1)}, f32[8,128]{1,0:T(8,128)S(1)}, u32[]{:S(2)}, u32[]{:S(2)}) collective-permute-start(f32[8,128]{1,0:T(8,128)S(1)} %get-tuple-element.19.row_ref), channel_id=1, source_target_pairs={{0,8},{8,0},{1,9},{9,1},{2,10},{10,2},{3,11},{11,3},{4,12},{12,4},... | collective-permute-start | bytes 12296 | tf_op jit(solution)/shard_map/ppermute | solution.py:164
  103.5 4.6 %collective-permute-start.3 = (f32[8,128]{1,0:T(8,128)S(1)}, f32[8,128]{1,0:T(8,128)S(1)}, u32[]{:S(2)}, u32[]{:S(2)}) collective-permute-start(f32[8,128]{1,0:T(8,128)S(1)} %add.23), channel_id=1, source_target_pairs={{0,1},{1,0},{2,3},{3,2},{4,5},{5,4},{6,7},{7,6},{8,9},{9,8},{10,11... | collective-permute-start | bytes 12296 | tf_op jit(solution)/shard_map/ppermute | solution.py:164
  108.2 5.8 %collective-permute-start.4 = (f32[8,128]{1,0:T(8,128)S(1)}, f32[8,128]{1,0:T(8,128)S(1)}, u32[]{:S(2)}, u32[]{:S(2)}) collective-permute-start(f32[8,128]{1,0:T(8,128)S(1)} %add.24), channel_id=1, source_target_pairs={{0,2},{1,3},{2,0},{3,1},{4,6},{5,7},{6,4},{7,5},{8,10},{9,11},{10,... | collective-permute-start | bytes 12296 | tf_op jit(solution)/shard_map/ppermute | solution.py:164
  114.0 5.0 %collective-permute-start.5 = (f32[8,128]{1,0:T(8,128)S(1)}, f32[8,128]{1,0:T(8,128)S(1)}, u32[]{:S(2)}, u32[]{:S(2)}) collective-permute-start(f32[8,128]{1,0:T(8,128)S(1)} %add.25), channel_id=1, source_target_pairs={{0,4},{4,0},{1,5},{5,1},{2,6},{6,2},{3,7},{7,3},{8,12},{12,8},{9,1... | collective-permute-start | bytes 12296 | tf_op jit(solution)/shard_map/ppermute | solution.py:164
  116.7 1.2 copy-start.8
  117.9 1.1 copy-start.10
  119.0 1.1 copy-start.4
  120.2 1.1 copy-start.7
  121.3 1.4 copy-start.9
  122.7 1.4 copy-start.11
  124.1 1.0 copy-start.13
  128.0 6.7 %collective-permute-start.6 = (f32[8,200,128]{2,1,0:T(8,128)S(1)}, f32[8,200,128]{2,1,0:T(8,128)S(1)}, u32[]{:S(2)}, u32[]{:S(2)}) collective-permute-start(f32[8,200,128]{2,1,0:T(8,128)S(1)} %get-tuple-element.24), channel_id=1, source_target_pairs={{0,8},{8,0},{1,9},{9,1},{2,10},{10,2},{3,11},{11,3},{4,12},{12,4},... | collective-permute-start | bytes 2457608 | tf_op jit(solution)/shard_map/ppermute | solution.py:164
Sparse Core Ops, SparseCore 0:
  33.6 49.1 all-gather.1

commit v5 on v1

--- a/solution.py
+++ b/solution.py
@@ -12,7 +12,8 @@
 WIDE = NF * FEAT
 CHUNK = ROWS // NF
 NCOL = NZ * NYH * CHUNK
-PIECE = FEAT + 8
+PIECE = FEAT
+NDP = NZ * NYH * NC
 TOTAL = 8192
 INV_TAU = 10.0
 VMEM = pl.BlockSpec(memory_space=pltpu.VMEM)
@@ -83,7 +84,7 @@
     return col == row, col == part
 
 
-def score_kernel(pos_ref, own_ref, oth_ref, cols_ref, ownp_ref, othp_ref, s_ref, row_ref, col_ref, hi, lo):
+def score_kernel(pos_ref, own_ref, oth_ref, cols_ref, ownp_ref, othp_ref, s_ref, sum_ref, hi, lo):
     core = pos_ref[1]
     for j, ref in enumerate((own_ref, oth_ref)):
         hi[j], lo[j] = split(ref[...])
@@ -91,66 +92,58 @@
     step = 256
     for c in range(0, NCOL, step):
         s_ref[:, c:c + step] = INV_TAU * dot3(rows, split(cols_ref[c:c + step, :]), ((1,), (1,)))
-    colsum = jnp.zeros((1, NCOL), jnp.float32)
     pos = jnp.zeros((1, ROWS), jnp.float32)
-    sums = []
+    sum_ref[...] = jnp.zeros((NDP + 8, ROWS), jnp.float32)
     for j, part in enumerate((ownp_ref, othp_ref)):
         s = s_ref[j * ROWS:(j + 1) * ROWS, :]
         diag, hit = tile_masks(pos_ref, core ^ j, part[...])
         e = jnp.where(diag, 0.0, jnp.exp(s))
-        colsum = colsum + jnp.sum(e, axis=0, keepdims=True)
+        hits = jnp.sum(jnp.where(hit, s, 0.0), axis=0, keepdims=True)
         lanes = e[:, :ROWS]
-        hits = jnp.sum(jnp.where(hit, s, 0.0), axis=0, keepdims=True)
         for c in range(NCOL // ROWS):
             pos = pos + hits[:, c * ROWS:(c + 1) * ROWS]
             if c:
                 lanes = lanes + e[:, c * ROWS:(c + 1) * ROWS]
-        sums.append(jnp.sum(lanes.T, axis=0, keepdims=True))
-    first = core == 0
-    row = jnp.concatenate([jnp.where(first, sums[0], sums[1]), jnp.where(first, sums[1], sums[0]),
-                           jnp.zeros((8 - NC, ROWS), jnp.float32)], axis=0)
-    nrow = NCOL // ROWS
-    col = jnp.concatenate([colsum[:, c * ROWS:(c + 1) * ROWS] for c in range(nrow)]
-                          + [pos, jnp.zeros((7 - nrow, ROWS), jnp.float32)], axis=0)
-    for k in range(NC * NF):
-        row_ref[k] = row
-    for k in range(NZ * NYH):
-        col_ref[k] = col
-
-
-def grad_kernel(pos_ref, s_ref, own_ref, oth_ref, cols_ref, ownp_ref, othp_ref, rows_ref, cols_l_ref, mine_ref, theirs_ref, w_hi, w_lo):
+        sum_ref[pl.ds(pos_ref[0] * NC + (core ^ j), 1), :] = jnp.sum(lanes.T, axis=0, keepdims=True)
+    sum_ref[NDP:NDP + 1, :] = pos
+
+
+def grad_kernel(pos_ref, s_ref, own_ref, oth_ref, cols_ref, ownp_ref, othp_ref, sum_ref, mine_ref, theirs_ref, loss_ref, w_hi, w_lo):
     core = pos_ref[1]
-    row_l = jnp.sum(rows_ref[...], axis=0)
-    col_l = jnp.sum(cols_l_ref[...], axis=0)
-    nrow = NCOL // ROWS
-    col_inv = jnp.concatenate([1.0 / col_l[c:c + 1, :] for c in range(nrow)], axis=1)
-    loss = jnp.sum(jnp.log(col_l[:nrow, :]), axis=0, keepdims=True) - col_l[nrow:nrow + 1, :]
+    zy, me = pos_ref[0], pos_ref[2]
+    every = sum_ref[:NDP, :]
+    logs = jnp.sum(jnp.log(every), axis=0, keepdims=True) - sum_ref[NDP:NDP + 1, :]
+    loss_ref[...] = jnp.sum(logs, axis=1, keepdims=True) / TOTAL
+    dp = lax.broadcasted_iota(jnp.int32, (NDP, NCOL), 0)
+    lane = lax.broadcasted_iota(jnp.int32, (NDP, NCOL), 1)
+    source = lax.broadcasted_iota(jnp.int32, (ROWS, NCOL), 0)
+    target = lax.broadcasted_iota(jnp.int32, (ROWS, NCOL), 1)
+    pick = jnp.where(source == me * CHUNK + target % CHUNK, 1.0, 0.0)
+    spread = lax.dot_general(1.0 / every, pick, (((1,), (0,)), ((), ())), precision=lax.Precision.HIGHEST,
+                             preferred_element_type=jnp.float32)
+    col_inv = jnp.sum(jnp.where(dp == (lane // CHUNK) * NC + core, spread, 0.0), axis=0, keepdims=True)
     projs = []
     for j, part in enumerate((ownp_ref, othp_ref)):
         s = s_ref[j * ROWS:(j + 1) * ROWS, :]
         half = core ^ j
         diag, hit = tile_masks(pos_ref, half, part[...])
-        inv = column(1.0 / jnp.where(half == 0, row_l[0:1, :], row_l[1:2, :]))
+        inv = column(1.0 / sum_ref[pl.ds(zy * NC + half, 1), :])
         w = jnp.where(diag, 0.0, jnp.exp(s) * (inv + col_inv)) - jnp.where(hit, 2.0, 0.0)
         projs.append(jnp.sum(w * s, axis=1, keepdims=True))
         w_hi[j], w_lo[j] = split(w)
     weights = (w_hi[...].reshape(NC * ROWS, NCOL), w_lo[...].reshape(NC * ROWS, NCOL))
     step = 2 * FEAT
-    tail = jnp.concatenate([loss, jnp.zeros((7, ROWS), jnp.float32)], axis=0)
     for c in range(WIDE // step):
         at = slice(c * step, (c + 1) * step)
         g = INV_TAU * dot3(weights, split(cols_ref[:, at]), ((1,), (0,)))
         for j, (units, out) in enumerate(((own_ref, mine_ref), (oth_ref, theirs_ref))):
             t = (g[j * ROWS:(j + 1) * ROWS, :] - units[:, at] * projs[j]).T
             for p in range(2):
-                out[2 * c + p, :FEAT, :] = t[p * FEAT:(p + 1) * FEAT, :]
-                out[2 * c + p, FEAT:, :] = tail
-
-
-def last_kernel(piece_ref, scale_ref, loss_ref, grad_ref):
-    total = jnp.sum(piece_ref[...], axis=0)
-    loss_ref[...] = jnp.sum(total[FEAT:FEAT + 1, :], axis=1, keepdims=True) / TOTAL
-    grad_ref[...] = total[:FEAT, :] * scale_ref[...]
+                out[2 * c + p] = t[p * FEAT:(p + 1) * FEAT, :]
+
+
+def last_kernel(piece_ref, scale_ref, grad_ref):
+    grad_ref[...] = jnp.sum(piece_ref[...], axis=0) * scale_ref[...]
 
 
 def swap(x, axes, size, k):
@@ -189,22 +182,21 @@
     cols = lax.all_gather(chunk, "z", axis=0, tiled=True)
     own, scale = call(norm_kernel, "norm", [f32(ROWS, WIDE), f32(1, ROWS)], [trade(copies, feat)])
     oth = swap(own, "core", NC, 1)
-    s, row, col = call(
+    s, sums = call(
         score_kernel, "scores",
-        [f32(NC * ROWS, NCOL), f32(NC * NF, 8, ROWS), f32(NZ * NYH, 8, ROWS)],
+        [f32(NC * ROWS, NCOL), f32(NDP + 8, ROWS)],
         [pos, own, oth, cols, own_p, oth_p],
         [pltpu.VMEM((NC, ROWS, WIDE), jnp.bfloat16)] * 2,
     )
-    rows_l = trade(row, ("core", "yl", "x"))
-    cols_l = trade(col, ("z", "yh"))
-    mine, theirs = call(
+    sums = lax.psum(sums, ("z", "yh", "core", "yl", "x"))
+    mine, theirs, loss = call(
         grad_kernel, "gradient",
-        [f32(NF, PIECE, ROWS)] * 2,
-        [pos, s, own, oth, cols, own_p, oth_p, rows_l, cols_l],
+        [f32(NF, PIECE, ROWS)] * 2 + [f32(1, 1)],
+        [pos, s, own, oth, cols, own_p, oth_p, sums],
         [pltpu.VMEM((NC, ROWS, NCOL), jnp.bfloat16)] * 2,
     )
     pieces = trade(mine + swap(theirs, "core", NC, 1), feat)
-    loss, grad = call(last_kernel, "finish", [f32(1, 1), f32(FEAT, ROWS)], [pieces, scale])
+    grad, = call(last_kernel, "finish", [f32(FEAT, ROWS)], [pieces, scale])
     return loss.reshape(()), grad.T
 
 

time: 151 us -> 216 us (1.43)
  blocking collectives: 83.3 us -> 148 us
    psum x0 -> x1, blocking collectives: none -> 97 us  [per_device(): sums = lax.psum(sums, ('z', 'yh', 'core', 'yl', 'x'))]
    all_to_all x5 -> x3, blocking collectives: 83.3 us -> 51 us  [trade(): return lax.all_to_all(x, axes, 0, 0, tiled=True)]
where the time goes in v5:
time: 216 us; the launch traced here: 215 us
  blocking collectives  148 us (69%)
  waiting for transfers between devices  29.8 us (14%)
  between operations  14.1 us (7%)
  starting transfers between devices  10.4 us (5%)
  Pallas kernels  9.05 us (4%)
  local copies, waits for them, and re-layouts  3 us (1%)
    psum x1, blocking collectives, per_device(): sums = lax.psum(sums, ('z', 'yh', 'core', 'yl', 'x'))  97 us
    all_to_all x3, blocking collectives, trade(): return lax.all_to_all(x, axes, 0, 0, tiled=True)  51 us
    all_gather x1, waiting for transfers between devices, per_device(): cols = lax.all_gather(chunk, 'z', axis=0, tiled=True)  27 us
    ppermute x3, starting transfers between devices, swap(): return lax.ppermute(x, axes, [(i, i ^ k) for i in range(size)])  10.4 us
    pallas_call x6, Pallas kernels, call(): pl.pallas_call(body, out_shape=outs, in_specs=[SMEM if a.shape == (3,) el...  9.05 us
  transfers between devices with their start and end apart: 4, of which 3 were waited for; matrix products, arithmetic and copies ran while one was open for 0% of the time, Pallas kernels for 0%

profile of v5, /device:TPU:1, one launch (start us, length us, event | category | flops | bytes accessed | tf_op | source)
XLA Modules:
  0.0 214.6 jit_solution(5232178533743680930)
XLA Ops:
  7.2 0.0 copy-start.2
  7.2 0.0 all-gather.2.cloned.1.call-start
  7.2 0.0 copy-start.1
  7.2 0.9 copy-done.1
  8.1 0.2 chunks.1
  8.3 24.1 %all_to_all.15.piece_ref = f32[32,24,128]{2,1,0:T(8,128)S(1)} all-to-all(f32[32,24,128]{2,1,0:T(8,128)S(1)} %chunks.1), channel_id=1, replica_groups=mesh['z'=8,'yh'=4,'core'=2,'yl'=2,'x'=4] {'yh','yl','x'}, dimensions={0} | all-to-all | bytes 786432 | tf_op jit(solution)/shard_map/all_to_all | solution.py:154
  32.4 1.1 columns.1
  33.4 0.0 all-gather.2.cloned.1.call-update
  33.5 12.9 %all_to_all.16.piece_ref = f32[8,192,128]{2,1,0:T(8,128)S(1)} all-to-all(f32[8,192,128]{2,1,0:T(8,128)S(1)} %get-tuple-element.11), channel_id=1, replica_groups=mesh['z'=8,'yh'=4,'core'=2,'yl'=2,'x'=4] {'yl','x'}, dimensions={0} | all-to-all | bytes 1572864 | tf_op jit(solution)/shard_map/all_to_all | solution.py:154
  46.3 0.5 norm.1
  46.8 5.9 %collective-permute-start = (f32[128,1536]{1,0:T(8,128)S(1)}, f32[128,1536]{1,0:T(8,128)S(1)}, u32[]{:S(2)}, u32[]{:S(2)}) collective-permute-start(f32[128,1536]{1,0:T(8,128)S(1)} %get-tuple-element.12.own_ref), channel_id=1, source_target_pairs={{0,8},{8,0},{1,9},{9,1},{2,10},{10,2},{3,11},{11,3},{4,12},{12,4},... | collective-permute-start | bytes 2359304 | tf_op jit(solution)/shard_map/ppermute | solution.py:150
  52.7 0.0 copy-done.2
  52.7 1.9 collective-permute-start.1
  54.7 0.1 pad_add_fusion.pos_ref
  54.8 0.1 copy.4.ownp_ref
  54.9 0.9 collective-permute-done.1
  55.8 0.1 copy.5.othp_ref
  55.9 0.0 collective-permute-done.oth_ref
  55.9 27.0 %all-gather.2.cloned.1.call-done.cols_ref = f32[512,1536]{1,0:T(8,128)} async-done(((f32[64,1536]{1,0:T(8,128)}), f32[512,1536]{1,0:T(8,128)}) %all-gather.2.cloned.1.call-update) | async-done | bytes 3145744 | tf_op jit(solution)/shard_map/all_gather | solution.py:182
  82.8 0.0 copy-start
  82.8 1.9 copy-done
  84.7 2.3 %scores.1 = (f32[256,512]{1,0:T(8,128)S(1)}, f32[72,128]{1,0:T(8,128)S(1)}) custom-call(s32[3]{0:T(128)S(1)} %pad_add_fusion.pos_ref, f32[128,1536]{1,0:T(8,128)S(1)} %get-tuple-element.12.own_ref, f32[128,1536]{1,0:T(8,128)S(1)} %collective-permute-done.oth_ref, f32[512,1536]{1,0:T(8,128)S(1)} %copy-done, s32[128,1]{1,0:T(8,128)S(1)} %copy.4.ownp_ref, ...), custom_call_target="tpu_custom_call" | custom-call | tf_op jit(solution)/shard_map/scores/pallas_call | solution.py:158
  87.0 97.0 %psum.7.sum_ref = f32[72,128]{1,0:T(8,128)S(1)} all-reduce(f32[72,128]{1,0:T(8,128)S(1)} %get-tuple-element.15), channel_id=1, replica_groups=mesh['z'=8,'yh'=4,'core'=2,'yl'=2,'x'=4] {'z','yh','core','yl','x'}, use_global_device_ids=true, to_apply=%region_0.0 | all-reduce | flops 9216 | bytes 73728 | tf_op jit(solution)/shard_map/psum | solution.py:191
  184.1 4.4 %gradient.1 = (f32[8,192,128]{2,1,0:T(8,128)S(1)}, f32[8,192,128]{2,1,0:T(8,128)S(1)}, f32[1,1]{1,0:T(1,128)}) custom-call(s32[3]{0:T(128)S(1)} %pad_add_fusion.pos_ref, f32[256,512]{1,0:T(8,128)S(1)} %get-tuple-element.14.s_ref, f32[128,1536]{1,0:T(8,128)S(1)} %get-tuple-element.12.own_ref, f32[128,1536]{1,0:T(8,128)S(1)} %collective-permute-done.oth_ref, ...), custom_call_target="tpu_custom_call" | custom-call | tf_op jit(solution)/shard_map/gradient/pallas_call | solution.py:158
  188.5 2.6 %collective-permute-start.2 = (f32[8,192,128]{2,1,0:T(8,128)S(1)}, f32[8,192,128]{2,1,0:T(8,128)S(1)}, u32[]{:S(2)}, u32[]{:S(2)}) collective-permute-start(f32[8,192,128]{2,1,0:T(8,128)S(1)} %get-tuple-element.18), channel_id=1, source_target_pairs={{0,8},{8,0},{1,9},{9,1},{2,10},{10,2},{3,11},{11,3},{4,12},{12,4},... | collective-permute-start | bytes 2359304 | tf_op jit(solution)/shard_map/ppermute | solution.py:150
  191.0 1.9 collective-permute-done.2
  192.9 0.1 add.13
  193.1 14.0 %all_to_all.17.piece_ref = f32[8,192,128]{2,1,0:T(8,128)S(1)} all-to-all(f32[8,192,128]{2,1,0:T(8,128)S(1)} %add.13), channel_id=1, replica_groups=mesh['z'=8,'yh'=4,'core'=2,'yl'=2,'x'=4] {'yl','x'}, dimensions={0} | all-to-all | bytes 1572864 | tf_op jit(solution)/shard_map/all_to_all | solution.py:154
  207.0 0.7 finish.1
Async XLA Ops:
  7.2 45.6 %copy-start.2 = (s32[128]{0:T(128)S(1)}, s32[128]{0:T(128)}, u32[]{:S(2)}) copy-start(s32[128]{0:T(128)} %param.3) | copy-start | bytes 1540
  7.2 75.7 %all-gather.2.cloned.1.call-start = ((), (), s32[]{:S(2)}) async-start(), calls=%async_computation.3 | async-start | bytes 3538944 | tf_op jit(solution)/shard_map/all_gather | solution.py:182
  7.2 0.9 copy-start.1
  46.8 9.1 %collective-permute-start = (f32[128,1536]{1,0:T(8,128)S(1)}, f32[128,1536]{1,0:T(8,128)S(1)}, u32[]{:S(2)}, u32[]{:S(2)}) collective-permute-start(f32[128,1536]{1,0:T(8,128)S(1)} %get-tuple-element.12.own_ref), channel_id=1, source_target_pairs={{0,8},{8,0},{1,9},{9,1},{2,10},{10,2},{3,11},{11,3},{4,12},{12,4},... | collective-permute-start | bytes 2359304 | tf_op jit(solution)/shard_map/ppermute | solution.py:150
  52.7 3.0 %collective-permute-start.1 = (s32[128]{0:T(128)S(1)}, s32[128]{0:T(128)S(1)}, u32[]{:S(2)}, u32[]{:S(2)}) collective-permute-start(s32[128]{0:T(128)S(1)} %copy-done.2), channel_id=1, source_target_pairs={{0,8},{8,0},{1,9},{9,1},{2,10},{10,2},{3,11},{11,3},{4,12},{12,4},... | collective-permute-start | bytes 1544 | tf_op jit(solution)/shard_map/ppermute | solution.py:150
  82.8 1.9 copy-start
  188.5 4.5 %collective-permute-start.2 = (f32[8,192,128]{2,1,0:T(8,128)S(1)}, f32[8,192,128]{2,1,0:T(8,128)S(1)}, u32[]{:S(2)}, u32[]{:S(2)}) collective-permute-start(f32[8,192,128]{2,1,0:T(8,128)S(1)} %get-tuple-element.18), channel_id=1, source_target_pairs={{0,8},{8,0},{1,9},{9,1},{2,10},{10,2},{3,11},{11,3},{4,12},{12,4},... | collective-permute-start | bytes 2359304 | tf_op jit(solution)/shard_map/ppermute | solution.py:150
Sparse Core Ops, SparseCore 0:
  33.6 49.2 all-gather.1

commit v6 on v1

--- a/solution.py
+++ b/solution.py
@@ -13,11 +13,13 @@
 CHUNK = ROWS // NF
 NCOL = NZ * NYH * CHUNK
 PIECE = FEAT + 8
+SHARE = NYH * CHUNK // 2
+PART = NZ * SHARE
 TOTAL = 8192
 INV_TAU = 10.0
 VMEM = pl.BlockSpec(memory_space=pltpu.VMEM)
 SMEM = pl.BlockSpec(memory_space=pltpu.SMEM)
-PARAMS = pltpu.CompilerParams(vmem_limit_bytes=48 * 1024 * 1024)
+PARAMS = pltpu.CompilerParams(vmem_limit_bytes=32 * 1024 * 1024)
 
 
 def f32(*shape):
@@ -59,38 +61,46 @@
             out_ref[y * NF + f] = piece
 
 
-def column_kernel(piece_ref, view_ref, unit_ref, copies_ref):
+def column_kernel(piece_ref, first_ref, second_ref):
     for y in range(NYH):
         x = jnp.concatenate([unpack(piece_ref[y * NF + f]) for f in range(NF)], axis=1)
         scale = lax.rsqrt(jnp.sum(x * x, axis=1, keepdims=True) + 1e-06)
-        unit_ref[y * CHUNK:(y + 1) * CHUNK, :] = x * scale
-    for f in range(NF):
-        copies_ref[f] = view_ref[...]
-
-
-def norm_kernel(piece_ref, unit_ref, scale_ref):
-    x = piece_ref[...].reshape(WIDE, ROWS)
-    scale = lax.rsqrt(jnp.sum(x * x, axis=0, keepdims=True) + 1e-06)
-    scale_ref[...] = scale
-    unit_ref[...] = (x * scale).T
+        out, at = (first_ref, y) if y < NYH // 2 else (second_ref, y - NYH // 2)
+        out[at * CHUNK:(at + 1) * CHUNK, :] = x * scale
+
+
+def norm_kernel(pos_ref, piece_ref, own_ref, oth_ref, scale_ref):
+    core = pos_ref[1]
+    for j, out in enumerate((own_ref, oth_ref)):
+        x = piece_ref[core ^ j]
+        scale = lax.rsqrt(jnp.sum(x * x, axis=0, keepdims=True) + 1e-06)
+        if j == 0:
+            scale_ref[...] = scale
+        out[...] = (x * scale).T
 
 
 def tile_masks(pos_ref, half, part):
     zy, core, me = pos_ref[0], pos_ref[1], pos_ref[2]
     lane = lax.broadcasted_iota(jnp.int32, (1, NCOL), 1)
-    col = ((lane // CHUNK) * NC + core) * ROWS + me * CHUNK + lane % CHUNK
+    y = (lane // PART) * (NYH // 2) + (lane % SHARE) // CHUNK
+    z = (lane % PART) // SHARE
+    col = ((z * NYH + y) * NC + core) * ROWS + me * CHUNK + lane % CHUNK
     row = (zy * NC + half) * ROWS + lax.broadcasted_iota(jnp.int32, (ROWS, 1), 0)
     return col == row, col == part
 
 
-def score_kernel(pos_ref, own_ref, oth_ref, cols_ref, ownp_ref, othp_ref, s_ref, row_ref, col_ref, hi, lo):
+def score_kernel(pos_ref, own_ref, oth_ref, first_ref, ownp_ref, othp_ref, *refs):
+    blocks, (s_ref, row_ref, col_ref, second_ref, hi, lo) = refs[:NZ], refs[NZ:]
     core = pos_ref[1]
+    z = pos_ref[0] // NYH
+    for k, block in enumerate(blocks):
+        at = pl.multiple_of(((z + NZ - k) % NZ) * SHARE, SHARE)
+        second_ref[pl.ds(at, SHARE), :] = block[...]
     for j, ref in enumerate((own_ref, oth_ref)):
         hi[j], lo[j] = split(ref[...])
     rows = (hi[...].reshape(NC * ROWS, WIDE), lo[...].reshape(NC * ROWS, WIDE))
-    step = 256
-    for c in range(0, NCOL, step):
-        s_ref[:, c:c + step] = INV_TAU * dot3(rows, split(cols_ref[c:c + step, :]), ((1,), (1,)))
+    for i, ref in enumerate((first_ref, second_ref)):
+        s_ref[:, i * PART:(i + 1) * PART] = INV_TAU * dot3(rows, split(ref[...]), ((1,), (1,)))
     colsum = jnp.zeros((1, NCOL), jnp.float32)
     pos = jnp.zeros((1, ROWS), jnp.float32)
     sums = []
@@ -118,7 +128,7 @@
         col_ref[k] = col
 
 
-def grad_kernel(pos_ref, s_ref, own_ref, oth_ref, cols_ref, ownp_ref, othp_ref, rows_ref, cols_l_ref, mine_ref, theirs_ref, w_hi, w_lo):
+def grad_kernel(pos_ref, s_ref, own_ref, oth_ref, first_ref, second_ref, ownp_ref, othp_ref, rows_ref, cols_l_ref, mine_ref, theirs_ref, w_hi, w_lo):
     core = pos_ref[1]
     row_l = jnp.sum(rows_ref[...], axis=0)
     col_l = jnp.sum(cols_l_ref[...], axis=0)
@@ -136,10 +146,14 @@
         w_hi[j], w_lo[j] = split(w)
     weights = (w_hi[...].reshape(NC * ROWS, NCOL), w_lo[...].reshape(NC * ROWS, NCOL))
     step = 2 * FEAT
+    cols = (first_ref, second_ref)
     tail = jnp.concatenate([loss, jnp.zeros((7, ROWS), jnp.float32)], axis=0)
     for c in range(WIDE // step):
         at = slice(c * step, (c + 1) * step)
-        g = INV_TAU * dot3(weights, split(cols_ref[:, at]), ((1,), (0,)))
+        g = INV_TAU * sum(
+            dot3([w[:, i * PART:(i + 1) * PART] for w in weights], split(ref[:, at]), ((1,), (0,)))
+            for i, ref in enumerate(cols)
+        )
         for j, (units, out) in enumerate(((own_ref, mine_ref), (oth_ref, theirs_ref))):
             t = (g[j * ROWS:(j + 1) * ROWS, :] - units[:, at] * projs[j]).T
             for p in range(2):
@@ -155,6 +169,18 @@
 
 def swap(x, axes, size, k):
     return lax.ppermute(x, axes, [(i, i ^ k) for i in range(size)])
+
+
+def around(x):
+    blocks = {0: x}
+    up = down = x
+    for k in range(1, NZ // 2 + 1):
+        up = lax.ppermute(up, "z", [(i, (i + 1) % NZ) for i in range(NZ)])
+        blocks[k] = up
+        if k < NZ // 2:
+            down = lax.ppermute(down, "z", [(i, (i - 1) % NZ) for i in range(NZ)])
+            blocks[NZ - k] = down
+    return [blocks[k] for k in range(NZ)]
 
 
 def trade(x, axes):
@@ -182,17 +208,19 @@
 
     own_p = partner.reshape(ROWS, 1)
     oth_p = swap(partner, "core", NC, 1).reshape(ROWS, 1)
+    whole = lax.all_gather(views.T, ("core", "yl", "x"), axis=0, tiled=True)
     packed = CHUNK * FEAT // ROWS
     chunks, = call(chunk_kernel, "chunks", [f32(NYH * NF, packed, ROWS)], [views.T])
     chunks = trade(chunks, ("yh", "yl", "x"))
-    chunk, copies = call(column_kernel, "columns", [f32(NYH * CHUNK, WIDE), f32(NF, FEAT, ROWS)], [chunks, views.T])
-    cols = lax.all_gather(chunk, "z", axis=0, tiled=True)
-    own, scale = call(norm_kernel, "norm", [f32(ROWS, WIDE), f32(1, ROWS)], [trade(copies, feat)])
-    oth = swap(own, "core", NC, 1)
-    s, row, col = call(
+    first, second = call(column_kernel, "columns", [f32(SHARE, WIDE)] * 2, [chunks])
+    cols = lax.all_gather(first, "z", axis=0, tiled=True)
+    ring = around(second)
+    own, oth, scale = call(norm_kernel, "norm", [f32(ROWS, WIDE)] * 2 + [f32(1, ROWS)],
+                           [pos, whole.reshape(NC, WIDE, ROWS)])
+    s, row, col, rest = call(
         score_kernel, "scores",
-        [f32(NC * ROWS, NCOL), f32(NC * NF, 8, ROWS), f32(NZ * NYH, 8, ROWS)],
-        [pos, own, oth, cols, own_p, oth_p],
+        [f32(NC * ROWS, NCOL), f32(NC * NF, 8, ROWS), f32(NZ * NYH, 8, ROWS), f32(PART, WIDE)],
+        [pos, own, oth, cols, own_p, oth_p, *ring],
         [pltpu.VMEM((NC, ROWS, WIDE), jnp.bfloat16)] * 2,
     )
     rows_l = trade(row, ("core", "yl", "x"))
@@ -200,7 +228,7 @@
     mine, theirs = call(
         grad_kernel, "gradient",
         [f32(NF, PIECE, ROWS)] * 2,
-        [pos, s, own, oth, cols, own_p, oth_p, rows_l, cols_l],
+        [pos, s, own, oth, cols, rest, own_p, oth_p, rows_l, cols_l],
         [pltpu.VMEM((NC, ROWS, NCOL), jnp.bfloat16)] * 2,
     )
     pieces = trade(mine + swap(theirs, "core", NC, 1), feat)

time: 151 us -> 167 us (1.11)
  starting transfers between devices: 11.8 us -> 41.9 us
  blocking collectives: 83.3 us -> 74.5 us
  waiting for transfers between devices: 29.8 us -> 23.9 us
    ppermute x0 -> x7, starting transfers between devices: none -> 27.5 us  [the longest x3 17.7 us: around(): down = lax.ppermute(down, 'z', [(i, (i - 1) % NZ) for i in range(NZ)])]
    all_gather x1 -> x2, waiting for transfers between devices: 27 us -> 17.2 us  [the longest x1 17.2 us: per_device(): cols = lax.all_gather(first, 'z', axis=0, tiled=True)]
    all_to_all x5 -> x4, blocking collectives: 83.3 us -> 74.5 us  [trade(): return lax.all_to_all(x, axes, 0, 0, tiled=True)]
    ppermute x0 -> x7, waiting for transfers between devices: none -> 3.42 us  [the longest x4 3.41 us: around(): up = lax.ppermute(up, 'z', [(i, (i + 1) % NZ) for i in range(NZ)])]
    ppermute x3 -> x2, starting transfers between devices: 11.7 us -> 14.4 us  [swap(): return lax.ppermute(x, axes, [(i, i ^ k) for i in range(size)])]
    unnamed x6 -> x10, local copies, waits for them, and re-layouts: 2.78 us -> 3.72 us
  transfers between devices with their start and end apart: 4 -> 11, of which waited for: 3 -> 6; matrix products, arithmetic and copies ran while one was open for 0% -> 0% of each run, Pallas kernels for 0% -> 1%
where the time goes in v6:
time: 167 us
  blocking collectives  74.5 us (45%)
  starting transfers between devices  41.9 us (25%)
  waiting for transfers between devices  23.9 us (14%)
  between operations  14.2 us (9%)
  Pallas kernels  8.2 us (5%)
  local copies, waits for them, and re-layouts  3.94 us (2%)
    all_to_all x4, blocking collectives, trade(): return lax.all_to_all(x, axes, 0, 0, tiled=True)  74.5 us
    ppermute x3, starting transfers between devices, around(): down = lax.ppermute(down, 'z', [(i, (i - 1) % NZ) for i in range(NZ)])  17.7 us
    all_gather x1, waiting for transfers between devices, per_device(): cols = lax.all_gather(first, 'z', axis=0, tiled=True)  17.2 us
    ppermute x2, starting transfers between devices, swap(): return lax.ppermute(x, axes, [(i, i ^ k) for i in range(size)])  14.4 us
    ppermute x4, starting transfers between devices, around(): up = lax.ppermute(up, 'z', [(i, (i + 1) % NZ) for i in range(NZ)])  9.73 us
    pallas_call x6, Pallas kernels, call(): pl.pallas_call(body, out_shape=outs, in_specs=[SMEM if a.shape == (3,) el...  8.2 us
    unnamed x10, local copies, waits for them, and re-layouts  3.72 us
    ppermute x4, waiting for transfers between devices, around(): up = lax.ppermute(up, 'z', [(i, (i + 1) % NZ) for i in range(NZ)])  3.41 us
  transfers between devices with their start and end apart: 11, of which 6 were waited for; matrix products, arithmetic and copies ran while one was open for 0% of the time, Pallas kernels for 1%

profile of v6, /device:TPU:1, one launch (start us, length us, event | category | flops | bytes accessed | tf_op | source)
XLA Modules:
  0.0 166.8 jit_solution(7660446143388352073)
XLA Ops:
  7.2 0.0 copy-start.4
  7.2 0.0 all-gather.3.cloned.1.call-start
  7.2 0.7 all-gather.3.cloned.1.call-update
  7.9 0.0 all-gather.5.cloned.1.call-start
  8.0 0.0 copy-start.3
  8.0 0.9 copy-done.3
  8.8 0.2 chunks.1
  9.0 24.1 %all_to_all.20.piece_ref = f32[32,24,128]{2,1,0:T(8,128)S(1)} all-to-all(f32[32,24,128]{2,1,0:T(8,128)S(1)} %chunks.1), channel_id=1, replica_groups=mesh['z'=8,'yh'=4,'core'=2,'yl'=2,'x'=4] {'yh','yl','x'}, dimensions={0} | all-to-all | bytes 786432 | tf_op jit(solution)/shard_map/all_to_all | solution.py:187
  33.1 1.0 columns.1
  34.1 0.0 all-gather.5.cloned.1.call-update
  34.1 4.0 %collective-permute-start.1 = (f32[32,1536]{1,0:T(8,128)S(1)}, f32[32,1536]{1,0:T(8,128)S(1)}, u32[]{:S(2)}, u32[]{:S(2)}) collective-permute-start(f32[32,1536]{1,0:T(8,128)S(1)} %get-tuple-element.18.refs_0_), channel_id=1, source_target_pairs={{0,64},{64,128},{128,192},{192,256},{256,320},{320,384},{384,448},... | collective-permute-start | bytes 589832 | tf_op jit(solution)/shard_map/ppermute | solution.py:178
  38.1 8.6 %collective-permute-start.5 = (f32[32,1536]{1,0:T(8,128)S(1)}, f32[32,1536]{1,0:T(8,128)S(1)}, u32[]{:S(2)}, u32[]{:S(2)}) collective-permute-start(f32[32,1536]{1,0:T(8,128)S(1)} %get-tuple-element.18.refs_0_), channel_id=1, source_target_pairs={{0,448},{64,0},{128,64},{192,128},{256,192},{320,256},{384,320},{4... | collective-permute-start | bytes 589832 | tf_op jit(solution)/shard_map/ppermute | solution.py:181
  46.7 1.1 collective-permute-done.1.refs_1_
  47.8 1.9 %collective-permute-start.2 = (f32[32,1536]{1,0:T(8,128)S(1)}, f32[32,1536]{1,0:T(8,128)S(1)}, u32[]{:S(2)}, u32[]{:S(2)}) collective-permute-start(f32[32,1536]{1,0:T(8,128)S(1)} %collective-permute-done.1.refs_1_), channel_id=1, source_target_pairs={{0,64},{64,128},{128,192},{192,256},{256,320},{320,384},{384,448},... | collective-permute-start | bytes 589832 | tf_op jit(solution)/shard_map/ppermute | solution.py:178
  49.7 0.0 collective-permute-done.5.refs_7_
  49.8 4.6 %collective-permute-start.6 = (f32[32,1536]{1,0:T(8,128)S(1)}, f32[32,1536]{1,0:T(8,128)S(1)}, u32[]{:S(2)}, u32[]{:S(2)}) collective-permute-start(f32[32,1536]{1,0:T(8,128)S(1)} %collective-permute-done.5.refs_7_), channel_id=1, source_target_pairs={{0,448},{64,0},{128,64},{192,128},{256,192},{320,256},{384,320},{4... | collective-permute-start | bytes 589832 | tf_op jit(solution)/shard_map/ppermute | solution.py:181
  54.3 1.1 collective-permute-done.2.refs_2_
  55.4 1.9 %collective-permute-start.3 = (f32[32,1536]{1,0:T(8,128)S(1)}, f32[32,1536]{1,0:T(8,128)S(1)}, u32[]{:S(2)}, u32[]{:S(2)}) collective-permute-start(f32[32,1536]{1,0:T(8,128)S(1)} %collective-permute-done.2.refs_2_), channel_id=1, source_target_pairs={{0,64},{64,128},{128,192},{192,256},{256,320},{320,384},{384,448},... | collective-permute-start | bytes 589832 | tf_op jit(solution)/shard_map/ppermute | solution.py:178
  57.4 0.0 collective-permute-done.6.refs_6_
  57.4 4.6 %collective-permute-start.7 = (f32[32,1536]{1,0:T(8,128)S(1)}, f32[32,1536]{1,0:T(8,128)S(1)}, u32[]{:S(2)}, u32[]{:S(2)}) collective-permute-start(f32[32,1536]{1,0:T(8,128)S(1)} %collective-permute-done.6.refs_6_), channel_id=1, source_target_pairs={{0,448},{64,0},{128,64},{192,128},{256,192},{320,256},{384,320},{4... | collective-permute-start | bytes 589832 | tf_op jit(solution)/shard_map/ppermute | solution.py:181
  61.9 1.2 collective-permute-done.3.refs_3_
  63.1 1.9 %collective-permute-start.4 = (f32[32,1536]{1,0:T(8,128)S(1)}, f32[32,1536]{1,0:T(8,128)S(1)}, u32[]{:S(2)}, u32[]{:S(2)}) collective-permute-start(f32[32,1536]{1,0:T(8,128)S(1)} %collective-permute-done.3.refs_3_), channel_id=1, source_target_pairs={{0,64},{64,128},{128,192},{192,256},{256,320},{320,384},{384,448},... | collective-permute-start | bytes 589832 | tf_op jit(solution)/shard_map/ppermute | solution.py:178
  65.1 0.0 copy-done.4
  65.1 10.4 %collective-permute-start = (s32[128]{0:T(128)S(1)}, s32[128]{0:T(128)S(1)}, u32[]{:S(2)}, u32[]{:S(2)}) collective-permute-start(s32[128]{0:T(128)S(1)} %copy-done.4), channel_id=1, source_target_pairs={{0,8},{8,0},{1,9},{9,1},{2,10},{10,2},{3,11},{11,3},{4,12},{12,4},... | collective-permute-start | bytes 1544 | tf_op jit(solution)/shard_map/ppermute | solution.py:171
  75.5 0.1 pad_add_fusion.pos_ref
  75.6 0.1 copy.4.ownp_ref
  75.7 0.6 collective-permute-done
  76.3 0.1 copy.5.othp_ref
  76.4 0.0 all-gather.3.cloned.1.call-done
  76.5 0.0 copy-start.2
  76.5 1.4 copy-done.2
  77.9 1.2 norm.1
  79.1 0.0 collective-permute-done.7.refs_5_
  79.1 0.0 collective-permute-done.4.refs_4_
  79.1 17.2 %all-gather.5.cloned.1.call-done.first_ref = f32[256,1536]{1,0:T(8,128)} async-done(((f32[32,1536]{1,0:T(8,128)}), f32[256,1536]{1,0:T(8,128)}) %all-gather.5.cloned.1.call-update) | async-done | bytes 1572880 | tf_op jit(solution)/shard_map/all_gather | solution.py:216
  96.3 0.0 copy-start
  96.3 1.4 copy-done
  97.7 0.0 copy-start.1
  97.7 2.4 %scores.1 = (f32[256,512]{1,0:T(8,128)S(1)}, f32[16,8,128]{2,1,0:T(8,128)S(1)}, f32[32,8,128]{2,1,0:T(8,128)S(1)}, f32[256,1536]{1,0:T(8,128)S(1)}) custom-call(s32[3]{0:T(128)S(1)} %pad_add_fusion.pos_ref, f32[128,1536]{1,0:T(8,128)S(1)} %get-tuple-element.15.own_ref, f32[128,1536]{1,0:T(8,128)S(1)} %get-tuple-element.16.oth_ref, f32[256,1536]{1,0:T(8,128)S(1)} %copy-done, ...), custom_call_target="tpu_custom_call" | custom-call | tf_op jit(solution)/shard_map/scores/pallas_call | solution.py:191
  100.1 15.6 %all_to_all.21.rows_ref = f32[16,8,128]{2,1,0:T(8,128)S(1)} all-to-all(f32[16,8,128]{2,1,0:T(8,128)S(1)} %get-tuple-element.21), channel_id=1, replica_groups=mesh['z'=8,'yh'=4,'core'=2,'yl'=2,'x'=4] {'core','yl','x'}, dimensions={0} | all-to-all | bytes 131072 | tf_op jit(solution)/shard_map/all_to_all | solution.py:187
  115.7 19.4 %all_to_all.22.cols_l_ref = f32[32,8,128]{2,1,0:T(8,128)S(1)} all-to-all(f32[32,8,128]{2,1,0:T(8,128)S(1)} %get-tuple-element.22), channel_id=1, replica_groups=mesh['z'=8,'yh'=4,'core'=2,'yl'=2,'x'=4] {'z','yh'}, dimensions={0} | all-to-all | bytes 262144 | tf_op jit(solution)/shard_map/all_to_all | solution.py:187
  135.0 0.0 copy-done.1
  135.0 2.8 %gradient.1 = (f32[8,200,128]{2,1,0:T(8,128)S(1)}, f32[8,200,128]{2,1,0:T(8,128)S(1)}) custom-call(s32[3]{0:T(128)S(1)} %pad_add_fusion.pos_ref, f32[256,512]{1,0:T(8,128)S(1)} %get-tuple-element.19.s_ref, f32[128,1536]{1,0:T(8,128)S(1)} %get-tuple-element.15.own_ref, f32[128,1536]{1,0:T(8,128)S(1)} %get-tuple-element.16.oth_ref, f32[256,1536]{1,0:T(8,128)S(1)} %copy-done.1, ...), custom_call_target="tpu_custom_call" | custom-call | tf_op jit(solution)/shard_map/gradient/pallas_call | solution.py:191
  137.8 3.9 %collective-permute-start.8 = (f32[8,200,128]{2,1,0:T(8,128)S(1)}, f32[8,200,128]{2,1,0:T(8,128)S(1)}, u32[]{:S(2)}, u32[]{:S(2)}) collective-permute-start(f32[8,200,128]{2,1,0:T(8,128)S(1)} %get-tuple-element.24), channel_id=1, source_target_pairs={{0,8},{8,0},{1,9},{9,1},{2,10},{10,2},{3,11},{11,3},{4,12},{12,4},... | collective-permute-start | bytes 2457608 | tf_op jit(solution)/shard_map/ppermute | solution.py:171
  141.8 1.9 %collective-permute-done.8 = f32[8,200,128]{2,1,0:T(8,128)S(1)} collective-permute-done((f32[8,200,128]{2,1,0:T(8,128)S(1)}, f32[8,200,128]{2,1,0:T(8,128)S(1)}, u32[]{:S(2)}, u32[]{:S(2)}) %collective-permute-start.8) | collective-permute-done | bytes 819232 | tf_op jit(solution)/shard_map/ppermute | solution.py:171
  143.7 0.1 add.11
  143.8 15.5 %all_to_all.23.piece_ref = f32[8,200,128]{2,1,0:T(8,128)S(1)} all-to-all(f32[8,200,128]{2,1,0:T(8,128)S(1)} %add.11), channel_id=1, replica_groups=mesh['z'=8,'yh'=4,'core'=2,'yl'=2,'x'=4] {'yl','x'}, dimensions={0} | all-to-all | bytes 1638400 | tf_op jit(solution)/shard_map/all_to_all | solution.py:187
  159.3 0.7 finish.1
Async XLA Ops:
  7.2 57.9 %copy-start.4 = (s32[128]{0:T(128)S(1)}, s32[128]{0:T(128)}, u32[]{:S(2)}) copy-start(s32[128]{0:T(128)} %param.3) | copy-start | bytes 1540
  7.2 69.3 %all-gather.3.cloned.1.call-start = ((), (), s32[]{:S(2)}) async-start(), calls=%async_computation.4 | async-start | bytes 1671168 | tf_op jit(solution)/shard_map/all_gather | solution.py:211
  7.9 88.4 %all-gather.5.cloned.1.call-start = ((), (), s32[]{:S(2)}) async-start(), calls=%async_computation.5 | async-start | bytes 1769472 | tf_op jit(solution)/shard_map/all_gather | solution.py:216
  8.0 0.9 copy-start.3
  34.1 13.7 %collective-permute-start.1 = (f32[32,1536]{1,0:T(8,128)S(1)}, f32[32,1536]{1,0:T(8,128)S(1)}, u32[]{:S(2)}, u32[]{:S(2)}) collective-permute-start(f32[32,1536]{1,0:T(8,128)S(1)} %get-tuple-element.18.refs_0_), channel_id=1, source_target_pairs={{0,64},{64,128},{128,192},{192,256},{256,320},{320,384},{384,448},... | collective-permute-start | bytes 589832 | tf_op jit(solution)/shard_map/ppermute | solution.py:178
  38.1 11.6 %collective-permute-start.5 = (f32[32,1536]{1,0:T(8,128)S(1)}, f32[32,1536]{1,0:T(8,128)S(1)}, u32[]{:S(2)}, u32[]{:S(2)}) collective-permute-start(f32[32,1536]{1,0:T(8,128)S(1)} %get-tuple-element.18.refs_0_), channel_id=1, source_target_pairs={{0,448},{64,0},{128,64},{192,128},{256,192},{320,256},{384,320},{4... | collective-permute-start | bytes 589832 | tf_op jit(solution)/shard_map/ppermute | solution.py:181
  47.8 7.6 %collective-permute-start.2 = (f32[32,1536]{1,0:T(8,128)S(1)}, f32[32,1536]{1,0:T(8,128)S(1)}, u32[]{:S(2)}, u32[]{:S(2)}) collective-permute-start(f32[32,1536]{1,0:T(8,128)S(1)} %collective-permute-done.1.refs_1_), channel_id=1, source_target_pairs={{0,64},{64,128},{128,192},{192,256},{256,320},{320,384},{384,448},... | collective-permute-start | bytes 589832 | tf_op jit(solution)/shard_map/ppermute | solution.py:178
  49.8 7.6 %collective-permute-start.6 = (f32[32,1536]{1,0:T(8,128)S(1)}, f32[32,1536]{1,0:T(8,128)S(1)}, u32[]{:S(2)}, u32[]{:S(2)}) collective-permute-start(f32[32,1536]{1,0:T(8,128)S(1)} %collective-permute-done.5.refs_7_), channel_id=1, source_target_pairs={{0,448},{64,0},{128,64},{192,128},{256,192},{320,256},{384,320},{4... | collective-permute-start | bytes 589832 | tf_op jit(solution)/shard_map/ppermute | solution.py:181
  55.4 7.7 %collective-permute-start.3 = (f32[32,1536]{1,0:T(8,128)S(1)}, f32[32,1536]{1,0:T(8,128)S(1)}, u32[]{:S(2)}, u32[]{:S(2)}) collective-permute-start(f32[32,1536]{1,0:T(8,128)S(1)} %collective-permute-done.2.refs_2_), channel_id=1, source_target_pairs={{0,64},{64,128},{128,192},{192,256},{256,320},{320,384},{384,448},... | collective-permute-start | bytes 589832 | tf_op jit(solution)/shard_map/ppermute | solution.py:178
  57.4 21.7 %collective-permute-start.7 = (f32[32,1536]{1,0:T(8,128)S(1)}, f32[32,1536]{1,0:T(8,128)S(1)}, u32[]{:S(2)}, u32[]{:S(2)}) collective-permute-start(f32[32,1536]{1,0:T(8,128)S(1)} %collective-permute-done.6.refs_6_), channel_id=1, source_target_pairs={{0,448},{64,0},{128,64},{192,128},{256,192},{320,256},{384,320},{4... | collective-permute-start | bytes 589832 | tf_op jit(solution)/shard_map/ppermute | solution.py:181
  63.1 16.0 %collective-permute-start.4 = (f32[32,1536]{1,0:T(8,128)S(1)}, f32[32,1536]{1,0:T(8,128)S(1)}, u32[]{:S(2)}, u32[]{:S(2)}) collective-permute-start(f32[32,1536]{1,0:T(8,128)S(1)} %collective-permute-done.3.refs_3_), channel_id=1, source_target_pairs={{0,64},{64,128},{128,192},{192,256},{256,320},{320,384},{384,448},... | collective-permute-start | bytes 589832 | tf_op jit(solution)/shard_map/ppermute | solution.py:178
  65.1 11.2 %collective-permute-start = (s32[128]{0:T(128)S(1)}, s32[128]{0:T(128)S(1)}, u32[]{:S(2)}, u32[]{:S(2)}) collective-permute-start(s32[128]{0:T(128)S(1)} %copy-done.4), channel_id=1, source_target_pairs={{0,8},{8,0},{1,9},{9,1},{2,10},{10,2},{3,11},{11,3},{4,12},{12,4},... | collective-permute-start | bytes 1544 | tf_op jit(solution)/shard_map/ppermute | solution.py:171
  76.5 1.4 copy-start.2
  96.3 1.4 copy-start
  97.7 37.3 %copy-start.1 = (f32[256,1536]{1,0:T(8,128)S(1)}, f32[256,1536]{1,0:T(8,128)}, u32[]{:S(2)}) copy-start(f32[256,1536]{1,0:T(8,128)} %all-gather.5.cloned.1.call-done.first_ref) | copy-start | bytes 4718596
  137.8 5.9 %collective-permute-start.8 = (f32[8,200,128]{2,1,0:T(8,128)S(1)}, f32[8,200,128]{2,1,0:T(8,128)S(1)}, u32[]{:S(2)}, u32[]{:S(2)}) collective-permute-start(f32[8,200,128]{2,1,0:T(8,128)S(1)} %get-tuple-element.24), channel_id=1, source_target_pairs={{0,8},{8,0},{1,9},{9,1},{2,10},{10,2},{3,11},{11,3},{4,12},{12,4},... | collective-permute-start | bytes 2457608 | tf_op jit(solution)/shard_map/ppermute | solution.py:171
Sparse Core Ops, SparseCore 0:
  10.2 44.3 all-gather.2
  56.6 39.6 all-gather.4

commit v7 on v1

--- a/solution.py
+++ b/solution.py
@@ -13,6 +13,9 @@
 CHUNK = ROWS // NF
 NCOL = NZ * NYH * CHUNK
 PIECE = FEAT + 8
+PACKED = CHUNK * FEAT // ROWS
+ORDER = [low * NX + x for x in range(NX) for low in range(NYL)]
+Z = ("zh", "zl")
 TOTAL = 8192
 INV_TAU = 10.0
 VMEM = pl.BlockSpec(memory_space=pltpu.VMEM)
@@ -51,17 +54,29 @@
     return jnp.concatenate([x[:CHUNK, :], jnp.concatenate([tail[:, :rest], tail[:, rest:]], axis=0)], axis=1)
 
 
-def chunk_kernel(view_ref, out_ref):
-    x = view_ref[...].T
-    for f in range(NF):
-        piece = pack(x[f * CHUNK:(f + 1) * CHUNK, :])
+def chunk_kernel(pos_ref, view_ref, keep_ref, send_ref, copy_ref, held):
+    copy_ref[...] = view_ref[...]
+    held[...] = view_ref[...].T
+    low = pos_ref[2] // NX
+    for ref, half in ((keep_ref, low), (send_ref, 1 - low)):
+        for x in range(NX):
+            at = pl.multiple_of((half * NX + x) * CHUNK, CHUNK)
+            ref[x] = pack(held[pl.ds(at, CHUNK), :])
+
+
+def pair_kernel(pos_ref, kept_ref, got_ref, out_ref):
+    first = pos_ref[2] // NX == 0
+    for x in range(NX):
+        kept, got = kept_ref[x], got_ref[x]
+        pair = [unpack(jnp.where(first, kept, got)), unpack(jnp.where(first, got, kept))]
+        both = jnp.concatenate(pair, axis=1)
         for y in range(NYH):
-            out_ref[y * NF + f] = piece
+            out_ref[y * NX + x] = both
 
 
 def column_kernel(piece_ref, view_ref, unit_ref, copies_ref):
     for y in range(NYH):
-        x = jnp.concatenate([unpack(piece_ref[y * NF + f]) for f in range(NF)], axis=1)
+        x = jnp.concatenate([piece_ref[y * NX + k] for k in range(NX)], axis=1)
         scale = lax.rsqrt(jnp.sum(x * x, axis=1, keepdims=True) + 1e-06)
         unit_ref[y * CHUNK:(y + 1) * CHUNK, :] = x * scale
     for f in range(NF):
@@ -69,7 +84,7 @@
 
 
 def norm_kernel(piece_ref, unit_ref, scale_ref):
-    x = piece_ref[...].reshape(WIDE, ROWS)
+    x = jnp.concatenate([piece_ref[f] for f in ORDER], axis=0)
     scale = lax.rsqrt(jnp.sum(x * x, axis=0, keepdims=True) + 1e-06)
     scale_ref[...] = scale
     unit_ref[...] = (x * scale).T
@@ -112,9 +127,16 @@
     nrow = NCOL // ROWS
     col = jnp.concatenate([colsum[:, c * ROWS:(c + 1) * ROWS] for c in range(nrow)]
                           + [pos, jnp.zeros((7 - nrow, ROWS), jnp.float32)], axis=0)
-    for k in range(NC * NF):
+    row_ref[...] = row
+    col_ref[...] = col
+
+
+def relay_kernel(row_a, row_b, col_a, col_b, row_ref, col_ref):
+    row = row_a[...] + row_b[...]
+    col = col_a[...] + col_b[...]
+    for k in range(NF):
         row_ref[k] = row
-    for k in range(NZ * NYH):
+    for k in range(NZ // 2 * NYH):
         col_ref[k] = col
 
 
@@ -135,16 +157,16 @@
         projs.append(jnp.sum(w * s, axis=1, keepdims=True))
         w_hi[j], w_lo[j] = split(w)
     weights = (w_hi[...].reshape(NC * ROWS, NCOL), w_lo[...].reshape(NC * ROWS, NCOL))
-    step = 2 * FEAT
+    step = 4 * FEAT
     tail = jnp.concatenate([loss, jnp.zeros((7, ROWS), jnp.float32)], axis=0)
     for c in range(WIDE // step):
         at = slice(c * step, (c + 1) * step)
         g = INV_TAU * dot3(weights, split(cols_ref[:, at]), ((1,), (0,)))
         for j, (units, out) in enumerate(((own_ref, mine_ref), (oth_ref, theirs_ref))):
             t = (g[j * ROWS:(j + 1) * ROWS, :] - units[:, at] * projs[j]).T
-            for p in range(2):
-                out[2 * c + p, :FEAT, :] = t[p * FEAT:(p + 1) * FEAT, :]
-                out[2 * c + p, FEAT:, :] = tail
+            for p in range(4):
+                out[ORDER[4 * c + p], :FEAT, :] = t[p * FEAT:(p + 1) * FEAT, :]
+                out[ORDER[4 * c + p], FEAT:, :] = tail
 
 
 def last_kernel(piece_ref, scale_ref, loss_ref, grad_ref):
@@ -174,7 +196,7 @@
 
 
 def per_device(views, partner):
-    zy = lax.axis_index(("z", "yh"))
+    zy = lax.axis_index(Z + ("yh",))
     core = lax.axis_index("core")
     me = lax.axis_index(("yl", "x"))
     pos = jnp.stack([zy, core, me]).astype(jnp.int32)
@@ -182,21 +204,24 @@
 
     own_p = partner.reshape(ROWS, 1)
     oth_p = swap(partner, "core", NC, 1).reshape(ROWS, 1)
-    packed = CHUNK * FEAT // ROWS
-    chunks, = call(chunk_kernel, "chunks", [f32(NYH * NF, packed, ROWS)], [views.T])
-    chunks = trade(chunks, ("yh", "yl", "x"))
-    chunk, copies = call(column_kernel, "columns", [f32(NYH * CHUNK, WIDE), f32(NF, FEAT, ROWS)], [chunks, views.T])
-    cols = lax.all_gather(chunk, "z", axis=0, tiled=True)
+    keep, send, copy = call(chunk_kernel, "chunks", [f32(NX, PACKED, ROWS)] * 2 + [f32(FEAT, ROWS)], [pos, views.T],
+                      [pltpu.VMEM((ROWS, FEAT), jnp.float32)])
+    pairs, = call(pair_kernel, "pairs", [f32(NYH * NX, CHUNK, 2 * FEAT)], [pos, keep, swap(send, "yl", NYL, 1)])
+    chunk, copies = call(column_kernel, "columns", [f32(NYH * CHUNK, WIDE), f32(NF, FEAT, ROWS)],
+                         [trade(pairs, ("yh", "x")), copy])
+    cols = lax.all_gather(chunk, Z, axis=0, tiled=True)
     own, scale = call(norm_kernel, "norm", [f32(ROWS, WIDE), f32(1, ROWS)], [trade(copies, feat)])
     oth = swap(own, "core", NC, 1)
     s, row, col = call(
         score_kernel, "scores",
-        [f32(NC * ROWS, NCOL), f32(NC * NF, 8, ROWS), f32(NZ * NYH, 8, ROWS)],
+        [f32(NC * ROWS, NCOL), f32(8, ROWS), f32(8, ROWS)],
         [pos, own, oth, cols, own_p, oth_p],
         [pltpu.VMEM((NC, ROWS, WIDE), jnp.bfloat16)] * 2,
     )
-    rows_l = trade(row, ("core", "yl", "x"))
-    cols_l = trade(col, ("z", "yh"))
+    row, col = call(relay_kernel, "relay", [f32(NF, 8, ROWS), f32(NZ // 2 * NYH, 8, ROWS)],
+                    [row, swap(row, "core", NC, 1), col, swap(col, "zl", 2, 1)])
+    rows_l = trade(row, feat)
+    cols_l = trade(col, ("zh", "yh"))
     mine, theirs = call(
         grad_kernel, "gradient",
         [f32(NF, PIECE, ROWS)] * 2,
@@ -209,8 +234,8 @@
 
 
 def solution(mesh):
-    fine = Mesh(mesh.devices.reshape(NZ, NYH, NC, NYL, NX), ("z", "yh", "core", "yl", "x"))
-    rows = ("z", "yh", "core")
+    fine = Mesh(mesh.devices.reshape(NZ // 2, 2, NYH, NC, NYL, NX), Z + ("yh", "core", "yl", "x"))
+    rows = Z + ("yh", "core")
     return jax.shard_map(
         per_device,
         mesh=fine,

time: 151 us -> 164 us (1.086)
  starting transfers between devices: 11.8 us -> 23.6 us
  waiting for transfers between devices: 29.8 us -> 34.7 us
  blocking collectives: 83.3 us -> 78.5 us
    ppermute x3 -> x6, starting transfers between devices: 11.7 us -> 23.6 us  [swap(): return lax.ppermute(x, axes, [(i, i ^ k) for i in range(size)])]
    all_to_all x5, blocking collectives: 83.3 us -> 78.5 us  [trade(): return lax.all_to_all(x, axes, 0, 0, tiled=True)]
    ppermute x3 -> x6, waiting for transfers between devices: 2.83 us -> 6.15 us  [swap(): return lax.ppermute(x, axes, [(i, i ^ k) for i in range(size)])]
    pallas_call x6 -> x8, Pallas kernels: 8.87 us -> 9.54 us  [call(): pl.pallas_call(body, out_shape=outs, in_specs=[SMEM if a.shape == (3,) el...]
  transfers between devices with their start and end apart: 4 -> 7, of which waited for: 3 -> 5; matrix products, arithmetic and copies ran while one was open for 0% -> 0% of each run, Pallas kernels for 0% -> 0%
where the time goes in v7:
time: 164 us
  blocking collectives  78.5 us (48%)
  waiting for transfers between devices  34.7 us (21%)
  starting transfers between devices  23.6 us (14%)
  between operations  14.2 us (9%)
  Pallas kernels  9.54 us (6%)
  local copies, waits for them, and re-layouts  3.01 us (2%)
    all_to_all x5, blocking collectives, trade(): return lax.all_to_all(x, axes, 0, 0, tiled=True)  78.5 us
    all_gather x1, waiting for transfers between devices, per_device(): cols = lax.all_gather(chunk, Z, axis=0, tiled=True)  28.5 us
    ppermute x6, starting transfers between devices, swap(): return lax.ppermute(x, axes, [(i, i ^ k) for i in range(size)])  23.6 us
    pallas_call x8, Pallas kernels, call(): pl.pallas_call(body, out_shape=outs, in_specs=[SMEM if a.shape == (3,) el...  9.54 us
    ppermute x6, waiting for transfers between devices, swap(): return lax.ppermute(x, axes, [(i, i ^ k) for i in range(size)])  6.15 us
  transfers between devices with their start and end apart: 7, of which 5 were waited for; matrix products, arithmetic and copies ran while one was open for 0% of the time, Pallas kernels for 0%

profile of v7, /device:TPU:1, one launch (start us, length us, event | category | flops | bytes accessed | tf_op | source)
XLA Modules:
  0.0 163.7 jit_solution(5615739377505093484)
XLA Ops:
  7.2 0.0 copy-start.2
  7.2 0.0 all-gather.2.cloned.1.call-start
  7.2 0.1 pad_add_fusion.pos_ref
  7.3 0.0 copy-start.1
  7.3 0.9 copy-done.1
  8.2 0.7 chunks.1
  8.9 4.0 %collective-permute-start = (f32[4,24,128]{2,1,0:T(8,128)S(1)}, f32[4,24,128]{2,1,0:T(8,128)S(1)}, u32[]{:S(2)}, u32[]{:S(2)}) collective-permute-start(f32[4,24,128]{2,1,0:T(8,128)S(1)} %get-tuple-element.19), channel_id=1, source_target_pairs={{0,4},{4,0},{1,5},{5,1},{2,6},{6,2},{3,7},{7,3},{8,12},{12,8},{9,1... | collective-permute-start | bytes 147464 | tf_op jit(solution)/shard_map/ppermute | solution.py:179
  13.0 1.5 collective-permute-done.got_ref
  14.4 0.7 pairs.1
  15.1 22.5 %all_to_all.25.piece_ref = f32[16,16,384]{2,1,0:T(8,128)S(1)} all-to-all(f32[16,16,384]{2,1,0:T(8,128)S(1)} %pairs.1), channel_id=1, replica_groups=mesh['zh'=4,'zl'=2,'yh'=4,'core'=2,'yl'=2,'x'=4] {'yh','x'}, dimensions={0} | all-to-all | bytes 786432 | tf_op jit(solution)/shard_map/all_to_all | solution.py:183
  37.7 0.9 columns.1
  38.5 0.0 all-gather.2.cloned.1.call-update
  38.6 11.6 %all_to_all.26.piece_ref = f32[8,192,128]{2,1,0:T(8,128)S(1)} all-to-all(f32[8,192,128]{2,1,0:T(8,128)S(1)} %get-tuple-element.21), channel_id=1, replica_groups=mesh['zh'=4,'zl'=2,'yh'=4,'core'=2,'yl'=2,'x'=4] {'yl','x'}, dimensions={0} | all-to-all | bytes 1572864 | tf_op jit(solution)/shard_map/all_to_all | solution.py:183
  50.2 0.5 norm.1
  50.7 6.5 %collective-permute-start.1 = (f32[128,1536]{1,0:T(8,128)S(1)}, f32[128,1536]{1,0:T(8,128)S(1)}, u32[]{:S(2)}, u32[]{:S(2)}) collective-permute-start(f32[128,1536]{1,0:T(8,128)S(1)} %get-tuple-element.22.own_ref), channel_id=1, source_target_pairs={{0,8},{8,0},{1,9},{9,1},{2,10},{10,2},{3,11},{11,3},{4,12},{12,4},... | collective-permute-start | bytes 2359304 | tf_op jit(solution)/shard_map/ppermute | solution.py:179
  57.2 0.0 copy-done.2
  57.2 1.9 %collective-permute-start.2 = (s32[128]{0:T(128)S(1)}, s32[128]{0:T(128)S(1)}, u32[]{:S(2)}, u32[]{:S(2)}) collective-permute-start(s32[128]{0:T(128)S(1)} %copy-done.2), channel_id=1, source_target_pairs={{0,8},{8,0},{1,9},{9,1},{2,10},{10,2},{3,11},{11,3},{4,12},{12,4},... | collective-permute-start | bytes 1544 | tf_op jit(solution)/shard_map/ppermute | solution.py:179
  59.1 0.1 copy.4.ownp_ref
  59.2 1.0 collective-permute-done.2
  60.2 0.1 copy.5.othp_ref
  60.3 0.0 collective-permute-done.1.oth_ref
  60.3 28.5 %all-gather.2.cloned.1.call-done.cols_ref = f32[512,1536]{1,0:T(8,128)} async-done(((f32[64,1536]{1,0:T(8,128)}), f32[512,1536]{1,0:T(8,128)}) %all-gather.2.cloned.1.call-update) | async-done | bytes 3145744 | tf_op jit(solution)/shard_map/all_gather | solution.py:212
  88.8 0.0 copy-start
  88.8 1.9 %copy-done = f32[512,1536]{1,0:T(8,128)S(1)} copy-done((f32[512,1536]{1,0:T(8,128)S(1)}, f32[512,1536]{1,0:T(8,128)}, u32[]{:S(2)}) %copy-start) | copy-done | bytes 3145752
  90.7 2.3 %scores.1 = (f32[256,512]{1,0:T(8,128)S(1)}, f32[8,128]{1,0:T(8,128)S(1)}, f32[8,128]{1,0:T(8,128)S(1)}) custom-call(s32[3]{0:T(128)S(1)} %pad_add_fusion.pos_ref, f32[128,1536]{1,0:T(8,128)S(1)} %get-tuple-element.22.own_ref, f32[128,1536]{1,0:T(8,128)S(1)} %collective-permute-done.1.oth_ref, f32[512,1536]{1,0:T(8,128)S(1)} %copy-done, ...), custom_call_target="tpu_custom_call" | custom-call | tf_op jit(solution)/shard_map/scores/pallas_call | solution.py:187
  93.0 2.6 %collective-permute-start.3 = (f32[8,128]{1,0:T(8,128)S(1)}, f32[8,128]{1,0:T(8,128)S(1)}, u32[]{:S(2)}, u32[]{:S(2)}) collective-permute-start(f32[8,128]{1,0:T(8,128)S(1)} %get-tuple-element.25.row_a), channel_id=1, source_target_pairs={{0,8},{8,0},{1,9},{9,1},{2,10},{10,2},{3,11},{11,3},{4,12},{12,4},... | collective-permute-start | bytes 12296 | tf_op jit(solution)/shard_map/ppermute | solution.py:179
  95.6 2.6 %collective-permute-start.4 = (f32[8,128]{1,0:T(8,128)S(1)}, f32[8,128]{1,0:T(8,128)S(1)}, u32[]{:S(2)}, u32[]{:S(2)}) collective-permute-start(f32[8,128]{1,0:T(8,128)S(1)} %get-tuple-element.26.col_a), channel_id=1, source_target_pairs={{0,64},{64,0},{1,65},{65,1},{2,66},{66,2},{3,67},{67,3},{4,68},{68... | collective-permute-start | bytes 12296 | tf_op jit(solution)/shard_map/ppermute | solution.py:179
  98.2 0.0 collective-permute-done.3.row_b
  98.2 1.8 %collective-permute-done.4.col_b = f32[8,128]{1,0:T(8,128)S(1)} collective-permute-done((f32[8,128]{1,0:T(8,128)S(1)}, f32[8,128]{1,0:T(8,128)S(1)}, u32[]{:S(2)}, u32[]{:S(2)}) %collective-permute-start.4) | collective-permute-done | bytes 4128 | tf_op jit(solution)/shard_map/ppermute | solution.py:179
  100.0 9.8 %all_to_all.27.rows_ref = f32[8,8,128]{2,1,0:T(8,128)S(1)} all-to-all(f32[8,8,128]{2,1,0:T(8,128)S(1)} %get-tuple-element.27), channel_id=1, replica_groups=mesh['zh'=4,'zl'=2,'yh'=4,'core'=2,'yl'=2,'x'=4] {'yl','x'}, dimensions={0} | all-to-all | bytes 65536 | tf_op jit(solution)/shard_map/all_to_all | solution.py:183
  109.8 19.1 %all_to_all.28.cols_l_ref = f32[16,8,128]{2,1,0:T(8,128)S(1)} all-to-all(f32[16,8,128]{2,1,0:T(8,128)S(1)} %get-tuple-element.28), channel_id=1, replica_groups=mesh['zh'=4,'zl'=2,'yh'=4,'core'=2,'yl'=2,'x'=4] {'zh','yh'}, dimensions={0} | all-to-all | bytes 131072 | tf_op jit(solution)/shard_map/all_to_all | solution.py:183
  128.8 3.7 %gradient.1 = (f32[8,200,128]{2,1,0:T(8,128)S(1)}, f32[8,200,128]{2,1,0:T(8,128)S(1)}) custom-call(s32[3]{0:T(128)S(1)} %pad_add_fusion.pos_ref, f32[256,512]{1,0:T(8,128)S(1)} %get-tuple-element.24.s_ref, f32[128,1536]{1,0:T(8,128)S(1)} %get-tuple-element.22.own_ref, f32[128,1536]{1,0:T(8,128)S(1)} %collective-permute-done.1.oth_ref, ...), custom_call_target="tpu_custom_call" | custom-call | tf_op jit(solution)/shard_map/gradient/pallas_call | solution.py:187
  132.6 6.0 %collective-permute-start.5 = (f32[8,200,128]{2,1,0:T(8,128)S(1)}, f32[8,200,128]{2,1,0:T(8,128)S(1)}, u32[]{:S(2)}, u32[]{:S(2)}) collective-permute-start(f32[8,200,128]{2,1,0:T(8,128)S(1)} %get-tuple-element.30), channel_id=1, source_target_pairs={{0,8},{8,0},{1,9},{9,1},{2,10},{10,2},{3,11},{11,3},{4,12},{12,4},... | collective-permute-start | bytes 2457608 | tf_op jit(solution)/shard_map/ppermute | solution.py:179
  138.6 1.9 %collective-permute-done.5 = f32[8,200,128]{2,1,0:T(8,128)S(1)} collective-permute-done((f32[8,200,128]{2,1,0:T(8,128)S(1)}, f32[8,200,128]{2,1,0:T(8,128)S(1)}, u32[]{:S(2)}, u32[]{:S(2)}) %collective-permute-start.5) | collective-permute-done | bytes 819232 | tf_op jit(solution)/shard_map/ppermute | solution.py:179
  140.6 0.1 add.15
  140.7 15.5 %all_to_all.29.piece_ref = f32[8,200,128]{2,1,0:T(8,128)S(1)} all-to-all(f32[8,200,128]{2,1,0:T(8,128)S(1)} %add.15), channel_id=1, replica_groups=mesh['zh'=4,'zl'=2,'yh'=4,'core'=2,'yl'=2,'x'=4] {'yl','x'}, dimensions={0} | all-to-all | bytes 1638400 | tf_op jit(solution)/shard_map/all_to_all | solution.py:183
  156.2 0.7 finish.1
  (1 shorter events, 0.0 us)
Async XLA Ops:
  7.2 50.0 %copy-start.2 = (s32[128]{0:T(128)S(1)}, s32[128]{0:T(128)}, u32[]{:S(2)}) copy-start(s32[128]{0:T(128)} %param.3) | copy-start | bytes 1540
  7.2 81.6 %all-gather.2.cloned.1.call-start = ((), (), s32[]{:S(2)}) async-start(), calls=%async_computation.5 | async-start | bytes 3538944 | tf_op jit(solution)/shard_map/all_gather | solution.py:212
  7.3 0.9 copy-start.1
  8.9 5.5 %collective-permute-start = (f32[4,24,128]{2,1,0:T(8,128)S(1)}, f32[4,24,128]{2,1,0:T(8,128)S(1)}, u32[]{:S(2)}, u32[]{:S(2)}) collective-permute-start(f32[4,24,128]{2,1,0:T(8,128)S(1)} %get-tuple-element.19), channel_id=1, source_target_pairs={{0,4},{4,0},{1,5},{5,1},{2,6},{6,2},{3,7},{7,3},{8,12},{12,8},{9,1... | collective-permute-start | bytes 147464 | tf_op jit(solution)/shard_map/ppermute | solution.py:179
  50.7 9.6 %collective-permute-start.1 = (f32[128,1536]{1,0:T(8,128)S(1)}, f32[128,1536]{1,0:T(8,128)S(1)}, u32[]{:S(2)}, u32[]{:S(2)}) collective-permute-start(f32[128,1536]{1,0:T(8,128)S(1)} %get-tuple-element.22.own_ref), channel_id=1, source_target_pairs={{0,8},{8,0},{1,9},{9,1},{2,10},{10,2},{3,11},{11,3},{4,12},{12,4},... | collective-permute-start | bytes 2359304 | tf_op jit(solution)/shard_map/ppermute | solution.py:179
  57.2 3.0 %collective-permute-start.2 = (s32[128]{0:T(128)S(1)}, s32[128]{0:T(128)S(1)}, u32[]{:S(2)}, u32[]{:S(2)}) collective-permute-start(s32[128]{0:T(128)S(1)} %copy-done.2), channel_id=1, source_target_pairs={{0,8},{8,0},{1,9},{9,1},{2,10},{10,2},{3,11},{11,3},{4,12},{12,4},... | collective-permute-start | bytes 1544 | tf_op jit(solution)/shard_map/ppermute | solution.py:179
  88.8 1.9 %copy-start = (f32[512,1536]{1,0:T(8,128)S(1)}, f32[512,1536]{1,0:T(8,128)}, u32[]{:S(2)}) copy-start(f32[512,1536]{1,0:T(8,128)} %all-gather.2.cloned.1.call-done.cols_ref) | copy-start | bytes 9437188
  93.0 5.1 %collective-permute-start.3 = (f32[8,128]{1,0:T(8,128)S(1)}, f32[8,128]{1,0:T(8,128)S(1)}, u32[]{:S(2)}, u32[]{:S(2)}) collective-permute-start(f32[8,128]{1,0:T(8,128)S(1)} %get-tuple-element.25.row_a), channel_id=1, source_target_pairs={{0,8},{8,0},{1,9},{9,1},{2,10},{10,2},{3,11},{11,3},{4,12},{12,4},... | collective-permute-start | bytes 12296 | tf_op jit(solution)/shard_map/ppermute | solution.py:179
  95.6 4.4 %collective-permute-start.4 = (f32[8,128]{1,0:T(8,128)S(1)}, f32[8,128]{1,0:T(8,128)S(1)}, u32[]{:S(2)}, u32[]{:S(2)}) collective-permute-start(f32[8,128]{1,0:T(8,128)S(1)} %get-tuple-element.26.col_a), channel_id=1, source_target_pairs={{0,64},{64,0},{1,65},{65,1},{2,66},{66,2},{3,67},{67,3},{4,68},{68... | collective-permute-start | bytes 12296 | tf_op jit(solution)/shard_map/ppermute | solution.py:179
  132.6 8.0 %collective-permute-start.5 = (f32[8,200,128]{2,1,0:T(8,128)S(1)}, f32[8,200,128]{2,1,0:T(8,128)S(1)}, u32[]{:S(2)}, u32[]{:S(2)}) collective-permute-start(f32[8,200,128]{2,1,0:T(8,128)S(1)} %get-tuple-element.30), channel_id=1, source_target_pairs={{0,8},{8,0},{1,9},{9,1},{2,10},{10,2},{3,11},{11,3},{4,12},{12,4},... | collective-permute-start | bytes 2457608 | tf_op jit(solution)/shard_map/ppermute | solution.py:179
Sparse Core Ops, SparseCore 0:
  38.7 50.0 all-gather.1

commit v8 on v1

--- a/solution.py
+++ b/solution.py
@@ -13,11 +13,13 @@
 CHUNK = ROWS // NF
 NCOL = NZ * NYH * CHUNK
 PIECE = FEAT + 8
+BLOCK = NYH * CHUNK
+HALF = BLOCK // 2
 TOTAL = 8192
 INV_TAU = 10.0
 VMEM = pl.BlockSpec(memory_space=pltpu.VMEM)
 SMEM = pl.BlockSpec(memory_space=pltpu.SMEM)
-PARAMS = pltpu.CompilerParams(vmem_limit_bytes=48 * 1024 * 1024)
+PARAMS = pltpu.CompilerParams(vmem_limit_bytes=32 * 1024 * 1024)
 
 
 def f32(*shape):
@@ -59,20 +61,21 @@
             out_ref[y * NF + f] = piece
 
 
-def column_kernel(piece_ref, view_ref, unit_ref, copies_ref):
+def column_kernel(piece_ref, unit_ref):
     for y in range(NYH):
         x = jnp.concatenate([unpack(piece_ref[y * NF + f]) for f in range(NF)], axis=1)
         scale = lax.rsqrt(jnp.sum(x * x, axis=1, keepdims=True) + 1e-06)
         unit_ref[y * CHUNK:(y + 1) * CHUNK, :] = x * scale
-    for f in range(NF):
-        copies_ref[f] = view_ref[...]
-
-
-def norm_kernel(piece_ref, unit_ref, scale_ref):
-    x = piece_ref[...].reshape(WIDE, ROWS)
-    scale = lax.rsqrt(jnp.sum(x * x, axis=0, keepdims=True) + 1e-06)
-    scale_ref[...] = scale
-    unit_ref[...] = (x * scale).T
+
+
+def norm_kernel(pos_ref, piece_ref, own_ref, oth_ref, scale_ref):
+    core = pos_ref[1]
+    for j, out in enumerate((own_ref, oth_ref)):
+        x = piece_ref[core ^ j]
+        scale = lax.rsqrt(jnp.sum(x * x, axis=0, keepdims=True) + 1e-06)
+        if j == 0:
+            scale_ref[...] = scale
+        out[...] = (x * scale).T
 
 
 def tile_masks(pos_ref, half, part):
@@ -83,8 +86,16 @@
     return col == row, col == part
 
 
-def score_kernel(pos_ref, own_ref, oth_ref, cols_ref, ownp_ref, othp_ref, s_ref, row_ref, col_ref, hi, lo):
+def score_kernel(pos_ref, own_ref, oth_ref, ownp_ref, othp_ref, *refs):
+    blocks, (s_ref, row_ref, col_ref, cols_ref, hi, lo) = refs[:-6], refs[-6:]
     core = pos_ref[1]
+    z = pos_ref[0] // NYH
+    for k, block in enumerate(blocks):
+        whole = k < NZ - 1
+        back = (k if k < NZ // 2 else k + 1) if whole else NZ // 2
+        at = ((z + NZ - back) % NZ) * BLOCK + (0 if whole else (k - NZ + 1) * HALF)
+        rows = BLOCK if whole else HALF
+        cols_ref[pl.ds(pl.multiple_of(at, HALF), rows), :] = block[...]
     for j, ref in enumerate((own_ref, oth_ref)):
         hi[j], lo[j] = split(ref[...])
     rows = (hi[...].reshape(NC * ROWS, WIDE), lo[...].reshape(NC * ROWS, WIDE))
@@ -135,16 +146,16 @@
         projs.append(jnp.sum(w * s, axis=1, keepdims=True))
         w_hi[j], w_lo[j] = split(w)
     weights = (w_hi[...].reshape(NC * ROWS, NCOL), w_lo[...].reshape(NC * ROWS, NCOL))
-    step = 2 * FEAT
+    step = 4 * FEAT
     tail = jnp.concatenate([loss, jnp.zeros((7, ROWS), jnp.float32)], axis=0)
     for c in range(WIDE // step):
         at = slice(c * step, (c + 1) * step)
         g = INV_TAU * dot3(weights, split(cols_ref[:, at]), ((1,), (0,)))
         for j, (units, out) in enumerate(((own_ref, mine_ref), (oth_ref, theirs_ref))):
             t = (g[j * ROWS:(j + 1) * ROWS, :] - units[:, at] * projs[j]).T
-            for p in range(2):
-                out[2 * c + p, :FEAT, :] = t[p * FEAT:(p + 1) * FEAT, :]
-                out[2 * c + p, FEAT:, :] = tail
+            for p in range(4):
+                out[4 * c + p, :FEAT, :] = t[p * FEAT:(p + 1) * FEAT, :]
+                out[4 * c + p, FEAT:, :] = tail
 
 
 def last_kernel(piece_ref, scale_ref, loss_ref, grad_ref):
@@ -155,6 +166,16 @@
 
 def swap(x, axes, size, k):
     return lax.ppermute(x, axes, [(i, i ^ k) for i in range(size)])
+
+
+def around(x):
+    def shift(block, by):
+        return lax.ppermute(block, "z", [(i, (i + by) % NZ) for i in range(NZ)])
+    up, down = [x], [x]
+    for _ in range(NZ // 2 - 1):
+        up.append(shift(up[-1], 1))
+        down.append(shift(down[-1], -1))
+    return up + down[:0:-1] + [shift(up[-1][:HALF], 1), shift(down[-1][HALF:], -1)]
 
 
 def trade(x, axes):
@@ -182,17 +203,18 @@
 
     own_p = partner.reshape(ROWS, 1)
     oth_p = swap(partner, "core", NC, 1).reshape(ROWS, 1)
+    whole = lax.all_gather(views.T, ("core", "yl", "x"), axis=0, tiled=True)
     packed = CHUNK * FEAT // ROWS
     chunks, = call(chunk_kernel, "chunks", [f32(NYH * NF, packed, ROWS)], [views.T])
     chunks = trade(chunks, ("yh", "yl", "x"))
-    chunk, copies = call(column_kernel, "columns", [f32(NYH * CHUNK, WIDE), f32(NF, FEAT, ROWS)], [chunks, views.T])
-    cols = lax.all_gather(chunk, "z", axis=0, tiled=True)
-    own, scale = call(norm_kernel, "norm", [f32(ROWS, WIDE), f32(1, ROWS)], [trade(copies, feat)])
-    oth = swap(own, "core", NC, 1)
-    s, row, col = call(
+    chunk, = call(column_kernel, "columns", [f32(BLOCK, WIDE)], [chunks])
+    ring = around(chunk)
+    own, oth, scale = call(norm_kernel, "norm", [f32(ROWS, WIDE)] * 2 + [f32(1, ROWS)],
+                           [pos, whole.reshape(NC, WIDE, ROWS)])
+    s, row, col, cols = call(
         score_kernel, "scores",
-        [f32(NC * ROWS, NCOL), f32(NC * NF, 8, ROWS), f32(NZ * NYH, 8, ROWS)],
-        [pos, own, oth, cols, own_p, oth_p],
+        [f32(NC * ROWS, NCOL), f32(NC * NF, 8, ROWS), f32(NZ * NYH, 8, ROWS), f32(NCOL, WIDE)],
+        [pos, own, oth, own_p, oth_p, *ring],
         [pltpu.VMEM((NC, ROWS, WIDE), jnp.bfloat16)] * 2,
     )
     rows_l = trade(row, ("core", "yl", "x"))

time: 151 us -> 152 us (level)
  starting transfers between devices: 11.8 us -> 48.2 us
  waiting for transfers between devices: 29.8 us -> 11.6 us
  blocking collectives: 83.3 us -> 66.1 us
    ppermute x0 -> x8, starting transfers between devices: none -> 33.4 us  [shift(): return lax.ppermute(block, 'z', [(i, (i + by) % NZ) for i in range(NZ)])]
    all_gather x1, waiting for transfers between devices: 27 us -> 0.01 us  [per_device(): whole = lax.all_gather(views.T, ('core', 'yl', 'x'), axis=0, tiled=True)]
    all_to_all x5 -> x4, blocking collectives: 83.3 us -> 66.1 us  [trade(): return lax.all_to_all(x, axes, 0, 0, tiled=True)]
    ppermute x0 -> x8, waiting for transfers between devices: none -> 8.92 us  [shift(): return lax.ppermute(block, 'z', [(i, (i + by) % NZ) for i in range(NZ)])]
    ppermute x3 -> x2, starting transfers between devices: 11.7 us -> 14.7 us  [swap(): return lax.ppermute(x, axes, [(i, i ^ k) for i in range(size)])]
  transfers between devices with their start and end apart: 4 -> 11, of which waited for: 3 -> 6; matrix products, arithmetic and copies ran while one was open for 0% -> 1% of each run, Pallas kernels for 0% -> 1%
where the time goes in v8:
time: 152 us
  blocking collectives  66.1 us (43%)
  starting transfers between devices  48.2 us (32%)
  between operations  14.2 us (9%)
  waiting for transfers between devices  11.6 us (8%)
  Pallas kernels  7.38 us (5%)
  local copies, waits for them, and re-layouts  3.88 us (3%)
    all_to_all x4, blocking collectives, trade(): return lax.all_to_all(x, axes, 0, 0, tiled=True)  66.1 us
    ppermute x8, starting transfers between devices, shift(): return lax.ppermute(block, 'z', [(i, (i + by) % NZ) for i in range(NZ)])  33.4 us
    ppermute x2, starting transfers between devices, swap(): return lax.ppermute(x, axes, [(i, i ^ k) for i in range(size)])  14.7 us
    ppermute x8, waiting for transfers between devices, shift(): return lax.ppermute(block, 'z', [(i, (i + by) % NZ) for i in range(NZ)])  8.92 us
    pallas_call x6, Pallas kernels, call(): pl.pallas_call(body, out_shape=outs, in_specs=[SMEM if a.shape == (3,) el...  7.38 us
  transfers between devices with their start and end apart: 11, of which 6 were waited for; matrix products, arithmetic and copies ran while one was open for 1% of the time, Pallas kernels for 1%

profile of v8, /device:TPU:1, one launch (start us, length us, event | category | flops | bytes accessed | tf_op | source)
XLA Modules:
  0.0 151.5 jit_solution(8589547092270281671)
XLA Ops:
  7.2 0.0 all-gather.2.cloned.1.call-start
  7.2 0.7 all-gather.2.cloned.1.call-update
  7.9 0.0 copy-start.1
  7.9 0.9 copy-done.1
  8.8 0.2 chunks.1
  9.0 24.1 %all_to_all.20.piece_ref = f32[32,24,128]{2,1,0:T(8,128)S(1)} all-to-all(f32[32,24,128]{2,1,0:T(8,128)S(1)} %chunks.1), channel_id=1, replica_groups=mesh['z'=8,'yh'=4,'core'=2,'yl'=2,'x'=4] {'yh','yl','x'}, dimensions={0} | all-to-all | bytes 786432 | tf_op jit(solution)/shard_map/all_to_all | solution.py:182
  33.1 0.3 columns.1.refs_0_
  33.4 10.7 %collective-permute-start.4 = (f32[64,1536]{1,0:T(8,128)S(1)}, f32[64,1536]{1,0:T(8,128)S(1)}, u32[]{:S(2)}, u32[]{:S(2)}) collective-permute-start(f32[64,1536]{1,0:T(8,128)S(1)} %columns.1.refs_0_), channel_id=1, source_target_pairs={{0,448},{64,0},{128,64},{192,128},{256,192},{320,256},{384,320},{4... | collective-permute-start | bytes 1179656 | tf_op jit(solution)/shard_map/ppermute | solution.py:173
  44.0 1.9 %collective-permute-start.1 = (f32[64,1536]{1,0:T(8,128)S(1)}, f32[64,1536]{1,0:T(8,128)S(1)}, u32[]{:S(2)}, u32[]{:S(2)}) collective-permute-start(f32[64,1536]{1,0:T(8,128)S(1)} %columns.1.refs_0_), channel_id=1, source_target_pairs={{0,64},{64,128},{128,192},{192,256},{256,320},{320,384},{384,448},... | collective-permute-start | bytes 1179656 | tf_op jit(solution)/shard_map/ppermute | solution.py:173
  46.0 2.8 %collective-permute-done.4.refs_6_ = f32[64,1536]{1,0:T(8,128)S(1)} collective-permute-done((f32[64,1536]{1,0:T(8,128)S(1)}, f32[64,1536]{1,0:T(8,128)S(1)}, u32[]{:S(2)}, u32[]{:S(2)}) %collective-permute-start.4) | collective-permute-done | bytes 393248 | tf_op jit(solution)/shard_map/ppermute | solution.py:173
  48.7 5.0 %collective-permute-start.5 = (f32[64,1536]{1,0:T(8,128)S(1)}, f32[64,1536]{1,0:T(8,128)S(1)}, u32[]{:S(2)}, u32[]{:S(2)}) collective-permute-start(f32[64,1536]{1,0:T(8,128)S(1)} %collective-permute-done.4.refs_6_), channel_id=1, source_target_pairs={{0,448},{64,0},{128,64},{192,128},{256,192},{320,256},{384,320},{4... | collective-permute-start | bytes 1179656 | tf_op jit(solution)/shard_map/ppermute | solution.py:173
  53.8 0.0 collective-permute-done.1.refs_1_
  53.8 1.9 %collective-permute-start.2 = (f32[64,1536]{1,0:T(8,128)S(1)}, f32[64,1536]{1,0:T(8,128)S(1)}, u32[]{:S(2)}, u32[]{:S(2)}) collective-permute-start(f32[64,1536]{1,0:T(8,128)S(1)} %collective-permute-done.1.refs_1_), channel_id=1, source_target_pairs={{0,64},{64,128},{128,192},{192,256},{256,320},{320,384},{384,448},... | collective-permute-start | bytes 1179656 | tf_op jit(solution)/shard_map/ppermute | solution.py:173
  55.7 2.8 %collective-permute-done.5.refs_5_ = f32[64,1536]{1,0:T(8,128)S(1)} collective-permute-done((f32[64,1536]{1,0:T(8,128)S(1)}, f32[64,1536]{1,0:T(8,128)S(1)}, u32[]{:S(2)}, u32[]{:S(2)}) %collective-permute-start.5) | collective-permute-done | bytes 393248 | tf_op jit(solution)/shard_map/ppermute | solution.py:173
  58.5 5.0 %collective-permute-start.6 = (f32[64,1536]{1,0:T(8,128)S(1)}, f32[64,1536]{1,0:T(8,128)S(1)}, u32[]{:S(2)}, u32[]{:S(2)}) collective-permute-start(f32[64,1536]{1,0:T(8,128)S(1)} %collective-permute-done.5.refs_5_), channel_id=1, source_target_pairs={{0,448},{64,0},{128,64},{192,128},{256,192},{320,256},{384,320},{4... | collective-permute-start | bytes 1179656 | tf_op jit(solution)/shard_map/ppermute | solution.py:173
  63.5 0.0 collective-permute-done.2.refs_2_
  63.5 1.9 %collective-permute-start.3 = (f32[64,1536]{1,0:T(8,128)S(1)}, f32[64,1536]{1,0:T(8,128)S(1)}, u32[]{:S(2)}, u32[]{:S(2)}) collective-permute-start(f32[64,1536]{1,0:T(8,128)S(1)} %collective-permute-done.2.refs_2_), channel_id=1, source_target_pairs={{0,64},{64,128},{128,192},{192,256},{256,320},{320,384},{384,448},... | collective-permute-start | bytes 1179656 | tf_op jit(solution)/shard_map/ppermute | solution.py:173
  65.4 3.1 %collective-permute-done.6.refs_4_ = f32[64,1536]{1,0:T(8,128)S(1)} collective-permute-done((f32[64,1536]{1,0:T(8,128)S(1)}, f32[64,1536]{1,0:T(8,128)S(1)}, u32[]{:S(2)}, u32[]{:S(2)}) %collective-permute-start.6) | collective-permute-done | bytes 393248 | tf_op jit(solution)/shard_map/ppermute | solution.py:173
  68.5 5.0 %collective-permute-start.8 = (f32[32,1536]{1,0:T(8,128)S(1)}, f32[32,1536]{1,0:T(8,128)S(1)}, u32[]{:S(2)}, u32[]{:S(2)}) collective-permute-start(f32[32,1536]{1,0:T(8,128)S(1)} %slice.9), channel_id=1, source_target_pairs={{0,448},{64,0},{128,64},{192,128},{256,192},{320,256},{384,320},{4... | collective-permute-start | bytes 589832 | tf_op jit(solution)/shard_map/ppermute | solution.py:173
  73.5 0.3 collective-permute-done.3.refs_3_
  73.8 0.7 slice.8
  74.5 1.9 %collective-permute-start.7 = (f32[32,1536]{1,0:T(8,128)}, f32[32,1536]{1,0:T(8,128)S(1)}, u32[]{:S(2)}, u32[]{:S(2)}) collective-permute-start(f32[32,1536]{1,0:T(8,128)} %slice.8), channel_id=1, source_target_pairs={{0,64},{64,128},{128,192},{192,256},{256,320},{320,384},{384,448},... | collective-permute-start | bytes 589832 | tf_op jit(solution)/shard_map/ppermute | solution.py:173
  76.4 10.8 %collective-permute-start = (s32[128]{0:T(128)}, s32[128]{0:T(128)S(1)}, u32[]{:S(2)}, u32[]{:S(2)}) collective-permute-start(s32[128]{0:T(128)} %param.3), channel_id=1, source_target_pairs={{0,8},{8,0},{1,9},{9,1},{2,10},{10,2},{3,11},{11,3},{4,12},{12,4},... | collective-permute-start | bytes 1544 | tf_op jit(solution)/shard_map/ppermute | solution.py:168
  87.3 0.1 pad_add_fusion.pos_ref
  87.4 0.8 copy.4.ownp_ref
  88.1 0.1 collective-permute-done
  88.2 0.1 copy.5.othp_ref
  88.3 0.0 all-gather.2.cloned.1.call-done
  88.3 0.0 copy-start
  88.3 1.4 copy-done
  89.7 1.2 norm.1
  91.0 0.0 collective-permute-done.8.refs_8_
  91.0 0.0 collective-permute-done.7.refs_7_
  91.0 2.5 %scores.1 = (f32[256,512]{1,0:T(8,128)S(1)}, f32[16,8,128]{2,1,0:T(8,128)S(1)}, f32[32,8,128]{2,1,0:T(8,128)S(1)}, f32[512,1536]{1,0:T(8,128)S(1)}) custom-call(s32[3]{0:T(128)S(1)} %pad_add_fusion.pos_ref, f32[128,1536]{1,0:T(8,128)S(1)} %get-tuple-element.13.own_ref, f32[128,1536]{1,0:T(8,128)S(1)} %get-tuple-element.14.oth_ref, ...), custom_call_target="tpu_custom_call" | custom-call | tf_op jit(solution)/shard_map/scores/pallas_call | solution.py:186
  93.5 10.0 %all_to_all.21.rows_ref = f32[16,8,128]{2,1,0:T(8,128)S(1)} all-to-all(f32[16,8,128]{2,1,0:T(8,128)S(1)} %get-tuple-element.17), channel_id=1, replica_groups=mesh['z'=8,'yh'=4,'core'=2,'yl'=2,'x'=4] {'core','yl','x'}, dimensions={0} | all-to-all | bytes 131072 | tf_op jit(solution)/shard_map/all_to_all | solution.py:182
  103.5 16.6 %all_to_all.22.cols_l_ref = f32[32,8,128]{2,1,0:T(8,128)S(1)} all-to-all(f32[32,8,128]{2,1,0:T(8,128)S(1)} %get-tuple-element.18), channel_id=1, replica_groups=mesh['z'=8,'yh'=4,'core'=2,'yl'=2,'x'=4] {'z','yh'}, dimensions={0} | all-to-all | bytes 262144 | tf_op jit(solution)/shard_map/all_to_all | solution.py:182
  120.0 2.5 %gradient.1 = (f32[8,200,128]{2,1,0:T(8,128)S(1)}, f32[8,200,128]{2,1,0:T(8,128)S(1)}) custom-call(s32[3]{0:T(128)S(1)} %pad_add_fusion.pos_ref, f32[256,512]{1,0:T(8,128)S(1)} %get-tuple-element.15.s_ref, f32[128,1536]{1,0:T(8,128)S(1)} %get-tuple-element.13.own_ref, f32[128,1536]{1,0:T(8,128)S(1)} %get-tuple-element.14.oth_ref, ...), custom_call_target="tpu_custom_call" | custom-call | tf_op jit(solution)/shard_map/gradient/pallas_call | solution.py:186
  122.6 3.9 %collective-permute-start.9 = (f32[8,200,128]{2,1,0:T(8,128)S(1)}, f32[8,200,128]{2,1,0:T(8,128)S(1)}, u32[]{:S(2)}, u32[]{:S(2)}) collective-permute-start(f32[8,200,128]{2,1,0:T(8,128)S(1)} %get-tuple-element.20), channel_id=1, source_target_pairs={{0,8},{8,0},{1,9},{9,1},{2,10},{10,2},{3,11},{11,3},{4,12},{12,4},... | collective-permute-start | bytes 2457608 | tf_op jit(solution)/shard_map/ppermute | solution.py:168
  126.5 1.9 %collective-permute-done.9 = f32[8,200,128]{2,1,0:T(8,128)S(1)} collective-permute-done((f32[8,200,128]{2,1,0:T(8,128)S(1)}, f32[8,200,128]{2,1,0:T(8,128)S(1)}, u32[]{:S(2)}, u32[]{:S(2)}) %collective-permute-start.9) | collective-permute-done | bytes 819232 | tf_op jit(solution)/shard_map/ppermute | solution.py:168
  128.4 0.1 add.11
  128.5 15.5 %all_to_all.23.piece_ref = f32[8,200,128]{2,1,0:T(8,128)S(1)} all-to-all(f32[8,200,128]{2,1,0:T(8,128)S(1)} %add.11), channel_id=1, replica_groups=mesh['z'=8,'yh'=4,'core'=2,'yl'=2,'x'=4] {'yl','x'}, dimensions={0} | all-to-all | bytes 1638400 | tf_op jit(solution)/shard_map/all_to_all | solution.py:182
  144.0 0.7 finish.1
  (1 shorter events, 0.0 us)
Async XLA Ops:
  7.2 81.2 %all-gather.2.cloned.1.call-start = ((), (), s32[]{:S(2)}) async-start(), calls=%async_computation.4 | async-start | bytes 1671168 | tf_op jit(solution)/shard_map/all_gather | solution.py:206
  7.9 0.9 copy-start.1
  33.4 15.4 %collective-permute-start.4 = (f32[64,1536]{1,0:T(8,128)S(1)}, f32[64,1536]{1,0:T(8,128)S(1)}, u32[]{:S(2)}, u32[]{:S(2)}) collective-permute-start(f32[64,1536]{1,0:T(8,128)S(1)} %columns.1.refs_0_), channel_id=1, source_target_pairs={{0,448},{64,0},{128,64},{192,128},{256,192},{320,256},{384,320},{4... | collective-permute-start | bytes 1179656 | tf_op jit(solution)/shard_map/ppermute | solution.py:173
  44.0 9.7 %collective-permute-start.1 = (f32[64,1536]{1,0:T(8,128)S(1)}, f32[64,1536]{1,0:T(8,128)S(1)}, u32[]{:S(2)}, u32[]{:S(2)}) collective-permute-start(f32[64,1536]{1,0:T(8,128)S(1)} %columns.1.refs_0_), channel_id=1, source_target_pairs={{0,64},{64,128},{128,192},{192,256},{256,320},{320,384},{384,448},... | collective-permute-start | bytes 1179656 | tf_op jit(solution)/shard_map/ppermute | solution.py:173
  48.7 9.7 %collective-permute-start.5 = (f32[64,1536]{1,0:T(8,128)S(1)}, f32[64,1536]{1,0:T(8,128)S(1)}, u32[]{:S(2)}, u32[]{:S(2)}) collective-permute-start(f32[64,1536]{1,0:T(8,128)S(1)} %collective-permute-done.4.refs_6_), channel_id=1, source_target_pairs={{0,448},{64,0},{128,64},{192,128},{256,192},{320,256},{384,320},{4... | collective-permute-start | bytes 1179656 | tf_op jit(solution)/shard_map/ppermute | solution.py:173
  53.8 9.7 %collective-permute-start.2 = (f32[64,1536]{1,0:T(8,128)S(1)}, f32[64,1536]{1,0:T(8,128)S(1)}, u32[]{:S(2)}, u32[]{:S(2)}) collective-permute-start(f32[64,1536]{1,0:T(8,128)S(1)} %collective-permute-done.1.refs_1_), channel_id=1, source_target_pairs={{0,64},{64,128},{128,192},{192,256},{256,320},{320,384},{384,448},... | collective-permute-start | bytes 1179656 | tf_op jit(solution)/shard_map/ppermute | solution.py:173
  58.5 10.0 %collective-permute-start.6 = (f32[64,1536]{1,0:T(8,128)S(1)}, f32[64,1536]{1,0:T(8,128)S(1)}, u32[]{:S(2)}, u32[]{:S(2)}) collective-permute-start(f32[64,1536]{1,0:T(8,128)S(1)} %collective-permute-done.5.refs_5_), channel_id=1, source_target_pairs={{0,448},{64,0},{128,64},{192,128},{256,192},{320,256},{384,320},{4... | collective-permute-start | bytes 1179656 | tf_op jit(solution)/shard_map/ppermute | solution.py:173
  63.5 10.3 %collective-permute-start.3 = (f32[64,1536]{1,0:T(8,128)S(1)}, f32[64,1536]{1,0:T(8,128)S(1)}, u32[]{:S(2)}, u32[]{:S(2)}) collective-permute-start(f32[64,1536]{1,0:T(8,128)S(1)} %collective-permute-done.2.refs_2_), channel_id=1, source_target_pairs={{0,64},{64,128},{128,192},{192,256},{256,320},{320,384},{384,448},... | collective-permute-start | bytes 1179656 | tf_op jit(solution)/shard_map/ppermute | solution.py:173
  68.5 22.5 %collective-permute-start.8 = (f32[32,1536]{1,0:T(8,128)S(1)}, f32[32,1536]{1,0:T(8,128)S(1)}, u32[]{:S(2)}, u32[]{:S(2)}) collective-permute-start(f32[32,1536]{1,0:T(8,128)S(1)} %slice.9), channel_id=1, source_target_pairs={{0,448},{64,0},{128,64},{192,128},{256,192},{320,256},{384,320},{4... | collective-permute-start | bytes 589832 | tf_op jit(solution)/shard_map/ppermute | solution.py:173
  74.5 16.5 %collective-permute-start.7 = (f32[32,1536]{1,0:T(8,128)}, f32[32,1536]{1,0:T(8,128)S(1)}, u32[]{:S(2)}, u32[]{:S(2)}) collective-permute-start(f32[32,1536]{1,0:T(8,128)} %slice.8), channel_id=1, source_target_pairs={{0,64},{64,128},{128,192},{192,256},{256,320},{320,384},{384,448},... | collective-permute-start | bytes 589832 | tf_op jit(solution)/shard_map/ppermute | solution.py:173
  76.4 11.8 %collective-permute-start = (s32[128]{0:T(128)}, s32[128]{0:T(128)S(1)}, u32[]{:S(2)}, u32[]{:S(2)}) collective-permute-start(s32[128]{0:T(128)} %param.3), channel_id=1, source_target_pairs={{0,8},{8,0},{1,9},{9,1},{2,10},{10,2},{3,11},{11,3},{4,12},{12,4},... | collective-permute-start | bytes 1544 | tf_op jit(solution)/shard_map/ppermute | solution.py:168
  88.3 1.4 copy-start
  122.6 5.9 %collective-permute-start.9 = (f32[8,200,128]{2,1,0:T(8,128)S(1)}, f32[8,200,128]{2,1,0:T(8,128)S(1)}, u32[]{:S(2)}, u32[]{:S(2)}) collective-permute-start(f32[8,200,128]{2,1,0:T(8,128)S(1)} %get-tuple-element.20), channel_id=1, source_target_pairs={{0,8},{8,0},{1,9},{9,1},{2,10},{10,2},{3,11},{11,3},{4,12},{12,4},... | collective-permute-start | bytes 2457608 | tf_op jit(solution)/shard_map/ppermute | solution.py:168
Sparse Core Ops, SparseCore 0:
  10.1 44.5 all-gather.1

commit v9 on v8

--- a/solution.py
+++ b/solution.py
@@ -53,7 +53,9 @@
     return jnp.concatenate([x[:CHUNK, :], jnp.concatenate([tail[:, :rest], tail[:, rest:]], axis=0)], axis=1)
 
 
-def chunk_kernel(view_ref, out_ref):
+def chunk_kernel(view_ref, partner_ref, out_ref, shard_ref):
+    shard_ref[:FEAT, :] = view_ref[...]
+    shard_ref[FEAT:, :] = jnp.broadcast_to(partner_ref[...].astype(jnp.float32), (PIECE - FEAT, ROWS))
     x = view_ref[...].T
     for f in range(NF):
         piece = pack(x[f * CHUNK:(f + 1) * CHUNK, :])
@@ -68,14 +70,18 @@
         unit_ref[y * CHUNK:(y + 1) * CHUNK, :] = x * scale
 
 
-def norm_kernel(pos_ref, piece_ref, own_ref, oth_ref, scale_ref):
+def norm_kernel(pos_ref, piece_ref, own_ref, oth_ref, scale_ref, ownp_ref, othp_ref, hi_ref, lo_ref):
     core = pos_ref[1]
-    for j, out in enumerate((own_ref, oth_ref)):
-        x = piece_ref[core ^ j]
+    for j, (out, part) in enumerate(((own_ref, ownp_ref), (oth_ref, othp_ref))):
+        x = piece_ref[core ^ j, :, :FEAT, :].reshape(WIDE, ROWS)
         scale = lax.rsqrt(jnp.sum(x * x, axis=0, keepdims=True) + 1e-06)
         if j == 0:
             scale_ref[...] = scale
-        out[...] = (x * scale).T
+        units = (x * scale).T
+        out[...] = units
+        part[...] = column(piece_ref[core ^ j, 0, FEAT:FEAT + 1, :]).astype(jnp.int32)
+        at = slice(j * ROWS, (j + 1) * ROWS)
+        hi_ref[at, :], lo_ref[at, :] = split(units)
 
 
 def tile_masks(pos_ref, half, part):
@@ -86,8 +92,8 @@
     return col == row, col == part
 
 
-def score_kernel(pos_ref, own_ref, oth_ref, ownp_ref, othp_ref, *refs):
-    blocks, (s_ref, row_ref, col_ref, cols_ref, hi, lo) = refs[:-6], refs[-6:]
+def score_kernel(pos_ref, hi_ref, lo_ref, ownp_ref, othp_ref, *refs):
+    blocks, (s_ref, row_ref, col_ref, cols_ref) = refs[:-4], refs[-4:]
     core = pos_ref[1]
     z = pos_ref[0] // NYH
     for k, block in enumerate(blocks):
@@ -96,9 +102,7 @@
         at = ((z + NZ - back) % NZ) * BLOCK + (0 if whole else (k - NZ + 1) * HALF)
         rows = BLOCK if whole else HALF
         cols_ref[pl.ds(pl.multiple_of(at, HALF), rows), :] = block[...]
-    for j, ref in enumerate((own_ref, oth_ref)):
-        hi[j], lo[j] = split(ref[...])
-    rows = (hi[...].reshape(NC * ROWS, WIDE), lo[...].reshape(NC * ROWS, WIDE))
+    rows = (hi_ref[...], lo_ref[...])
     step = 256
     for c in range(0, NCOL, step):
         s_ref[:, c:c + step] = INV_TAU * dot3(rows, split(cols_ref[c:c + step, :]), ((1,), (1,)))
@@ -201,21 +205,23 @@
     pos = jnp.stack([zy, core, me]).astype(jnp.int32)
     feat = ("yl", "x")
 
-    own_p = partner.reshape(ROWS, 1)
-    oth_p = swap(partner, "core", NC, 1).reshape(ROWS, 1)
-    whole = lax.all_gather(views.T, ("core", "yl", "x"), axis=0, tiled=True)
     packed = CHUNK * FEAT // ROWS
-    chunks, = call(chunk_kernel, "chunks", [f32(NYH * NF, packed, ROWS)], [views.T])
+    chunks, shard = call(chunk_kernel, "chunks", [f32(NYH * NF, packed, ROWS), f32(PIECE, ROWS)],
+                         [views.T, partner.reshape(1, ROWS)])
+    whole = lax.all_gather(shard, ("core", "yl", "x"), axis=0, tiled=True)
     chunks = trade(chunks, ("yh", "yl", "x"))
     chunk, = call(column_kernel, "columns", [f32(BLOCK, WIDE)], [chunks])
     ring = around(chunk)
-    own, oth, scale = call(norm_kernel, "norm", [f32(ROWS, WIDE)] * 2 + [f32(1, ROWS)],
-                           [pos, whole.reshape(NC, WIDE, ROWS)])
+    ids, bf16 = jax.ShapeDtypeStruct((ROWS, 1), jnp.int32), jax.ShapeDtypeStruct((NC * ROWS, WIDE), jnp.bfloat16)
+    own, oth, scale, own_p, oth_p, hi, lo = call(
+        norm_kernel, "norm",
+        [f32(ROWS, WIDE)] * 2 + [f32(1, ROWS), ids, ids, bf16, bf16],
+        [pos, whole.reshape(NC, NF, PIECE, ROWS)],
+    )
     s, row, col, cols = call(
         score_kernel, "scores",
         [f32(NC * ROWS, NCOL), f32(NC * NF, 8, ROWS), f32(NZ * NYH, 8, ROWS), f32(NCOL, WIDE)],
-        [pos, own, oth, own_p, oth_p, *ring],
-        [pltpu.VMEM((NC, ROWS, WIDE), jnp.bfloat16)] * 2,
+        [pos, hi, lo, own_p, oth_p, *ring],
     )
     rows_l = trade(row, ("core", "yl", "x"))
     cols_l = trade(col, ("z", "yh"))

time: 152 us -> 151 us (level)
  starting transfers between devices: 48.2 us -> 37.1 us
  blocking collectives: 66.1 us -> 71.2 us
  waiting for transfers between devices: 11.6 us -> 16.7 us
    ppermute x2 -> x1, starting transfers between devices: 14.7 us -> 3.6 us  [swap(): return lax.ppermute(x, axes, [(i, i ^ k) for i in range(size)])]
    ppermute x8, waiting for transfers between devices: 8.92 us -> 14.8 us  [shift(): return lax.ppermute(block, 'z', [(i, (i + by) % NZ) for i in range(NZ)])]
    all_to_all x4, blocking collectives: 66.1 us -> 71.2 us  [trade(): return lax.all_to_all(x, axes, 0, 0, tiled=True)]
  transfers between devices with their start and end apart: 11 -> 10, of which waited for: 6 -> 6; matrix products, arithmetic and copies ran while one was open for 1% -> 0% of each run, Pallas kernels for 1% -> 1%
where the time goes in v9:
time: 151 us; the launch traced here: 150 us
  blocking collectives  71.2 us (47%)
  starting transfers between devices  37.1 us (25%)
  waiting for transfers between devices  16.7 us (11%)
  between operations  14.2 us (9%)
  Pallas kernels  7.98 us (5%)
  local copies, waits for them, and re-layouts  3 us (2%)
    all_to_all x4, blocking collectives, trade(): return lax.all_to_all(x, axes, 0, 0, tiled=True)  71.2 us
    ppermute x8, starting transfers between devices, shift(): return lax.ppermute(block, 'z', [(i, (i + by) % NZ) for i in range(NZ)])  33.5 us
    ppermute x8, waiting for transfers between devices, shift(): return lax.ppermute(block, 'z', [(i, (i + by) % NZ) for i in range(NZ)])  14.8 us
    pallas_call x6, Pallas kernels, call(): pl.pallas_call(body, out_shape=outs, in_specs=[SMEM if a.shape == (3,) el...  7.98 us
    ppermute x1, starting transfers between devices, swap(): return lax.ppermute(x, axes, [(i, i ^ k) for i in range(size)])  3.6 us
  transfers between devices with their start and end apart: 10, of which 6 were waited for; matrix products, arithmetic and copies ran while one was open for 0% of the time, Pallas kernels for 1%

profile of v9, /device:TPU:1, one launch (start us, length us, event | category | flops | bytes accessed | tf_op | source)
XLA Modules:
  0.0 150.3 jit_solution(9223725635705006455)
XLA Ops:
  7.2 0.0 all-gather.2.cloned.1.call-start
  7.2 0.0 copy-start.1
  7.2 0.9 copy-done.1
  8.1 0.0 copy-start.2
  8.1 0.7 copy-done.2
  8.8 0.7 chunks.1
  9.5 0.0 all-gather.2.cloned.1.call-update
  9.5 24.1 %all_to_all.20.piece_ref = f32[32,24,128]{2,1,0:T(8,128)S(1)} all-to-all(f32[32,24,128]{2,1,0:T(8,128)S(1)} %get-tuple-element.24), channel_id=1, replica_groups=mesh['z'=8,'yh'=4,'core'=2,'yl'=2,'x'=4] {'yh','yl','x'}, dimensions={0} | all-to-all | bytes 786432 | tf_op jit(solution)/shard_map/all_to_all | solution.py:186
  33.6 0.3 columns.1.refs_0_
  33.9 10.7 %collective-permute-start.3 = (f32[64,1536]{1,0:T(8,128)S(1)}, f32[64,1536]{1,0:T(8,128)S(1)}, u32[]{:S(2)}, u32[]{:S(2)}) collective-permute-start(f32[64,1536]{1,0:T(8,128)S(1)} %columns.1.refs_0_), channel_id=1, source_target_pairs={{0,448},{64,0},{128,64},{192,128},{256,192},{320,256},{384,320},{4... | collective-permute-start | bytes 1179656 | tf_op jit(solution)/shard_map/ppermute | solution.py:177
  44.7 1.9 %collective-permute-start = (f32[64,1536]{1,0:T(8,128)S(1)}, f32[64,1536]{1,0:T(8,128)S(1)}, u32[]{:S(2)}, u32[]{:S(2)}) collective-permute-start(f32[64,1536]{1,0:T(8,128)S(1)} %columns.1.refs_0_), channel_id=1, source_target_pairs={{0,64},{64,128},{128,192},{192,256},{256,320},{320,384},{384,448},... | collective-permute-start | bytes 1179656 | tf_op jit(solution)/shard_map/ppermute | solution.py:177
  46.6 2.8 %collective-permute-done.3.refs_6_ = f32[64,1536]{1,0:T(8,128)S(1)} collective-permute-done((f32[64,1536]{1,0:T(8,128)S(1)}, f32[64,1536]{1,0:T(8,128)S(1)}, u32[]{:S(2)}, u32[]{:S(2)}) %collective-permute-start.3) | collective-permute-done | bytes 393248 | tf_op jit(solution)/shard_map/ppermute | solution.py:177
  49.4 5.0 %collective-permute-start.4 = (f32[64,1536]{1,0:T(8,128)S(1)}, f32[64,1536]{1,0:T(8,128)S(1)}, u32[]{:S(2)}, u32[]{:S(2)}) collective-permute-start(f32[64,1536]{1,0:T(8,128)S(1)} %collective-permute-done.3.refs_6_), channel_id=1, source_target_pairs={{0,448},{64,0},{128,64},{192,128},{256,192},{320,256},{384,320},{4... | collective-permute-start | bytes 1179656 | tf_op jit(solution)/shard_map/ppermute | solution.py:177
  54.4 0.0 collective-permute-done.refs_1_
  54.4 1.9 %collective-permute-start.1 = (f32[64,1536]{1,0:T(8,128)S(1)}, f32[64,1536]{1,0:T(8,128)S(1)}, u32[]{:S(2)}, u32[]{:S(2)}) collective-permute-start(f32[64,1536]{1,0:T(8,128)S(1)} %collective-permute-done.refs_1_), channel_id=1, source_target_pairs={{0,64},{64,128},{128,192},{192,256},{256,320},{320,384},{384,448},... | collective-permute-start | bytes 1179656 | tf_op jit(solution)/shard_map/ppermute | solution.py:177
  56.3 2.8 %collective-permute-done.4.refs_5_ = f32[64,1536]{1,0:T(8,128)S(1)} collective-permute-done((f32[64,1536]{1,0:T(8,128)S(1)}, f32[64,1536]{1,0:T(8,128)S(1)}, u32[]{:S(2)}, u32[]{:S(2)}) %collective-permute-start.4) | collective-permute-done | bytes 393248 | tf_op jit(solution)/shard_map/ppermute | solution.py:177
  59.1 5.0 %collective-permute-start.5 = (f32[64,1536]{1,0:T(8,128)S(1)}, f32[64,1536]{1,0:T(8,128)S(1)}, u32[]{:S(2)}, u32[]{:S(2)}) collective-permute-start(f32[64,1536]{1,0:T(8,128)S(1)} %collective-permute-done.4.refs_5_), channel_id=1, source_target_pairs={{0,448},{64,0},{128,64},{192,128},{256,192},{320,256},{384,320},{4... | collective-permute-start | bytes 1179656 | tf_op jit(solution)/shard_map/ppermute | solution.py:177
  64.1 0.0 collective-permute-done.1.refs_2_
  64.1 1.9 %collective-permute-start.2 = (f32[64,1536]{1,0:T(8,128)S(1)}, f32[64,1536]{1,0:T(8,128)S(1)}, u32[]{:S(2)}, u32[]{:S(2)}) collective-permute-start(f32[64,1536]{1,0:T(8,128)S(1)} %collective-permute-done.1.refs_2_), channel_id=1, source_target_pairs={{0,64},{64,128},{128,192},{192,256},{256,320},{320,384},{384,448},... | collective-permute-start | bytes 1179656 | tf_op jit(solution)/shard_map/ppermute | solution.py:177
  66.1 3.6 %collective-permute-done.5.refs_4_ = f32[64,1536]{1,0:T(8,128)S(1)} collective-permute-done((f32[64,1536]{1,0:T(8,128)S(1)}, f32[64,1536]{1,0:T(8,128)S(1)}, u32[]{:S(2)}, u32[]{:S(2)}) %collective-permute-start.5) | collective-permute-done | bytes 393248 | tf_op jit(solution)/shard_map/ppermute | solution.py:177
  69.7 5.0 %collective-permute-start.7 = (f32[32,1536]{1,0:T(8,128)S(1)}, f32[32,1536]{1,0:T(8,128)S(1)}, u32[]{:S(2)}, u32[]{:S(2)}) collective-permute-start(f32[32,1536]{1,0:T(8,128)S(1)} %slice.9), channel_id=1, source_target_pairs={{0,448},{64,0},{128,64},{192,128},{256,192},{320,256},{384,320},{4... | collective-permute-start | bytes 589832 | tf_op jit(solution)/shard_map/ppermute | solution.py:177
  74.7 0.3 collective-permute-done.2.refs_3_
  75.0 1.9 %collective-permute-start.6 = (f32[32,1536]{1,0:T(8,128)S(1)}, f32[32,1536]{1,0:T(8,128)S(1)}, u32[]{:S(2)}, u32[]{:S(2)}) collective-permute-start(f32[32,1536]{1,0:T(8,128)S(1)} %slice.8), channel_id=1, source_target_pairs={{0,64},{64,128},{128,192},{192,256},{256,320},{320,384},{384,448},... | collective-permute-start | bytes 589832 | tf_op jit(solution)/shard_map/ppermute | solution.py:177
  76.9 0.1 pad_add_fusion.pos_ref
  77.0 0.0 all-gather.2.cloned.1.call-done
  77.0 0.0 copy-start
  77.0 1.4 copy-done
  78.4 1.3 norm.1
  79.7 0.0 collective-permute-done.7.refs_8_
  79.7 5.3 %collective-permute-done.6.refs_7_ = f32[32,1536]{1,0:T(8,128)S(1)} collective-permute-done((f32[32,1536]{1,0:T(8,128)S(1)}, f32[32,1536]{1,0:T(8,128)S(1)}, u32[]{:S(2)}, u32[]{:S(2)}) %collective-permute-start.6) | collective-permute-done | bytes 196640 | tf_op jit(solution)/shard_map/ppermute | solution.py:177
  85.1 2.5 %scores.1 = (f32[256,512]{1,0:T(8,128)S(1)}, f32[16,8,128]{2,1,0:T(8,128)S(1)}, f32[32,8,128]{2,1,0:T(8,128)S(1)}, f32[512,1536]{1,0:T(8,128)S(1)}) custom-call(s32[3]{0:T(128)S(1)} %pad_add_fusion.pos_ref, bf16[256,1536]{1,0:T(8,128)(2,1)S(1)} %get-tuple-element.20.hi_ref, bf16[256,1536]{1,0:T(8,128)(2,1)S(1)} %get-tuple-element.21.lo_ref, ...), custom_call_target="tpu_custom_call" | custom-call | tf_op jit(solution)/shard_map/scores/pallas_call | solution.py:190
  87.5 17.5 %all_to_all.21.rows_ref = f32[16,8,128]{2,1,0:T(8,128)S(1)} all-to-all(f32[16,8,128]{2,1,0:T(8,128)S(1)} %get-tuple-element.29), channel_id=1, replica_groups=mesh['z'=8,'yh'=4,'core'=2,'yl'=2,'x'=4] {'core','yl','x'}, dimensions={0} | all-to-all | bytes 131072 | tf_op jit(solution)/shard_map/all_to_all | solution.py:186
  105.0 14.2 %all_to_all.22.cols_l_ref = f32[32,8,128]{2,1,0:T(8,128)S(1)} all-to-all(f32[32,8,128]{2,1,0:T(8,128)S(1)} %get-tuple-element.30), channel_id=1, replica_groups=mesh['z'=8,'yh'=4,'core'=2,'yl'=2,'x'=4] {'z','yh'}, dimensions={0} | all-to-all | bytes 262144 | tf_op jit(solution)/shard_map/all_to_all | solution.py:186
  119.2 2.5 %gradient.1 = (f32[8,200,128]{2,1,0:T(8,128)S(1)}, f32[8,200,128]{2,1,0:T(8,128)S(1)}) custom-call(s32[3]{0:T(128)S(1)} %pad_add_fusion.pos_ref, f32[256,512]{1,0:T(8,128)S(1)} %get-tuple-element.25.s_ref, f32[128,1536]{1,0:T(8,128)S(1)} %get-tuple-element.26.own_ref, f32[128,1536]{1,0:T(8,128)S(1)} %get-tuple-element.27.oth_ref, ...), custom_call_target="tpu_custom_call" | custom-call | tf_op jit(solution)/shard_map/gradient/pallas_call | solution.py:190
  121.8 3.6 %collective-permute-start.8 = (f32[8,200,128]{2,1,0:T(8,128)S(1)}, f32[8,200,128]{2,1,0:T(8,128)S(1)}, u32[]{:S(2)}, u32[]{:S(2)}) collective-permute-start(f32[8,200,128]{2,1,0:T(8,128)S(1)} %get-tuple-element.32), channel_id=1, source_target_pairs={{0,8},{8,0},{1,9},{9,1},{2,10},{10,2},{3,11},{11,3},{4,12},{12,4},... | collective-permute-start | bytes 2457608 | tf_op jit(solution)/shard_map/ppermute | solution.py:172
  125.4 1.9 %collective-permute-done.8 = f32[8,200,128]{2,1,0:T(8,128)S(1)} collective-permute-done((f32[8,200,128]{2,1,0:T(8,128)S(1)}, f32[8,200,128]{2,1,0:T(8,128)S(1)}, u32[]{:S(2)}, u32[]{:S(2)}) %collective-permute-start.8) | collective-permute-done | bytes 819232 | tf_op jit(solution)/shard_map/ppermute | solution.py:172
  127.3 0.1 add.11
  127.4 15.3 %all_to_all.23.piece_ref = f32[8,200,128]{2,1,0:T(8,128)S(1)} all-to-all(f32[8,200,128]{2,1,0:T(8,128)S(1)} %add.11), channel_id=1, replica_groups=mesh['z'=8,'yh'=4,'core'=2,'yl'=2,'x'=4] {'yl','x'}, dimensions={0} | all-to-all | bytes 1638400 | tf_op jit(solution)/shard_map/all_to_all | solution.py:186
  142.8 0.7 finish.1
  (2 shorter events, 0.0 us)
Async XLA Ops:
  7.2 69.8 %all-gather.2.cloned.1.call-start = ((), (), s32[]{:S(2)}) async-start(), calls=%async_computation.4 | async-start | bytes 1740800 | tf_op jit(solution)/shard_map/all_gather | solution.py:211
  7.2 0.9 copy-start.1
  8.1 0.7 copy-start.2
  33.9 15.4 %collective-permute-start.3 = (f32[64,1536]{1,0:T(8,128)S(1)}, f32[64,1536]{1,0:T(8,128)S(1)}, u32[]{:S(2)}, u32[]{:S(2)}) collective-permute-start(f32[64,1536]{1,0:T(8,128)S(1)} %columns.1.refs_0_), channel_id=1, source_target_pairs={{0,448},{64,0},{128,64},{192,128},{256,192},{320,256},{384,320},{4... | collective-permute-start | bytes 1179656 | tf_op jit(solution)/shard_map/ppermute | solution.py:177
  44.7 9.7 %collective-permute-start = (f32[64,1536]{1,0:T(8,128)S(1)}, f32[64,1536]{1,0:T(8,128)S(1)}, u32[]{:S(2)}, u32[]{:S(2)}) collective-permute-start(f32[64,1536]{1,0:T(8,128)S(1)} %columns.1.refs_0_), channel_id=1, source_target_pairs={{0,64},{64,128},{128,192},{192,256},{256,320},{320,384},{384,448},... | collective-permute-start | bytes 1179656 | tf_op jit(solution)/shard_map/ppermute | solution.py:177
  49.4 9.7 %collective-permute-start.4 = (f32[64,1536]{1,0:T(8,128)S(1)}, f32[64,1536]{1,0:T(8,128)S(1)}, u32[]{:S(2)}, u32[]{:S(2)}) collective-permute-start(f32[64,1536]{1,0:T(8,128)S(1)} %collective-permute-done.3.refs_6_), channel_id=1, source_target_pairs={{0,448},{64,0},{128,64},{192,128},{256,192},{320,256},{384,320},{4... | collective-permute-start | bytes 1179656 | tf_op jit(solution)/shard_map/ppermute | solution.py:177
  54.4 9.7 %collective-permute-start.1 = (f32[64,1536]{1,0:T(8,128)S(1)}, f32[64,1536]{1,0:T(8,128)S(1)}, u32[]{:S(2)}, u32[]{:S(2)}) collective-permute-start(f32[64,1536]{1,0:T(8,128)S(1)} %collective-permute-done.refs_1_), channel_id=1, source_target_pairs={{0,64},{64,128},{128,192},{192,256},{256,320},{320,384},{384,448},... | collective-permute-start | bytes 1179656 | tf_op jit(solution)/shard_map/ppermute | solution.py:177
  59.1 10.6 %collective-permute-start.5 = (f32[64,1536]{1,0:T(8,128)S(1)}, f32[64,1536]{1,0:T(8,128)S(1)}, u32[]{:S(2)}, u32[]{:S(2)}) collective-permute-start(f32[64,1536]{1,0:T(8,128)S(1)} %collective-permute-done.4.refs_5_), channel_id=1, source_target_pairs={{0,448},{64,0},{128,64},{192,128},{256,192},{320,256},{384,320},{4... | collective-permute-start | bytes 1179656 | tf_op jit(solution)/shard_map/ppermute | solution.py:177
  64.1 10.8 %collective-permute-start.2 = (f32[64,1536]{1,0:T(8,128)S(1)}, f32[64,1536]{1,0:T(8,128)S(1)}, u32[]{:S(2)}, u32[]{:S(2)}) collective-permute-start(f32[64,1536]{1,0:T(8,128)S(1)} %collective-permute-done.1.refs_2_), channel_id=1, source_target_pairs={{0,64},{64,128},{128,192},{192,256},{256,320},{320,384},{384,448},... | collective-permute-start | bytes 1179656 | tf_op jit(solution)/shard_map/ppermute | solution.py:177
  69.7 10.0 %collective-permute-start.7 = (f32[32,1536]{1,0:T(8,128)S(1)}, f32[32,1536]{1,0:T(8,128)S(1)}, u32[]{:S(2)}, u32[]{:S(2)}) collective-permute-start(f32[32,1536]{1,0:T(8,128)S(1)} %slice.9), channel_id=1, source_target_pairs={{0,448},{64,0},{128,64},{192,128},{256,192},{320,256},{384,320},{4... | collective-permute-start | bytes 589832 | tf_op jit(solution)/shard_map/ppermute | solution.py:177
  75.0 10.1 %collective-permute-start.6 = (f32[32,1536]{1,0:T(8,128)S(1)}, f32[32,1536]{1,0:T(8,128)S(1)}, u32[]{:S(2)}, u32[]{:S(2)}) collective-permute-start(f32[32,1536]{1,0:T(8,128)S(1)} %slice.8), channel_id=1, source_target_pairs={{0,64},{64,128},{128,192},{192,256},{256,320},{320,384},{384,448},... | collective-permute-start | bytes 589832 | tf_op jit(solution)/shard_map/ppermute | solution.py:177
  77.0 1.4 copy-start
  121.8 5.5 %collective-permute-start.8 = (f32[8,200,128]{2,1,0:T(8,128)S(1)}, f32[8,200,128]{2,1,0:T(8,128)S(1)}, u32[]{:S(2)}, u32[]{:S(2)}) collective-permute-start(f32[8,200,128]{2,1,0:T(8,128)S(1)} %get-tuple-element.32), channel_id=1, source_target_pairs={{0,8},{8,0},{1,9},{9,1},{2,10},{10,2},{3,11},{11,3},{4,12},{12,4},... | collective-permute-start | bytes 2457608 | tf_op jit(solution)/shard_map/ppermute | solution.py:172
Sparse Core Ops, SparseCore 0:
  10.1 44.5 all-gather.1

commit v10 on v9

--- a/solution.py
+++ b/solution.py
@@ -53,9 +53,8 @@
     return jnp.concatenate([x[:CHUNK, :], jnp.concatenate([tail[:, :rest], tail[:, rest:]], axis=0)], axis=1)
 
 
-def chunk_kernel(view_ref, partner_ref, out_ref, shard_ref):
-    shard_ref[:FEAT, :] = view_ref[...]
-    shard_ref[FEAT:, :] = jnp.broadcast_to(partner_ref[...].astype(jnp.float32), (PIECE - FEAT, ROWS))
+def chunk_kernel(view_ref, out_ref, copy_ref):
+    copy_ref[...] = view_ref[...]
     x = view_ref[...].T
     for f in range(NF):
         piece = pack(x[f * CHUNK:(f + 1) * CHUNK, :])
@@ -63,7 +62,9 @@
             out_ref[y * NF + f] = piece
 
 
-def column_kernel(piece_ref, unit_ref):
+def column_kernel(piece_ref, view_ref, partner_ref, unit_ref, shard_ref):
+    shard_ref[:FEAT, :] = view_ref[...]
+    shard_ref[FEAT:, :] = jnp.broadcast_to(partner_ref[...].astype(jnp.float32), (PIECE - FEAT, ROWS))
     for y in range(NYH):
         x = jnp.concatenate([unpack(piece_ref[y * NF + f]) for f in range(NF)], axis=1)
         scale = lax.rsqrt(jnp.sum(x * x, axis=1, keepdims=True) + 1e-06)
@@ -98,8 +99,8 @@
     z = pos_ref[0] // NYH
     for k, block in enumerate(blocks):
         whole = k < NZ - 1
-        back = (k if k < NZ // 2 else k + 1) if whole else NZ // 2
-        at = ((z + NZ - back) % NZ) * BLOCK + (0 if whole else (k - NZ + 1) * HALF)
+        ahead = (k if k < NZ // 2 else NZ // 2 - 1 - k) if whole else NZ // 2
+        at = ((z + NZ + ahead * (1 - 2 * (z % 2))) % NZ) * BLOCK + (0 if whole else (k - NZ + 1) * HALF)
         rows = BLOCK if whole else HALF
         cols_ref[pl.ds(pl.multiple_of(at, HALF), rows), :] = block[...]
     rows = (hi_ref[...], lo_ref[...])
@@ -173,13 +174,15 @@
 
 
 def around(x):
-    def shift(block, by):
-        return lax.ppermute(block, "z", [(i, (i + by) % NZ) for i in range(NZ)])
-    up, down = [x], [x]
+    pair = [(i, i ^ 1) for i in range(NZ)]
+    between = [(i, ((i - 1) ^ 1) + 1 & NZ - 1) for i in range(NZ)]
+    a, b = [x], [x]
     for _ in range(NZ // 2 - 1):
-        up.append(shift(up[-1], 1))
-        down.append(shift(down[-1], -1))
-    return up + down[:0:-1] + [shift(up[-1][:HALF], 1), shift(down[-1][HALF:], -1)]
+        got = lax.ppermute(b[-1], "z", pair), lax.ppermute(a[-1], "z", between)
+        a.append(got[0])
+        b.append(got[1])
+    last = lax.ppermute(b[-1][:HALF], "z", pair), lax.ppermute(a[-1][HALF:], "z", between)
+    return a + b[1:] + list(last)
 
 
 def trade(x, axes):
@@ -206,11 +209,10 @@
     feat = ("yl", "x")
 
     packed = CHUNK * FEAT // ROWS
-    chunks, shard = call(chunk_kernel, "chunks", [f32(NYH * NF, packed, ROWS), f32(PIECE, ROWS)],
-                         [views.T, partner.reshape(1, ROWS)])
+    chunks, copy = call(chunk_kernel, "chunks", [f32(NYH * NF, packed, ROWS), f32(FEAT, ROWS)], [views.T])
+    chunk, shard = call(column_kernel, "columns", [f32(BLOCK, WIDE), f32(PIECE, ROWS)],
+                        [trade(chunks, ("yh", "yl", "x")), copy, partner.reshape(1, ROWS)])
     whole = lax.all_gather(shard, ("core", "yl", "x"), axis=0, tiled=True)
-    chunks = trade(chunks, ("yh", "yl", "x"))
-    chunk, = call(column_kernel, "columns", [f32(BLOCK, WIDE)], [chunks])
     ring = around(chunk)
     ids, bf16 = jax.ShapeDtypeStruct((ROWS, 1), jnp.int32), jax.ShapeDtypeStruct((NC * ROWS, WIDE), jnp.bfloat16)
     own, oth, scale, own_p, oth_p, hi, lo = call(

time: 151 us -> 150 us (level)
  waiting for transfers between devices: 16.7 us -> 23.2 us
  starting transfers between devices: 37.1 us -> 31 us
    ppermute x8, waiting for transfers between devices: 14.8 us -> 21.3 us  [the longest x6 19.5 us: around(): got = (lax.ppermute(b[-1], 'z', pair), lax.ppermute(a[-1], 'z', between))]
    ppermute x8, starting transfers between devices: 33.5 us -> 27.1 us  [the longest x6 22.1 us: around(): got = (lax.ppermute(b[-1], 'z', pair), lax.ppermute(a[-1], 'z', between))]
where the time goes in v10:
time: 150 us
  blocking collectives  70.2 us (47%)
  starting transfers between devices  31 us (21%)
  waiting for transfers between devices  23.2 us (15%)
  between operations  14.2 us (9%)
  Pallas kernels  8 us (5%)
  local copies, waits for them, and re-layouts  3 us (2%)
    all_to_all x4, blocking collectives, trade(): return lax.all_to_all(x, axes, 0, 0, tiled=True)  70.2 us
    ppermute x6, starting transfers between devices, around(): got = (lax.ppermute(b[-1], 'z', pair), lax.ppermute(a[-1], 'z', between))  22.1 us
    ppermute x6, waiting for transfers between devices, around(): got = (lax.ppermute(b[-1], 'z', pair), lax.ppermute(a[-1], 'z', between))  19.5 us
    pallas_call x6, Pallas kernels, call(): pl.pallas_call(body, out_shape=outs, in_specs=[SMEM if a.shape == (3,) el...  8 us
    ppermute x1, starting transfers between devices, swap(): return lax.ppermute(x, axes, [(i, i ^ k) for i in range(size)])  3.92 us
    ppermute x1, starting transfers between devices, around(): lax.ppermute(a[-1][HALF:], 'z', between)  3.02 us
  transfers between devices with their start and end apart: 10, of which 6 were waited for; matrix products, arithmetic and copies ran while one was open for 0% of the time, Pallas kernels for 1%

profile of v10, /device:TPU:1, one launch (start us, length us, event | category | flops | bytes accessed | tf_op | source)
XLA Modules:
  0.0 149.8 jit_solution(10959828054115938534)
XLA Ops:
  7.2 0.0 all-gather.2.cloned.1.call-start
  7.2 0.0 copy-start.1
  7.2 0.9 copy-done.1
  8.1 0.2 chunks.1
  8.3 24.1 %all_to_all.20.piece_ref = f32[32,24,128]{2,1,0:T(8,128)S(1)} all-to-all(f32[32,24,128]{2,1,0:T(8,128)S(1)} %get-tuple-element.21), channel_id=1, replica_groups=mesh['z'=8,'yh'=4,'core'=2,'yl'=2,'x'=4] {'yh','yl','x'}, dimensions={0} | all-to-all | bytes 786432 | tf_op jit(solution)/shard_map/all_to_all | solution.py:189
  32.4 0.0 copy-start.2
  32.4 0.7 copy-done.2
  33.0 0.9 columns.1
  33.9 0.0 all-gather.2.cloned.1.call-update
  33.9 10.7 %collective-permute-start.1 = (f32[64,1536]{1,0:T(8,128)S(1)}, f32[64,1536]{1,0:T(8,128)S(1)}, u32[]{:S(2)}, u32[]{:S(2)}) collective-permute-start(f32[64,1536]{1,0:T(8,128)S(1)} %get-tuple-element.28.refs_0_), channel_id=1, source_target_pairs={{0,448},{64,128},{128,64},{192,256},{256,192},{320,384},{384,320},... | collective-permute-start | bytes 1179656 | tf_op jit(solution)/shard_map/ppermute | solution.py:181
  44.6 1.9 %collective-permute-start = (f32[64,1536]{1,0:T(8,128)S(1)}, f32[64,1536]{1,0:T(8,128)S(1)}, u32[]{:S(2)}, u32[]{:S(2)}) collective-permute-start(f32[64,1536]{1,0:T(8,128)S(1)} %get-tuple-element.28.refs_0_), channel_id=1, source_target_pairs={{0,64},{64,0},{128,192},{192,128},{256,320},{320,256},{384,448},{4... | collective-permute-start | bytes 1179656 | tf_op jit(solution)/shard_map/ppermute | solution.py:181
  46.5 5.0 %collective-permute-done.1.refs_4_ = f32[64,1536]{1,0:T(8,128)S(1)} collective-permute-done((f32[64,1536]{1,0:T(8,128)S(1)}, f32[64,1536]{1,0:T(8,128)S(1)}, u32[]{:S(2)}, u32[]{:S(2)}) %collective-permute-start.1) | collective-permute-done | bytes 393248 | tf_op jit(solution)/shard_map/ppermute | solution.py:181
  51.5 1.9 %collective-permute-start.2 = (f32[64,1536]{1,0:T(8,128)S(1)}, f32[64,1536]{1,0:T(8,128)S(1)}, u32[]{:S(2)}, u32[]{:S(2)}) collective-permute-start(f32[64,1536]{1,0:T(8,128)S(1)} %collective-permute-done.1.refs_4_), channel_id=1, source_target_pairs={{0,64},{64,0},{128,192},{192,128},{256,320},{320,256},{384,448},{4... | collective-permute-start | bytes 1179656 | tf_op jit(solution)/shard_map/ppermute | solution.py:181
  53.5 0.9 collective-permute-done.refs_1_
  54.3 3.4 %collective-permute-start.3 = (f32[64,1536]{1,0:T(8,128)S(1)}, f32[64,1536]{1,0:T(8,128)S(1)}, u32[]{:S(2)}, u32[]{:S(2)}) collective-permute-start(f32[64,1536]{1,0:T(8,128)S(1)} %collective-permute-done.refs_1_), channel_id=1, source_target_pairs={{0,448},{64,128},{128,64},{192,256},{256,192},{320,384},{384,320},... | collective-permute-start | bytes 1179656 | tf_op jit(solution)/shard_map/ppermute | solution.py:181
  57.7 6.2 %collective-permute-done.2.refs_2_ = f32[64,1536]{1,0:T(8,128)S(1)} collective-permute-done((f32[64,1536]{1,0:T(8,128)S(1)}, f32[64,1536]{1,0:T(8,128)S(1)}, u32[]{:S(2)}, u32[]{:S(2)}) %collective-permute-start.2) | collective-permute-done | bytes 393248 | tf_op jit(solution)/shard_map/ppermute | solution.py:181
  63.9 1.9 %collective-permute-start.5 = (f32[64,1536]{1,0:T(8,128)S(1)}, f32[64,1536]{1,0:T(8,128)S(1)}, u32[]{:S(2)}, u32[]{:S(2)}) collective-permute-start(f32[64,1536]{1,0:T(8,128)S(1)} %collective-permute-done.2.refs_2_), channel_id=1, source_target_pairs={{0,448},{64,128},{128,64},{192,256},{256,192},{320,384},{384,320},... | collective-permute-start | bytes 1179656 | tf_op jit(solution)/shard_map/ppermute | solution.py:181
  65.8 0.0 collective-permute-done.3.refs_5_
  65.9 2.3 %collective-permute-start.4 = (f32[64,1536]{1,0:T(8,128)S(1)}, f32[64,1536]{1,0:T(8,128)S(1)}, u32[]{:S(2)}, u32[]{:S(2)}) collective-permute-start(f32[64,1536]{1,0:T(8,128)S(1)} %collective-permute-done.3.refs_5_), channel_id=1, source_target_pairs={{0,64},{64,0},{128,192},{192,128},{256,320},{320,256},{384,448},{4... | collective-permute-start | bytes 1179656 | tf_op jit(solution)/shard_map/ppermute | solution.py:181
  68.2 7.4 %collective-permute-done.5.refs_6_ = f32[64,1536]{1,0:T(8,128)S(1)} collective-permute-done((f32[64,1536]{1,0:T(8,128)S(1)}, f32[64,1536]{1,0:T(8,128)S(1)}, u32[]{:S(2)}, u32[]{:S(2)}) %collective-permute-start.5) | collective-permute-done | bytes 393248 | tf_op jit(solution)/shard_map/ppermute | solution.py:181
  75.6 1.9 %collective-permute-start.6 = (f32[32,1536]{1,0:T(8,128)S(1)}, f32[32,1536]{1,0:T(8,128)S(1)}, u32[]{:S(2)}, u32[]{:S(2)}) collective-permute-start(f32[32,1536]{1,0:T(8,128)S(1)} %slice.8), channel_id=1, source_target_pairs={{0,64},{64,0},{128,192},{192,128},{256,320},{320,256},{384,448},{4... | collective-permute-start | bytes 589832 | tf_op jit(solution)/shard_map/ppermute | solution.py:184
  77.5 0.0 collective-permute-done.4.refs_3_
  77.6 3.0 %collective-permute-start.7 = (f32[32,1536]{1,0:T(8,128)S(1)}, f32[32,1536]{1,0:T(8,128)S(1)}, u32[]{:S(2)}, u32[]{:S(2)}) collective-permute-start(f32[32,1536]{1,0:T(8,128)S(1)} %slice.9), channel_id=1, source_target_pairs={{0,448},{64,128},{128,64},{192,256},{256,192},{320,384},{384,320},... | collective-permute-start | bytes 589832 | tf_op jit(solution)/shard_map/ppermute | solution.py:184
  80.6 0.1 pad_add_fusion.pos_ref
  80.7 0.0 all-gather.2.cloned.1.call-done
  80.7 0.0 copy-start
  80.7 1.4 copy-done
  82.1 1.3 norm.1
  83.4 0.0 collective-permute-done.6.refs_7_
  83.4 1.8 %collective-permute-done.7.refs_8_ = f32[32,1536]{1,0:T(8,128)S(1)} collective-permute-done((f32[32,1536]{1,0:T(8,128)S(1)}, f32[32,1536]{1,0:T(8,128)S(1)}, u32[]{:S(2)}, u32[]{:S(2)}) %collective-permute-start.7) | collective-permute-done | bytes 196640 | tf_op jit(solution)/shard_map/ppermute | solution.py:184
  85.2 2.5 %scores.1 = (f32[256,512]{1,0:T(8,128)S(1)}, f32[16,8,128]{2,1,0:T(8,128)S(1)}, f32[32,8,128]{2,1,0:T(8,128)S(1)}, f32[512,1536]{1,0:T(8,128)S(1)}) custom-call(s32[3]{0:T(128)S(1)} %pad_add_fusion.pos_ref, bf16[256,1536]{1,0:T(8,128)(2,1)S(1)} %get-tuple-element.24.hi_ref, bf16[256,1536]{1,0:T(8,128)(2,1)S(1)} %get-tuple-element.25.lo_ref, ...), custom_call_target="tpu_custom_call" | custom-call | tf_op jit(solution)/shard_map/scores/pallas_call | solution.py:193
  87.7 13.3 %all_to_all.21.rows_ref = f32[16,8,128]{2,1,0:T(8,128)S(1)} all-to-all(f32[16,8,128]{2,1,0:T(8,128)S(1)} %get-tuple-element.33), channel_id=1, replica_groups=mesh['z'=8,'yh'=4,'core'=2,'yl'=2,'x'=4] {'core','yl','x'}, dimensions={0} | all-to-all | bytes 131072 | tf_op jit(solution)/shard_map/all_to_all | solution.py:189
  101.0 17.2 %all_to_all.22.cols_l_ref = f32[32,8,128]{2,1,0:T(8,128)S(1)} all-to-all(f32[32,8,128]{2,1,0:T(8,128)S(1)} %get-tuple-element.34), channel_id=1, replica_groups=mesh['z'=8,'yh'=4,'core'=2,'yl'=2,'x'=4] {'z','yh'}, dimensions={0} | all-to-all | bytes 262144 | tf_op jit(solution)/shard_map/all_to_all | solution.py:189
  118.2 2.5 %gradient.1 = (f32[8,200,128]{2,1,0:T(8,128)S(1)}, f32[8,200,128]{2,1,0:T(8,128)S(1)}) custom-call(s32[3]{0:T(128)S(1)} %pad_add_fusion.pos_ref, f32[256,512]{1,0:T(8,128)S(1)} %get-tuple-element.29.s_ref, f32[128,1536]{1,0:T(8,128)S(1)} %get-tuple-element.30.own_ref, f32[128,1536]{1,0:T(8,128)S(1)} %get-tuple-element.31.oth_ref, ...), custom_call_target="tpu_custom_call" | custom-call | tf_op jit(solution)/shard_map/gradient/pallas_call | solution.py:193
  120.8 3.9 %collective-permute-start.8 = (f32[8,200,128]{2,1,0:T(8,128)S(1)}, f32[8,200,128]{2,1,0:T(8,128)S(1)}, u32[]{:S(2)}, u32[]{:S(2)}) collective-permute-start(f32[8,200,128]{2,1,0:T(8,128)S(1)} %get-tuple-element.36), channel_id=1, source_target_pairs={{0,8},{8,0},{1,9},{9,1},{2,10},{10,2},{3,11},{11,3},{4,12},{12,4},... | collective-permute-start | bytes 2457608 | tf_op jit(solution)/shard_map/ppermute | solution.py:173
  124.7 1.9 %collective-permute-done.8 = f32[8,200,128]{2,1,0:T(8,128)S(1)} collective-permute-done((f32[8,200,128]{2,1,0:T(8,128)S(1)}, f32[8,200,128]{2,1,0:T(8,128)S(1)}, u32[]{:S(2)}, u32[]{:S(2)}) %collective-permute-start.8) | collective-permute-done | bytes 819232 | tf_op jit(solution)/shard_map/ppermute | solution.py:173
  126.6 0.1 add.11
  126.7 15.5 %all_to_all.23.piece_ref = f32[8,200,128]{2,1,0:T(8,128)S(1)} all-to-all(f32[8,200,128]{2,1,0:T(8,128)S(1)} %add.11), channel_id=1, replica_groups=mesh['z'=8,'yh'=4,'core'=2,'yl'=2,'x'=4] {'yl','x'}, dimensions={0} | all-to-all | bytes 1638400 | tf_op jit(solution)/shard_map/all_to_all | solution.py:189
  142.2 0.7 finish.1
  (2 shorter events, 0.0 us)
Async XLA Ops:
  7.2 73.5 %all-gather.2.cloned.1.call-start = ((), (), s32[]{:S(2)}) async-start(), calls=%async_computation.4 | async-start | bytes 1740800 | tf_op jit(solution)/shard_map/all_gather | solution.py:215
  7.2 0.9 copy-start.1
  32.4 0.7 copy-start.2
  33.9 17.6 %collective-permute-start.1 = (f32[64,1536]{1,0:T(8,128)S(1)}, f32[64,1536]{1,0:T(8,128)S(1)}, u32[]{:S(2)}, u32[]{:S(2)}) collective-permute-start(f32[64,1536]{1,0:T(8,128)S(1)} %get-tuple-element.28.refs_0_), channel_id=1, source_target_pairs={{0,448},{64,128},{128,64},{192,256},{256,192},{320,384},{384,320},... | collective-permute-start | bytes 1179656 | tf_op jit(solution)/shard_map/ppermute | solution.py:181
  44.6 9.7 %collective-permute-start = (f32[64,1536]{1,0:T(8,128)S(1)}, f32[64,1536]{1,0:T(8,128)S(1)}, u32[]{:S(2)}, u32[]{:S(2)}) collective-permute-start(f32[64,1536]{1,0:T(8,128)S(1)} %get-tuple-element.28.refs_0_), channel_id=1, source_target_pairs={{0,64},{64,0},{128,192},{192,128},{256,320},{320,256},{384,448},{4... | collective-permute-start | bytes 1179656 | tf_op jit(solution)/shard_map/ppermute | solution.py:181
  51.5 12.4 %collective-permute-start.2 = (f32[64,1536]{1,0:T(8,128)S(1)}, f32[64,1536]{1,0:T(8,128)S(1)}, u32[]{:S(2)}, u32[]{:S(2)}) collective-permute-start(f32[64,1536]{1,0:T(8,128)S(1)} %collective-permute-done.1.refs_4_), channel_id=1, source_target_pairs={{0,64},{64,0},{128,192},{192,128},{256,320},{320,256},{384,448},{4... | collective-permute-start | bytes 1179656 | tf_op jit(solution)/shard_map/ppermute | solution.py:181
  54.3 11.5 %collective-permute-start.3 = (f32[64,1536]{1,0:T(8,128)S(1)}, f32[64,1536]{1,0:T(8,128)S(1)}, u32[]{:S(2)}, u32[]{:S(2)}) collective-permute-start(f32[64,1536]{1,0:T(8,128)S(1)} %collective-permute-done.refs_1_), channel_id=1, source_target_pairs={{0,448},{64,128},{128,64},{192,256},{256,192},{320,384},{384,320},... | collective-permute-start | bytes 1179656 | tf_op jit(solution)/shard_map/ppermute | solution.py:181
  63.9 11.6 %collective-permute-start.5 = (f32[64,1536]{1,0:T(8,128)S(1)}, f32[64,1536]{1,0:T(8,128)S(1)}, u32[]{:S(2)}, u32[]{:S(2)}) collective-permute-start(f32[64,1536]{1,0:T(8,128)S(1)} %collective-permute-done.2.refs_2_), channel_id=1, source_target_pairs={{0,448},{64,128},{128,64},{192,256},{256,192},{320,384},{384,320},... | collective-permute-start | bytes 1179656 | tf_op jit(solution)/shard_map/ppermute | solution.py:181
  65.9 11.7 %collective-permute-start.4 = (f32[64,1536]{1,0:T(8,128)S(1)}, f32[64,1536]{1,0:T(8,128)S(1)}, u32[]{:S(2)}, u32[]{:S(2)}) collective-permute-start(f32[64,1536]{1,0:T(8,128)S(1)} %collective-permute-done.3.refs_5_), channel_id=1, source_target_pairs={{0,64},{64,0},{128,192},{192,128},{256,320},{320,256},{384,448},{4... | collective-permute-start | bytes 1179656 | tf_op jit(solution)/shard_map/ppermute | solution.py:181
  75.6 7.8 %collective-permute-start.6 = (f32[32,1536]{1,0:T(8,128)S(1)}, f32[32,1536]{1,0:T(8,128)S(1)}, u32[]{:S(2)}, u32[]{:S(2)}) collective-permute-start(f32[32,1536]{1,0:T(8,128)S(1)} %slice.8), channel_id=1, source_target_pairs={{0,64},{64,0},{128,192},{192,128},{256,320},{320,256},{384,448},{4... | collective-permute-start | bytes 589832 | tf_op jit(solution)/shard_map/ppermute | solution.py:184
  77.6 7.6 %collective-permute-start.7 = (f32[32,1536]{1,0:T(8,128)S(1)}, f32[32,1536]{1,0:T(8,128)S(1)}, u32[]{:S(2)}, u32[]{:S(2)}) collective-permute-start(f32[32,1536]{1,0:T(8,128)S(1)} %slice.9), channel_id=1, source_target_pairs={{0,448},{64,128},{128,64},{192,256},{256,192},{320,384},{384,320},... | collective-permute-start | bytes 589832 | tf_op jit(solution)/shard_map/ppermute | solution.py:184
  80.7 1.4 copy-start
  120.8 5.9 %collective-permute-start.8 = (f32[8,200,128]{2,1,0:T(8,128)S(1)}, f32[8,200,128]{2,1,0:T(8,128)S(1)}, u32[]{:S(2)}, u32[]{:S(2)}) collective-permute-start(f32[8,200,128]{2,1,0:T(8,128)S(1)} %get-tuple-element.36), channel_id=1, source_target_pairs={{0,8},{8,0},{1,9},{9,1},{2,10},{10,2},{3,11},{11,3},{4,12},{12,4},... | collective-permute-start | bytes 2457608 | tf_op jit(solution)/shard_map/ppermute | solution.py:173
Sparse Core Ops, SparseCore 0:
  34.1 39.6 all-gather.1

commit v11 on v10

--- a/solution.py
+++ b/solution.py
@@ -71,15 +71,14 @@
         unit_ref[y * CHUNK:(y + 1) * CHUNK, :] = x * scale
 
 
-def norm_kernel(pos_ref, piece_ref, own_ref, oth_ref, scale_ref, ownp_ref, othp_ref, hi_ref, lo_ref):
+def norm_kernel(pos_ref, piece_ref, scale_ref, ownp_ref, othp_ref, hi_ref, lo_ref):
     core = pos_ref[1]
-    for j, (out, part) in enumerate(((own_ref, ownp_ref), (oth_ref, othp_ref))):
+    for j, part in enumerate((ownp_ref, othp_ref)):
         x = piece_ref[core ^ j, :, :FEAT, :].reshape(WIDE, ROWS)
         scale = lax.rsqrt(jnp.sum(x * x, axis=0, keepdims=True) + 1e-06)
         if j == 0:
             scale_ref[...] = scale
         units = (x * scale).T
-        out[...] = units
         part[...] = column(piece_ref[core ^ j, 0, FEAT:FEAT + 1, :]).astype(jnp.int32)
         at = slice(j * ROWS, (j + 1) * ROWS)
         hi_ref[at, :], lo_ref[at, :] = split(units)
@@ -93,20 +92,39 @@
     return col == row, col == part
 
 
-def score_kernel(pos_ref, hi_ref, lo_ref, ownp_ref, othp_ref, *refs):
+def place(z, ahead):
+    return (z + NZ + ahead * (1 - 2 * (z % 2))) % NZ * BLOCK
+
+
+def gather_blocks(z, blocks, cols_ref):
+    for k, block in enumerate(blocks):
+        ahead = k if k < NZ // 2 else NZ // 2 - 1 - k
+        cols_ref[pl.ds(pl.multiple_of(place(z, ahead), BLOCK), BLOCK), :] = block[...]
+
+
+def early_kernel(pos_ref, hi_ref, lo_ref, *refs):
+    blocks, (s_ref, cols) = refs[:-2], refs[-2:]
+    z = pos_ref[0] // NYH
+    gather_blocks(z, blocks, cols)
+    late = pl.multiple_of(place(z, NZ // 2), BLOCK)
+    cols[pl.ds(late, BLOCK), :] = jnp.zeros((BLOCK, WIDE), jnp.float32)
+    rows = (hi_ref[...], lo_ref[...])
+    step = 256
+    for c in range(0, NCOL, step):
+        s_ref[:, c:c + step] = INV_TAU * dot3(rows, split(cols[c:c + step, :]), ((1,), (1,)))
+
+
+def score_kernel(pos_ref, hi_ref, lo_ref, ownp_ref, othp_ref, early_ref, *refs):
     blocks, (s_ref, row_ref, col_ref, cols_ref) = refs[:-4], refs[-4:]
     core = pos_ref[1]
     z = pos_ref[0] // NYH
-    for k, block in enumerate(blocks):
-        whole = k < NZ - 1
-        ahead = (k if k < NZ // 2 else NZ // 2 - 1 - k) if whole else NZ // 2
-        at = ((z + NZ + ahead * (1 - 2 * (z % 2))) % NZ) * BLOCK + (0 if whole else (k - NZ + 1) * HALF)
-        rows = BLOCK if whole else HALF
-        cols_ref[pl.ds(pl.multiple_of(at, HALF), rows), :] = block[...]
-    rows = (hi_ref[...], lo_ref[...])
-    step = 256
-    for c in range(0, NCOL, step):
-        s_ref[:, c:c + step] = INV_TAU * dot3(rows, split(cols_ref[c:c + step, :]), ((1,), (1,)))
+    gather_blocks(z, blocks[:-2], cols_ref)
+    late = place(z, NZ // 2)
+    for k, half in enumerate(blocks[-2:]):
+        cols_ref[pl.ds(pl.multiple_of(late + k * HALF, HALF), HALF), :] = half[...]
+    s_ref[...] = early_ref[...]
+    at = pl.ds(pl.multiple_of(late // ROWS * ROWS, ROWS), ROWS)
+    s_ref[:, at] = INV_TAU * dot3((hi_ref[...], lo_ref[...]), split(cols_ref[at, :]), ((1,), (1,)))
     colsum = jnp.zeros((1, NCOL), jnp.float32)
     pos = jnp.zeros((1, ROWS), jnp.float32)
     sums = []
@@ -134,7 +152,7 @@
         col_ref[k] = col
 
 
-def grad_kernel(pos_ref, s_ref, own_ref, oth_ref, cols_ref, ownp_ref, othp_ref, rows_ref, cols_l_ref, mine_ref, theirs_ref, w_hi, w_lo):
+def grad_kernel(pos_ref, s_ref, cols_ref, ownp_ref, othp_ref, rows_ref, cols_l_ref, mine_ref, theirs_ref, w_hi, w_lo):
     core = pos_ref[1]
     row_l = jnp.sum(rows_ref[...], axis=0)
     col_l = jnp.sum(cols_l_ref[...], axis=0)
@@ -148,25 +166,28 @@
         diag, hit = tile_masks(pos_ref, half, part[...])
         inv = column(1.0 / jnp.where(half == 0, row_l[0:1, :], row_l[1:2, :]))
         w = jnp.where(diag, 0.0, jnp.exp(s) * (inv + col_inv)) - jnp.where(hit, 2.0, 0.0)
-        projs.append(jnp.sum(w * s, axis=1, keepdims=True))
+        ws = w * s
+        lanes = sum(ws[:, c * ROWS:(c + 1) * ROWS] for c in range(NCOL // ROWS))
+        projs.append(jnp.sum(lanes.T, axis=0, keepdims=True))
         w_hi[j], w_lo[j] = split(w)
     weights = (w_hi[...].reshape(NC * ROWS, NCOL), w_lo[...].reshape(NC * ROWS, NCOL))
     step = 4 * FEAT
-    tail = jnp.concatenate([loss, jnp.zeros((7, ROWS), jnp.float32)], axis=0)
+    tails = [jnp.concatenate([loss, proj, jnp.zeros((6, ROWS), jnp.float32)], axis=0) for proj in projs]
     for c in range(WIDE // step):
         at = slice(c * step, (c + 1) * step)
         g = INV_TAU * dot3(weights, split(cols_ref[:, at]), ((1,), (0,)))
-        for j, (units, out) in enumerate(((own_ref, mine_ref), (oth_ref, theirs_ref))):
-            t = (g[j * ROWS:(j + 1) * ROWS, :] - units[:, at] * projs[j]).T
+        for j, out in enumerate((mine_ref, theirs_ref)):
+            t = g[j * ROWS:(j + 1) * ROWS, :].T
             for p in range(4):
                 out[4 * c + p, :FEAT, :] = t[p * FEAT:(p + 1) * FEAT, :]
-                out[4 * c + p, FEAT:, :] = tail
-
-
-def last_kernel(piece_ref, scale_ref, loss_ref, grad_ref):
+                out[4 * c + p, FEAT:, :] = tails[j]
+
+
+def last_kernel(piece_ref, scale_ref, view_ref, loss_ref, grad_ref):
     total = jnp.sum(piece_ref[...], axis=0)
     loss_ref[...] = jnp.sum(total[FEAT:FEAT + 1, :], axis=1, keepdims=True) / TOTAL
-    grad_ref[...] = total[:FEAT, :] * scale_ref[...]
+    scale = scale_ref[...]
+    grad_ref[...] = (total[:FEAT, :] - view_ref[...] * scale * total[FEAT + 1:FEAT + 2, :]) * scale
 
 
 def swap(x, axes, size, k):
@@ -215,26 +236,28 @@
     whole = lax.all_gather(shard, ("core", "yl", "x"), axis=0, tiled=True)
     ring = around(chunk)
     ids, bf16 = jax.ShapeDtypeStruct((ROWS, 1), jnp.int32), jax.ShapeDtypeStruct((NC * ROWS, WIDE), jnp.bfloat16)
-    own, oth, scale, own_p, oth_p, hi, lo = call(
+    scale, own_p, oth_p, hi, lo = call(
         norm_kernel, "norm",
-        [f32(ROWS, WIDE)] * 2 + [f32(1, ROWS), ids, ids, bf16, bf16],
+        [f32(1, ROWS), ids, ids, bf16, bf16],
         [pos, whole.reshape(NC, NF, PIECE, ROWS)],
     )
+    early, = call(early_kernel, "early", [f32(NC * ROWS, NCOL)], [pos, hi, lo, *ring[:-2]],
+                  [pltpu.VMEM((NCOL, WIDE), jnp.float32)])
     s, row, col, cols = call(
         score_kernel, "scores",
         [f32(NC * ROWS, NCOL), f32(NC * NF, 8, ROWS), f32(NZ * NYH, 8, ROWS), f32(NCOL, WIDE)],
-        [pos, hi, lo, own_p, oth_p, *ring],
+        [pos, hi, lo, own_p, oth_p, early, *ring],
     )
     rows_l = trade(row, ("core", "yl", "x"))
     cols_l = trade(col, ("z", "yh"))
     mine, theirs = call(
         grad_kernel, "gradient",
         [f32(NF, PIECE, ROWS)] * 2,
-        [pos, s, own, oth, cols, own_p, oth_p, rows_l, cols_l],
+        [pos, s, cols, own_p, oth_p, rows_l, cols_l],
         [pltpu.VMEM((NC, ROWS, NCOL), jnp.bfloat16)] * 2,
     )
     pieces = trade(mine + swap(theirs, "core", NC, 1), feat)
-    loss, grad = call(last_kernel, "finish", [f32(1, 1), f32(FEAT, ROWS)], [pieces, scale])
+    loss, grad = call(last_kernel, "finish", [f32(1, 1), f32(FEAT, ROWS)], [pieces, scale, copy])
     return loss.reshape(()), grad.T
 
 

time: 150 us -> 151 us (level)
  waiting for transfers between devices: 23.2 us -> 21.4 us
  Pallas kernels: 8 us -> 9.53 us
    ppermute x1, waiting for transfers between devices: 1.8 us -> 0.01 us  [around(): lax.ppermute(a[-1][HALF:], 'z', between)]
    pallas_call x6 -> x7, Pallas kernels: 8 us -> 9.53 us  [call(): pl.pallas_call(body, out_shape=outs, in_specs=[SMEM if a.shape == (3,) el...]
  transfers between devices with their start and end apart: 10 -> 10, of which waited for: 6 -> 5; matrix products, arithmetic and copies ran while one was open for 0% -> 1% of each run, Pallas kernels for 1% -> 2%
where the time goes in v11:
time: 151 us; the launch traced here: 150 us
  blocking collectives  70.1 us (46%)
  starting transfers between devices  31 us (21%)
  waiting for transfers between devices  21.4 us (14%)
  between operations  14.2 us (9%)
  Pallas kernels  9.53 us (6%)
  local copies, waits for them, and re-layouts  3.68 us (2%)
    all_to_all x4, blocking collectives, trade(): return lax.all_to_all(x, axes, 0, 0, tiled=True)  70.1 us
    ppermute x6, starting transfers between devices, around(): got = (lax.ppermute(b[-1], 'z', pair), lax.ppermute(a[-1], 'z', between))  22.1 us
    ppermute x6, waiting for transfers between devices, around(): got = (lax.ppermute(b[-1], 'z', pair), lax.ppermute(a[-1], 'z', between))  19.5 us
    pallas_call x7, Pallas kernels, call(): pl.pallas_call(body, out_shape=outs, in_specs=[SMEM if a.shape == (3,) el...  9.53 us
    ppermute x1, starting transfers between devices, swap(): return lax.ppermute(x, axes, [(i, i ^ k) for i in range(size)])  3.93 us
  transfers between devices with their start and end apart: 10, of which 5 were waited for; matrix products, arithmetic and copies ran while one was open for 1% of the time, Pallas kernels for 2%

profile of v11, /device:TPU:1, one launch (start us, length us, event | category | flops | bytes accessed | tf_op | source)
XLA Modules:
  0.0 150.1 jit_solution(11771744490329330996)
XLA Ops:
  7.2 0.0 all-gather.2.cloned.1.call-start
  7.2 0.0 copy-start.1
  7.2 0.9 copy-done.1
  8.1 0.2 chunks.1
  8.3 24.1 %all_to_all.20.piece_ref = f32[32,24,128]{2,1,0:T(8,128)S(1)} all-to-all(f32[32,24,128]{2,1,0:T(8,128)S(1)} %get-tuple-element.19), channel_id=1, replica_groups=mesh['z'=8,'yh'=4,'core'=2,'yl'=2,'x'=4] {'yh','yl','x'}, dimensions={0} | all-to-all | bytes 786432 | tf_op jit(solution)/shard_map/all_to_all | solution.py:210
  32.4 0.0 copy-start.2
  32.4 0.7 copy-done.2
  33.0 0.9 columns.1
  33.9 0.0 all-gather.2.cloned.1.call-update
  33.9 10.7 %collective-permute-start.1 = (f32[64,1536]{1,0:T(8,128)S(1)}, f32[64,1536]{1,0:T(8,128)S(1)}, u32[]{:S(2)}, u32[]{:S(2)}) collective-permute-start(f32[64,1536]{1,0:T(8,128)S(1)} %get-tuple-element.26.refs_0_), channel_id=1, source_target_pairs={{0,448},{64,128},{128,64},{192,256},{256,192},{320,384},{384,320},... | collective-permute-start | bytes 1179656 | tf_op jit(solution)/shard_map/ppermute | solution.py:202
  44.6 1.9 %collective-permute-start = (f32[64,1536]{1,0:T(8,128)S(1)}, f32[64,1536]{1,0:T(8,128)S(1)}, u32[]{:S(2)}, u32[]{:S(2)}) collective-permute-start(f32[64,1536]{1,0:T(8,128)S(1)} %get-tuple-element.26.refs_0_), channel_id=1, source_target_pairs={{0,64},{64,0},{128,192},{192,128},{256,320},{320,256},{384,448},{4... | collective-permute-start | bytes 1179656 | tf_op jit(solution)/shard_map/ppermute | solution.py:202
  46.5 5.0 %collective-permute-done.1.refs_4_ = f32[64,1536]{1,0:T(8,128)S(1)} collective-permute-done((f32[64,1536]{1,0:T(8,128)S(1)}, f32[64,1536]{1,0:T(8,128)S(1)}, u32[]{:S(2)}, u32[]{:S(2)}) %collective-permute-start.1) | collective-permute-done | bytes 393248 | tf_op jit(solution)/shard_map/ppermute | solution.py:202
  51.5 1.9 %collective-permute-start.2 = (f32[64,1536]{1,0:T(8,128)S(1)}, f32[64,1536]{1,0:T(8,128)S(1)}, u32[]{:S(2)}, u32[]{:S(2)}) collective-permute-start(f32[64,1536]{1,0:T(8,128)S(1)} %collective-permute-done.1.refs_4_), channel_id=1, source_target_pairs={{0,64},{64,0},{128,192},{192,128},{256,320},{320,256},{384,448},{4... | collective-permute-start | bytes 1179656 | tf_op jit(solution)/shard_map/ppermute | solution.py:202
  53.4 0.9 collective-permute-done.refs_1_
  54.3 3.4 %collective-permute-start.3 = (f32[64,1536]{1,0:T(8,128)S(1)}, f32[64,1536]{1,0:T(8,128)S(1)}, u32[]{:S(2)}, u32[]{:S(2)}) collective-permute-start(f32[64,1536]{1,0:T(8,128)S(1)} %collective-permute-done.refs_1_), channel_id=1, source_target_pairs={{0,448},{64,128},{128,64},{192,256},{256,192},{320,384},{384,320},... | collective-permute-start | bytes 1179656 | tf_op jit(solution)/shard_map/ppermute | solution.py:202
  57.7 6.2 %collective-permute-done.2.refs_2_ = f32[64,1536]{1,0:T(8,128)S(1)} collective-permute-done((f32[64,1536]{1,0:T(8,128)S(1)}, f32[64,1536]{1,0:T(8,128)S(1)}, u32[]{:S(2)}, u32[]{:S(2)}) %collective-permute-start.2) | collective-permute-done | bytes 393248 | tf_op jit(solution)/shard_map/ppermute | solution.py:202
  63.9 1.9 %collective-permute-start.5 = (f32[64,1536]{1,0:T(8,128)S(1)}, f32[64,1536]{1,0:T(8,128)S(1)}, u32[]{:S(2)}, u32[]{:S(2)}) collective-permute-start(f32[64,1536]{1,0:T(8,128)S(1)} %collective-permute-done.2.refs_2_), channel_id=1, source_target_pairs={{0,448},{64,128},{128,64},{192,256},{256,192},{320,384},{384,320},... | collective-permute-start | bytes 1179656 | tf_op jit(solution)/shard_map/ppermute | solution.py:202
  65.8 0.0 collective-permute-done.3.refs_5_
  65.8 2.3 %collective-permute-start.4 = (f32[64,1536]{1,0:T(8,128)S(1)}, f32[64,1536]{1,0:T(8,128)S(1)}, u32[]{:S(2)}, u32[]{:S(2)}) collective-permute-start(f32[64,1536]{1,0:T(8,128)S(1)} %collective-permute-done.3.refs_5_), channel_id=1, source_target_pairs={{0,64},{64,0},{128,192},{192,128},{256,320},{320,256},{384,448},{4... | collective-permute-start | bytes 1179656 | tf_op jit(solution)/shard_map/ppermute | solution.py:202
  68.2 7.4 %collective-permute-done.5.refs_6_ = f32[64,1536]{1,0:T(8,128)S(1)} collective-permute-done((f32[64,1536]{1,0:T(8,128)S(1)}, f32[64,1536]{1,0:T(8,128)S(1)}, u32[]{:S(2)}, u32[]{:S(2)}) %collective-permute-start.5) | collective-permute-done | bytes 393248 | tf_op jit(solution)/shard_map/ppermute | solution.py:202
  75.6 1.9 %collective-permute-start.6 = (f32[32,1536]{1,0:T(8,128)S(1)}, f32[32,1536]{1,0:T(8,128)S(1)}, u32[]{:S(2)}, u32[]{:S(2)}) collective-permute-start(f32[32,1536]{1,0:T(8,128)S(1)} %slice.8), channel_id=1, source_target_pairs={{0,64},{64,0},{128,192},{192,128},{256,320},{320,256},{384,448},{4... | collective-permute-start | bytes 589832 | tf_op jit(solution)/shard_map/ppermute | solution.py:205
  77.5 0.0 collective-permute-done.4.refs_3_
  77.5 0.7 slice.9
  78.2 3.0 %collective-permute-start.7 = (f32[32,1536]{1,0:T(8,128)}, f32[32,1536]{1,0:T(8,128)S(1)}, u32[]{:S(2)}, u32[]{:S(2)}) collective-permute-start(f32[32,1536]{1,0:T(8,128)} %slice.9), channel_id=1, source_target_pairs={{0,448},{64,128},{128,64},{192,256},{256,192},{320,384},{384,320},... | collective-permute-start | bytes 589832 | tf_op jit(solution)/shard_map/ppermute | solution.py:205
  81.2 0.1 pad_add_fusion.pos_ref
  81.3 0.0 all-gather.2.cloned.1.call-done
  81.3 0.0 copy-start
  81.3 1.4 copy-done
  82.7 1.3 norm.1
  84.0 2.2 %early.1.early_ref = f32[256,512]{1,0:T(8,128)S(1)} custom-call(s32[3]{0:T(128)S(1)} %pad_add_fusion.pos_ref, bf16[256,1536]{1,0:T(8,128)(2,1)S(1)} %get-tuple-element.22.hi_ref, bf16[256,1536]{1,0:T(8,128)(2,1)S(1)} %get-tuple-element.23.lo_ref, f32[64,1536]{1,0:T(8,128)S(1)} %get-tuple-element.26.refs_0_, f32[64,1536]{1,0:T(8,128)S(1)} %collective-permute-done.refs_1_, ...), custom_call_target="tpu_custom_call" | custom-call | tf_op jit(solution)/shard_map/early/pallas_call | solution.py:214
  86.3 0.0 collective-permute-done.6.refs_7_
  86.3 0.0 collective-permute-done.7.refs_8_
  86.3 1.8 %scores.1 = (f32[256,512]{1,0:T(8,128)S(1)}, f32[16,8,128]{2,1,0:T(8,128)S(1)}, f32[32,8,128]{2,1,0:T(8,128)S(1)}, f32[512,1536]{1,0:T(8,128)S(1)}) custom-call(s32[3]{0:T(128)S(1)} %pad_add_fusion.pos_ref, bf16[256,1536]{1,0:T(8,128)(2,1)S(1)} %get-tuple-element.22.hi_ref, bf16[256,1536]{1,0:T(8,128)(2,1)S(1)} %get-tuple-element.23.lo_ref, ...), custom_call_target="tpu_custom_call" | custom-call | tf_op jit(solution)/shard_map/scores/pallas_call | solution.py:214
  88.1 14.2 %all_to_all.21.rows_ref = f32[16,8,128]{2,1,0:T(8,128)S(1)} all-to-all(f32[16,8,128]{2,1,0:T(8,128)S(1)} %get-tuple-element.29), channel_id=1, replica_groups=mesh['z'=8,'yh'=4,'core'=2,'yl'=2,'x'=4] {'core','yl','x'}, dimensions={0} | all-to-all | bytes 131072 | tf_op jit(solution)/shard_map/all_to_all | solution.py:210
  102.3 16.3 %all_to_all.22.cols_l_ref = f32[32,8,128]{2,1,0:T(8,128)S(1)} all-to-all(f32[32,8,128]{2,1,0:T(8,128)S(1)} %get-tuple-element.30), channel_id=1, replica_groups=mesh['z'=8,'yh'=4,'core'=2,'yl'=2,'x'=4] {'z','yh'}, dimensions={0} | all-to-all | bytes 262144 | tf_op jit(solution)/shard_map/all_to_all | solution.py:210
  118.6 2.5 %gradient.1 = (f32[8,200,128]{2,1,0:T(8,128)S(1)}, f32[8,200,128]{2,1,0:T(8,128)S(1)}) custom-call(s32[3]{0:T(128)S(1)} %pad_add_fusion.pos_ref, f32[256,512]{1,0:T(8,128)S(1)} %get-tuple-element.27.s_ref, f32[512,1536]{1,0:T(8,128)S(1)} %get-tuple-element.28.cols_ref, s32[128,1]{1,0:T(8,128)S(1)} %get-tuple-element.24.ownp_ref, ...), custom_call_target="tpu_custom_call" | custom-call | tf_op jit(solution)/shard_map/gradient/pallas_call | solution.py:214
  121.1 3.9 %collective-permute-start.8 = (f32[8,200,128]{2,1,0:T(8,128)S(1)}, f32[8,200,128]{2,1,0:T(8,128)S(1)}, u32[]{:S(2)}, u32[]{:S(2)}) collective-permute-start(f32[8,200,128]{2,1,0:T(8,128)S(1)} %get-tuple-element.32), channel_id=1, source_target_pairs={{0,8},{8,0},{1,9},{9,1},{2,10},{10,2},{3,11},{11,3},{4,12},{12,4},... | collective-permute-start | bytes 2457608 | tf_op jit(solution)/shard_map/ppermute | solution.py:194
  125.0 1.9 %collective-permute-done.8 = f32[8,200,128]{2,1,0:T(8,128)S(1)} collective-permute-done((f32[8,200,128]{2,1,0:T(8,128)S(1)}, f32[8,200,128]{2,1,0:T(8,128)S(1)}, u32[]{:S(2)}, u32[]{:S(2)}) %collective-permute-start.8) | collective-permute-done | bytes 819232 | tf_op jit(solution)/shard_map/ppermute | solution.py:194
  126.9 0.1 add.11
  127.0 15.5 %all_to_all.23.piece_ref = f32[8,200,128]{2,1,0:T(8,128)S(1)} all-to-all(f32[8,200,128]{2,1,0:T(8,128)S(1)} %add.11), channel_id=1, replica_groups=mesh['z'=8,'yh'=4,'core'=2,'yl'=2,'x'=4] {'yl','x'}, dimensions={0} | all-to-all | bytes 1638400 | tf_op jit(solution)/shard_map/all_to_all | solution.py:210
  142.5 0.7 finish.1
  (1 shorter events, 0.0 us)
Async XLA Ops:
  7.2 74.1 %all-gather.2.cloned.1.call-start = ((), (), s32[]{:S(2)}) async-start(), calls=%async_computation.4 | async-start | bytes 1740800 | tf_op jit(solution)/shard_map/all_gather | solution.py:236
  7.2 0.9 copy-start.1
  32.4 0.7 copy-start.2
  33.9 17.6 %collective-permute-start.1 = (f32[64,1536]{1,0:T(8,128)S(1)}, f32[64,1536]{1,0:T(8,128)S(1)}, u32[]{:S(2)}, u32[]{:S(2)}) collective-permute-start(f32[64,1536]{1,0:T(8,128)S(1)} %get-tuple-element.26.refs_0_), channel_id=1, source_target_pairs={{0,448},{64,128},{128,64},{192,256},{256,192},{320,384},{384,320},... | collective-permute-start | bytes 1179656 | tf_op jit(solution)/shard_map/ppermute | solution.py:202
  44.6 9.7 %collective-permute-start = (f32[64,1536]{1,0:T(8,128)S(1)}, f32[64,1536]{1,0:T(8,128)S(1)}, u32[]{:S(2)}, u32[]{:S(2)}) collective-permute-start(f32[64,1536]{1,0:T(8,128)S(1)} %get-tuple-element.26.refs_0_), channel_id=1, source_target_pairs={{0,64},{64,0},{128,192},{192,128},{256,320},{320,256},{384,448},{4... | collective-permute-start | bytes 1179656 | tf_op jit(solution)/shard_map/ppermute | solution.py:202
  51.5 12.4 %collective-permute-start.2 = (f32[64,1536]{1,0:T(8,128)S(1)}, f32[64,1536]{1,0:T(8,128)S(1)}, u32[]{:S(2)}, u32[]{:S(2)}) collective-permute-start(f32[64,1536]{1,0:T(8,128)S(1)} %collective-permute-done.1.refs_4_), channel_id=1, source_target_pairs={{0,64},{64,0},{128,192},{192,128},{256,320},{320,256},{384,448},{4... | collective-permute-start | bytes 1179656 | tf_op jit(solution)/shard_map/ppermute | solution.py:202
  54.3 11.5 %collective-permute-start.3 = (f32[64,1536]{1,0:T(8,128)S(1)}, f32[64,1536]{1,0:T(8,128)S(1)}, u32[]{:S(2)}, u32[]{:S(2)}) collective-permute-start(f32[64,1536]{1,0:T(8,128)S(1)} %collective-permute-done.refs_1_), channel_id=1, source_target_pairs={{0,448},{64,128},{128,64},{192,256},{256,192},{320,384},{384,320},... | collective-permute-start | bytes 1179656 | tf_op jit(solution)/shard_map/ppermute | solution.py:202
  63.9 11.6 %collective-permute-start.5 = (f32[64,1536]{1,0:T(8,128)S(1)}, f32[64,1536]{1,0:T(8,128)S(1)}, u32[]{:S(2)}, u32[]{:S(2)}) collective-permute-start(f32[64,1536]{1,0:T(8,128)S(1)} %collective-permute-done.2.refs_2_), channel_id=1, source_target_pairs={{0,448},{64,128},{128,64},{192,256},{256,192},{320,384},{384,320},... | collective-permute-start | bytes 1179656 | tf_op jit(solution)/shard_map/ppermute | solution.py:202
  65.8 11.7 %collective-permute-start.4 = (f32[64,1536]{1,0:T(8,128)S(1)}, f32[64,1536]{1,0:T(8,128)S(1)}, u32[]{:S(2)}, u32[]{:S(2)}) collective-permute-start(f32[64,1536]{1,0:T(8,128)S(1)} %collective-permute-done.3.refs_5_), channel_id=1, source_target_pairs={{0,64},{64,0},{128,192},{192,128},{256,320},{320,256},{384,448},{4... | collective-permute-start | bytes 1179656 | tf_op jit(solution)/shard_map/ppermute | solution.py:202
  75.6 10.7 %collective-permute-start.6 = (f32[32,1536]{1,0:T(8,128)S(1)}, f32[32,1536]{1,0:T(8,128)S(1)}, u32[]{:S(2)}, u32[]{:S(2)}) collective-permute-start(f32[32,1536]{1,0:T(8,128)S(1)} %slice.8), channel_id=1, source_target_pairs={{0,64},{64,0},{128,192},{192,128},{256,320},{320,256},{384,448},{4... | collective-permute-start | bytes 589832 | tf_op jit(solution)/shard_map/ppermute | solution.py:205
  78.2 8.1 %collective-permute-start.7 = (f32[32,1536]{1,0:T(8,128)}, f32[32,1536]{1,0:T(8,128)S(1)}, u32[]{:S(2)}, u32[]{:S(2)}) collective-permute-start(f32[32,1536]{1,0:T(8,128)} %slice.9), channel_id=1, source_target_pairs={{0,448},{64,128},{128,64},{192,256},{256,192},{320,384},{384,320},... | collective-permute-start | bytes 589832 | tf_op jit(solution)/shard_map/ppermute | solution.py:205
  81.3 1.4 copy-start
  121.1 5.9 %collective-permute-start.8 = (f32[8,200,128]{2,1,0:T(8,128)S(1)}, f32[8,200,128]{2,1,0:T(8,128)S(1)}, u32[]{:S(2)}, u32[]{:S(2)}) collective-permute-start(f32[8,200,128]{2,1,0:T(8,128)S(1)} %get-tuple-element.32), channel_id=1, source_target_pairs={{0,8},{8,0},{1,9},{9,1},{2,10},{10,2},{3,11},{11,3},{4,12},{12,4},... | collective-permute-start | bytes 2457608 | tf_op jit(solution)/shard_map/ppermute | solution.py:194
Sparse Core Ops, SparseCore 0:
  34.0 39.6 all-gather.1

commit v12 on v3

--- a/solution.py
+++ b/solution.py
@@ -13,12 +13,12 @@
 CHUNK = ROWS // NF
 NCOL = NZ * NYH * CHUNK
 PIECE = FEAT + 8
+BLOCK = NYH * CHUNK
 TOTAL = 8192
 INV_TAU = 10.0
 VMEM = pl.BlockSpec(memory_space=pltpu.VMEM)
 SMEM = pl.BlockSpec(memory_space=pltpu.SMEM)
 HBM = pl.BlockSpec(memory_space=pltpu.HBM)
-MIB = 1024 * 1024
 
 
 def f32(*shape):
@@ -52,7 +52,8 @@
     return jnp.concatenate([x[:CHUNK, :], jnp.concatenate([tail[:, :rest], tail[:, rest:]], axis=0)], axis=1)
 
 
-def chunk_kernel(view_ref, out_ref):
+def chunk_kernel(view_ref, out_ref, copy_ref):
+    copy_ref[...] = view_ref[...]
     x = view_ref[...].T
     for f in range(NF):
         piece = pack(x[f * CHUNK:(f + 1) * CHUNK, :])
@@ -60,7 +61,9 @@
             out_ref[y * NF + f] = piece
 
 
-def column_kernel(piece_ref, unit_ref):
+def column_kernel(piece_ref, view_ref, unit_ref, copies_ref):
+    for f in range(NF):
+        copies_ref[f] = view_ref[...]
     for y in range(NYH):
         x = jnp.concatenate([unpack(piece_ref[y * NF + f]) for f in range(NF)], axis=1)
         scale = lax.rsqrt(jnp.sum(x * x, axis=1, keepdims=True) + 1e-06)
@@ -68,10 +71,16 @@
 
 
 def norm_kernel(piece_ref, unit_ref, scale_ref):
-    x = piece_ref[...]
+    x = piece_ref[...].reshape(WIDE, ROWS)
     scale = lax.rsqrt(jnp.sum(x * x, axis=0, keepdims=True) + 1e-06)
     scale_ref[...] = scale
     unit_ref[...] = (x * scale).T
+
+
+def rows_kernel(own_ref, oth_ref, hi_ref, lo_ref):
+    for j, ref in enumerate((own_ref, oth_ref)):
+        at = slice(j * ROWS, (j + 1) * ROWS)
+        hi_ref[at, :], lo_ref[at, :] = split(ref[...])
 
 
 def tile_masks(pos_ref, half, part):
@@ -82,21 +91,18 @@
     return col == row, col == part
 
 
-def score_kernel(pos_ref, own_ref, oth_ref, cols_hbm, ownp_ref, othp_ref, s_ref, row_ref, col_ref, hi, lo, cols, sems):
+def score_kernel(pos_ref, hi_ref, lo_ref, ownp_ref, othp_ref, far_ref, s_ref, row_ref, col_ref, cols_ref, sems):
     core = pos_ref[1]
     step = 256
     copies = []
     for i in range(NCOL // step):
         at = pl.ds(i * step, step)
-        copies.append(pltpu.make_async_copy(cols_hbm.at[at, :], cols.at[at, :], sems.at[i]))
+        copies.append(pltpu.make_async_copy(far_ref.at[at, :], cols_ref.at[at, :], sems.at[i]))
         copies[-1].start()
-    for j, ref in enumerate((own_ref, oth_ref)):
-        hi[j], lo[j] = split(ref[...])
-    rows = (hi[...].reshape(NC * ROWS, WIDE), lo[...].reshape(NC * ROWS, WIDE))
     for i, copy in enumerate(copies):
         at = slice(i * step, (i + 1) * step)
         copy.wait()
-        s_ref[:, at] = INV_TAU * dot3(rows, split(cols[at, :]), ((1,), (1,)))
+        s_ref[:, at] = INV_TAU * dot3((hi_ref[...], lo_ref[...]), split(cols_ref[at, :]), ((1,), (1,)))
     colsum = jnp.zeros((1, NCOL), jnp.float32)
     pos = jnp.zeros((1, ROWS), jnp.float32)
     sums = []
@@ -118,12 +124,13 @@
     nrow = NCOL // ROWS
     col = jnp.concatenate([colsum[:, c * ROWS:(c + 1) * ROWS] for c in range(nrow)]
                           + [pos, jnp.zeros((7 - nrow, ROWS), jnp.float32)], axis=0)
-    row_ref[...] = row
+    for k in range(NC * NF):
+        row_ref[k] = row
     for k in range(NZ * NYH):
         col_ref[k] = col
 
 
-def grad_kernel(pos_ref, s_ref, own_ref, oth_ref, cols_ref, ownp_ref, othp_ref, rows_ref, cols_l_ref, mine_ref, theirs_ref, w_hi, w_lo):
+def grad_kernel(pos_ref, s_ref, cols_ref, ownp_ref, othp_ref, rows_ref, cols_l_ref, mine_ref, theirs_ref, w_hi, w_lo):
     core = pos_ref[1]
     row_l = jnp.sum(rows_ref[...], axis=0)
     col_l = jnp.sum(cols_l_ref[...], axis=0)
@@ -137,25 +144,28 @@
         diag, hit = tile_masks(pos_ref, half, part[...])
         inv = column(1.0 / jnp.where(half == 0, row_l[0:1, :], row_l[1:2, :]))
         w = jnp.where(diag, 0.0, jnp.exp(s) * (inv + col_inv)) - jnp.where(hit, 2.0, 0.0)
-        projs.append(jnp.sum(w * s, axis=1, keepdims=True))
+        ws = w * s
+        lanes = sum(ws[:, c * ROWS:(c + 1) * ROWS] for c in range(NCOL // ROWS))
+        projs.append(jnp.sum(lanes.T, axis=0, keepdims=True))
         w_hi[j], w_lo[j] = split(w)
     weights = (w_hi[...].reshape(NC * ROWS, NCOL), w_lo[...].reshape(NC * ROWS, NCOL))
-    step = 2 * FEAT
-    tail = jnp.concatenate([loss, jnp.zeros((7, ROWS), jnp.float32)], axis=0)
+    step = 4 * FEAT
+    tails = [jnp.concatenate([loss, proj, jnp.zeros((6, ROWS), jnp.float32)], axis=0) for proj in projs]
     for c in range(WIDE // step):
         at = slice(c * step, (c + 1) * step)
         g = INV_TAU * dot3(weights, split(cols_ref[:, at]), ((1,), (0,)))
-        for j, (units, out) in enumerate(((own_ref, mine_ref), (oth_ref, theirs_ref))):
-            t = (g[j * ROWS:(j + 1) * ROWS, :] - units[:, at] * projs[j]).T
-            for p in range(2):
-                out[2 * c + p, :FEAT, :] = t[p * FEAT:(p + 1) * FEAT, :]
-                out[2 * c + p, FEAT:, :] = tail
-
-
-def last_kernel(piece_ref, scale_ref, loss_ref, grad_ref):
+        for j, out in enumerate((mine_ref, theirs_ref)):
+            t = g[j * ROWS:(j + 1) * ROWS, :].T
+            for p in range(4):
+                out[4 * c + p, :FEAT, :] = t[p * FEAT:(p + 1) * FEAT, :]
+                out[4 * c + p, FEAT:, :] = tails[j]
+
+
+def last_kernel(piece_ref, scale_ref, view_ref, loss_ref, grad_ref):
     total = jnp.sum(piece_ref[...], axis=0)
     loss_ref[...] = jnp.sum(total[FEAT:FEAT + 1, :], axis=1, keepdims=True) / TOTAL
-    grad_ref[...] = total[:FEAT, :] * scale_ref[...]
+    scale = scale_ref[...]
+    grad_ref[...] = (total[:FEAT, :] - view_ref[...] * scale * total[FEAT + 1:FEAT + 2, :]) * scale
 
 
 def swap(x, axes, size, k):
@@ -173,7 +183,7 @@
         in_specs=[SMEM if a.shape == (3,) else HBM if i in far else VMEM for i, a in enumerate(args)],
         out_specs=[VMEM] * len(outs),
         scratch_shapes=list(scratch),
-        compiler_params=pltpu.CompilerParams(vmem_limit_bytes=limit * MIB),
+        compiler_params=pltpu.CompilerParams(vmem_limit_bytes=limit * 1024 * 1024),
         name=name,
     )(*args)
 
@@ -185,33 +195,33 @@
     pos = jnp.stack([zy, core, me]).astype(jnp.int32)
     feat = ("yl", "x")
 
+    packed = CHUNK * FEAT // ROWS
+    chunks, copy = call(chunk_kernel, "chunks", [f32(NYH * NF, packed, ROWS), f32(FEAT, ROWS)], [views.T])
+    chunk, copies = call(column_kernel, "columns", [f32(BLOCK, WIDE), f32(NF, FEAT, ROWS)],
+                         [trade(chunks, ("yh", "yl", "x")), copy])
+    far = lax.all_gather(chunk, "z", axis=0, tiled=True)
+    own, scale = call(norm_kernel, "norm", [f32(ROWS, WIDE), f32(1, ROWS)], [trade(copies, feat)])
+    hi, lo = call(rows_kernel, "rows", [jax.ShapeDtypeStruct((NC * ROWS, WIDE), jnp.bfloat16)] * 2,
+                  [own, swap(own, "core", NC, 1)])
     own_p = partner.reshape(ROWS, 1)
     oth_p = swap(partner, "core", NC, 1).reshape(ROWS, 1)
-    packed = CHUNK * FEAT // ROWS
-    whole = lax.all_gather(views.T, feat, axis=0, tiled=True)
-    chunks, = call(chunk_kernel, "chunks", [f32(NYH * NF, packed, ROWS)], [views.T])
-    chunk, = call(column_kernel, "columns", [f32(NYH * CHUNK, WIDE)], [trade(chunks, ("yh", "yl", "x"))])
-    cols = lax.all_gather(chunk, "z", axis=0, tiled=True)
-    own, scale = call(norm_kernel, "norm", [f32(ROWS, WIDE), f32(1, ROWS)], [whole])
-    oth = swap(own, "core", NC, 1)
-    s, row, col = call(
+    s, row, col, cols = call(
         score_kernel, "scores",
-        [f32(NC * ROWS, NCOL), f32(8, ROWS), f32(NZ * NYH, 8, ROWS)],
-        [pos, own, oth, cols, own_p, oth_p],
-        [pltpu.VMEM((NC, ROWS, WIDE), jnp.bfloat16)] * 2
-        + [pltpu.VMEM((NCOL, WIDE), jnp.float32), pltpu.SemaphoreType.DMA((NCOL // 256,))],
-        far=(3,), limit=48,
+        [f32(NC * ROWS, NCOL), f32(NC * NF, 8, ROWS), f32(NZ * NYH, 8, ROWS), f32(NCOL, WIDE)],
+        [pos, hi, lo, own_p, oth_p, far],
+        [pltpu.SemaphoreType.DMA((NCOL // 256,))],
+        far=(5,), limit=48,
     )
-    rows_l = lax.all_gather(row, ("core", "yl", "x"), axis=0, tiled=False)
+    rows_l = trade(row, ("core", "yl", "x"))
     cols_l = trade(col, ("z", "yh"))
     mine, theirs = call(
         grad_kernel, "gradient",
         [f32(NF, PIECE, ROWS)] * 2,
-        [pos, s, own, oth, cols, own_p, oth_p, rows_l, cols_l],
+        [pos, s, cols, own_p, oth_p, rows_l, cols_l],
         [pltpu.VMEM((NC, ROWS, NCOL), jnp.bfloat16)] * 2,
     )
     pieces = trade(mine + swap(theirs, "core", NC, 1), feat)
-    loss, grad = call(last_kernel, "finish", [f32(1, 1), f32(FEAT, ROWS)], [pieces, scale])
+    loss, grad = call(last_kernel, "finish", [f32(1, 1), f32(FEAT, ROWS)], [pieces, scale, copy])
     return loss.reshape(()), grad.T
 
 

time: 168 us -> 150 us (0.89)
  waiting for transfers between devices: 12.8 us -> 29.6 us
  blocking collectives: 96.9 us -> 83.3 us
  starting transfers between devices: 22.7 us -> 11.8 us
  local copies, waits for them, and re-layouts: 11.1 us -> 1.11 us
    all_gather x2 -> x0, blocking collectives: 54.9 us -> none  [the longest x1 30.2 us: per_device(): rows_l = lax.all_gather(row, ('core', 'yl', 'x'), axis=0, tiled=False)]
    all_to_all x2 -> x5, blocking collectives: 42.1 us -> 83.3 us  [trade(): return lax.all_to_all(x, axes, 0, 0, tiled=True)]
    all_gather x1, waiting for transfers between devices: 9.57 us -> 26.7 us  [per_device(): far = lax.all_gather(chunk, 'z', axis=0, tiled=True)]
    unnamed x24 -> x4, local copies, waits for them, and re-layouts: 10.9 us -> 0.89 us
    all_to_all x1 -> x0, starting transfers between devices: 9.09 us -> none  [trade(): return lax.all_to_all(x, axes, 0, 0, tiled=True)]
    ppermute x3, starting transfers between devices: 13.6 us -> 11.7 us  [swap(): return lax.ppermute(x, axes, [(i, i ^ k) for i in range(size)])]
    pallas_call x6 -> x7, Pallas kernels: 9.74 us -> 10 us  [call(): pl.pallas_call(body, out_shape=outs, in_specs=[SMEM if a.shape == (3,) el...]
  transfers between devices with their start and end apart: 5 -> 4, of which waited for: 3 -> 3; matrix products, arithmetic and copies ran while one was open for 0% -> 0% of each run, Pallas kernels for 0% -> 0%
where the time goes in v12:
time: 150 us
  blocking collectives  83.3 us (56%)
  waiting for transfers between devices  29.6 us (20%)
  between operations  14.1 us (9%)
  starting transfers between devices  11.8 us (8%)
  Pallas kernels  10 us (7%)
    all_to_all x5, blocking collectives, trade(): return lax.all_to_all(x, axes, 0, 0, tiled=True)  83.3 us
    all_gather x1, waiting for transfers between devices, per_device(): far = lax.all_gather(chunk, 'z', axis=0, tiled=True)  26.7 us
    ppermute x3, starting transfers between devices, swap(): return lax.ppermute(x, axes, [(i, i ^ k) for i in range(size)])  11.7 us
    pallas_call x7, Pallas kernels, call(): pl.pallas_call(body, out_shape=outs, in_specs=[SMEM if a.shape == (3,) el...  10 us
  transfers between devices with their start and end apart: 4, of which 3 were waited for; matrix products, arithmetic and copies ran while one was open for 0% of the time, Pallas kernels for 0%

profile of v12, /device:TPU:1, one launch (start us, length us, event | category | flops | bytes accessed | tf_op | source)
XLA Modules:
  0.0 150.0 jit_solution(3983865483708851637)
XLA Ops:
  7.2 0.0 copy-start.1
  7.2 0.0 all-gather.2.cloned.1.call-start
  7.2 0.0 copy-start
  7.2 0.9 copy-done
  8.1 0.2 chunks.1
  8.3 24.1 %all_to_all.25.piece_ref = f32[32,24,128]{2,1,0:T(8,128)S(1)} all-to-all(f32[32,24,128]{2,1,0:T(8,128)S(1)} %get-tuple-element.18), channel_id=1, replica_groups=mesh['z'=8,'yh'=4,'core'=2,'yl'=2,'x'=4] {'yh','yl','x'}, dimensions={0} | all-to-all | bytes 786432 | tf_op jit(solution)/shard_map/all_to_all | solution.py:176
  32.4 1.1 columns.1
  33.4 0.0 all-gather.2.cloned.1.call-update
  33.5 12.9 %all_to_all.26.piece_ref = f32[8,192,128]{2,1,0:T(8,128)S(1)} all-to-all(f32[8,192,128]{2,1,0:T(8,128)S(1)} %get-tuple-element.20), channel_id=1, replica_groups=mesh['z'=8,'yh'=4,'core'=2,'yl'=2,'x'=4] {'yl','x'}, dimensions={0} | all-to-all | bytes 1572864 | tf_op jit(solution)/shard_map/all_to_all | solution.py:176
  46.3 0.5 norm.1
  46.8 5.9 %collective-permute-start = (f32[128,1536]{1,0:T(8,128)S(1)}, f32[128,1536]{1,0:T(8,128)S(1)}, u32[]{:S(2)}, u32[]{:S(2)}) collective-permute-start(f32[128,1536]{1,0:T(8,128)S(1)} %get-tuple-element.21.own_ref), channel_id=1, source_target_pairs={{0,8},{8,0},{1,9},{9,1},{2,10},{10,2},{3,11},{11,3},{4,12},{12,4},... | collective-permute-start | bytes 2359304 | tf_op jit(solution)/shard_map/ppermute | solution.py:172
  52.7 0.0 copy-done.1
  52.7 1.9 %collective-permute-start.1 = (s32[128]{0:T(128)S(1)}, s32[128]{0:T(128)S(1)}, u32[]{:S(2)}, u32[]{:S(2)}) collective-permute-start(s32[128]{0:T(128)S(1)} %copy-done.1), channel_id=1, source_target_pairs={{0,8},{8,0},{1,9},{9,1},{2,10},{10,2},{3,11},{11,3},{4,12},{12,4},... | collective-permute-start | bytes 1544 | tf_op jit(solution)/shard_map/ppermute | solution.py:172
  54.7 0.1 pad_add_fusion.pos_ref
  54.8 0.1 copy.4.ownp_ref
  54.9 0.9 collective-permute-done.1
  55.8 0.1 copy.5.othp_ref
  55.9 0.0 collective-permute-done.oth_ref
  55.9 0.2 rows.1
  56.1 26.7 %all-gather.2.cloned.1.call-done.far_ref = f32[512,1536]{1,0:T(8,128)} async-done(((f32[64,1536]{1,0:T(8,128)}), f32[512,1536]{1,0:T(8,128)}) %all-gather.2.cloned.1.call-update) | async-done | bytes 3145744 | tf_op jit(solution)/shard_map/all_gather | solution.py:202
  82.8 4.9 %scores.1 = (f32[256,512]{1,0:T(8,128)S(1)}, f32[16,8,128]{2,1,0:T(8,128)S(1)}, f32[32,8,128]{2,1,0:T(8,128)S(1)}, f32[512,1536]{1,0:T(8,128)S(1)}) custom-call(s32[3]{0:T(128)S(1)} %pad_add_fusion.pos_ref, bf16[256,1536]{1,0:T(8,128)(2,1)S(1)} %get-tuple-element.22.hi_ref, bf16[256,1536]{1,0:T(8,128)(2,1)S(1)} %get-tuple-element.23.lo_ref, ...), custom_call_target="tpu_custom_call" | custom-call | tf_op jit(solution)/shard_map/scores/pallas_call | solution.py:180
  87.7 11.5 %all_to_all.27.rows_ref = f32[16,8,128]{2,1,0:T(8,128)S(1)} all-to-all(f32[16,8,128]{2,1,0:T(8,128)S(1)} %get-tuple-element.27), channel_id=1, replica_groups=mesh['z'=8,'yh'=4,'core'=2,'yl'=2,'x'=4] {'core','yl','x'}, dimensions={0} | all-to-all | bytes 131072 | tf_op jit(solution)/shard_map/all_to_all | solution.py:176
  99.2 19.3 %all_to_all.28.cols_l_ref = f32[32,8,128]{2,1,0:T(8,128)S(1)} all-to-all(f32[32,8,128]{2,1,0:T(8,128)S(1)} %get-tuple-element.28), channel_id=1, replica_groups=mesh['z'=8,'yh'=4,'core'=2,'yl'=2,'x'=4] {'z','yh'}, dimensions={0} | all-to-all | bytes 262144 | tf_op jit(solution)/shard_map/all_to_all | solution.py:176
  118.5 2.5 %gradient.1 = (f32[8,200,128]{2,1,0:T(8,128)S(1)}, f32[8,200,128]{2,1,0:T(8,128)S(1)}) custom-call(s32[3]{0:T(128)S(1)} %pad_add_fusion.pos_ref, f32[256,512]{1,0:T(8,128)S(1)} %get-tuple-element.25.s_ref, f32[512,1536]{1,0:T(8,128)S(1)} %get-tuple-element.26.cols_ref, s32[128,1]{1,0:T(8,128)S(1)} %copy.4.ownp_ref, s32[128,1]{1,0:T(8,128)S(1)} %copy.5.othp_ref, ...), custom_call_target="tpu_custom_call" | custom-call | tf_op jit(solution)/shard_map/gradient/pallas_call | solution.py:180
  121.0 3.9 %collective-permute-start.2 = (f32[8,200,128]{2,1,0:T(8,128)S(1)}, f32[8,200,128]{2,1,0:T(8,128)S(1)}, u32[]{:S(2)}, u32[]{:S(2)}) collective-permute-start(f32[8,200,128]{2,1,0:T(8,128)S(1)} %get-tuple-element.30), channel_id=1, source_target_pairs={{0,8},{8,0},{1,9},{9,1},{2,10},{10,2},{3,11},{11,3},{4,12},{12,4},... | collective-permute-start | bytes 2457608 | tf_op jit(solution)/shard_map/ppermute | solution.py:172
  125.0 1.9 %collective-permute-done.2 = f32[8,200,128]{2,1,0:T(8,128)S(1)} collective-permute-done((f32[8,200,128]{2,1,0:T(8,128)S(1)}, f32[8,200,128]{2,1,0:T(8,128)S(1)}, u32[]{:S(2)}, u32[]{:S(2)}) %collective-permute-start.2) | collective-permute-done | bytes 819232 | tf_op jit(solution)/shard_map/ppermute | solution.py:172
  126.9 0.1 add.11
  127.0 15.5 %all_to_all.29.piece_ref = f32[8,200,128]{2,1,0:T(8,128)S(1)} all-to-all(f32[8,200,128]{2,1,0:T(8,128)S(1)} %add.11), channel_id=1, replica_groups=mesh['z'=8,'yh'=4,'core'=2,'yl'=2,'x'=4] {'yl','x'}, dimensions={0} | all-to-all | bytes 1638400 | tf_op jit(solution)/shard_map/all_to_all | solution.py:176
  142.5 0.7 finish.1
Async XLA Ops:
  7.2 45.6 %copy-start.1 = (s32[128]{0:T(128)S(1)}, s32[128]{0:T(128)}, u32[]{:S(2)}) copy-start(s32[128]{0:T(128)} %param.3) | copy-start | bytes 1540
  7.2 75.7 %all-gather.2.cloned.1.call-start = ((), (), s32[]{:S(2)}) async-start(), calls=%async_computation.5 | async-start | bytes 3538944 | tf_op jit(solution)/shard_map/all_gather | solution.py:202
  7.2 0.9 copy-start
  46.8 9.1 %collective-permute-start = (f32[128,1536]{1,0:T(8,128)S(1)}, f32[128,1536]{1,0:T(8,128)S(1)}, u32[]{:S(2)}, u32[]{:S(2)}) collective-permute-start(f32[128,1536]{1,0:T(8,128)S(1)} %get-tuple-element.21.own_ref), channel_id=1, source_target_pairs={{0,8},{8,0},{1,9},{9,1},{2,10},{10,2},{3,11},{11,3},{4,12},{12,4},... | collective-permute-start | bytes 2359304 | tf_op jit(solution)/shard_map/ppermute | solution.py:172
  52.7 3.0 %collective-permute-start.1 = (s32[128]{0:T(128)S(1)}, s32[128]{0:T(128)S(1)}, u32[]{:S(2)}, u32[]{:S(2)}) collective-permute-start(s32[128]{0:T(128)S(1)} %copy-done.1), channel_id=1, source_target_pairs={{0,8},{8,0},{1,9},{9,1},{2,10},{10,2},{3,11},{11,3},{4,12},{12,4},... | collective-permute-start | bytes 1544 | tf_op jit(solution)/shard_map/ppermute | solution.py:172
  121.0 5.9 %collective-permute-start.2 = (f32[8,200,128]{2,1,0:T(8,128)S(1)}, f32[8,200,128]{2,1,0:T(8,128)S(1)}, u32[]{:S(2)}, u32[]{:S(2)}) collective-permute-start(f32[8,200,128]{2,1,0:T(8,128)S(1)} %get-tuple-element.30), channel_id=1, source_target_pairs={{0,8},{8,0},{1,9},{9,1},{2,10},{10,2},{3,11},{11,3},{4,12},{12,4},... | collective-permute-start | bytes 2457608 | tf_op jit(solution)/shard_map/ppermute | solution.py:172
Sparse Core Ops, SparseCore 0:
  33.6 49.2 all-gather.1

commit v13 on v12

--- a/solution.py
+++ b/solution.py
@@ -1,3 +1,5 @@
+import functools
+
 import jax
 import jax.numpy as jnp
 from jax import lax
@@ -61,9 +63,12 @@
             out_ref[y * NF + f] = piece
 
 
-def column_kernel(piece_ref, view_ref, unit_ref, copies_ref):
+def copies_kernel(view_ref, after_ref, copies_ref):
     for f in range(NF):
         copies_ref[f] = view_ref[...]
+
+
+def column_kernel(piece_ref, unit_ref):
     for y in range(NYH):
         x = jnp.concatenate([unpack(piece_ref[y * NF + f]) for f in range(NF)], axis=1)
         scale = lax.rsqrt(jnp.sum(x * x, axis=1, keepdims=True) + 1e-06)
@@ -130,35 +135,30 @@
         col_ref[k] = col
 
 
-def grad_kernel(pos_ref, s_ref, cols_ref, ownp_ref, othp_ref, rows_ref, cols_l_ref, mine_ref, theirs_ref, w_hi, w_lo):
+def grad_kernel(j, pos_ref, s_ref, cols_ref, part_ref, rows_ref, cols_l_ref, out_ref):
     core = pos_ref[1]
     row_l = jnp.sum(rows_ref[...], axis=0)
     col_l = jnp.sum(cols_l_ref[...], axis=0)
     nrow = NCOL // ROWS
     col_inv = jnp.concatenate([1.0 / col_l[c:c + 1, :] for c in range(nrow)], axis=1)
     loss = jnp.sum(jnp.log(col_l[:nrow, :]), axis=0, keepdims=True) - col_l[nrow:nrow + 1, :]
-    projs = []
-    for j, part in enumerate((ownp_ref, othp_ref)):
-        s = s_ref[j * ROWS:(j + 1) * ROWS, :]
-        half = core ^ j
-        diag, hit = tile_masks(pos_ref, half, part[...])
-        inv = column(1.0 / jnp.where(half == 0, row_l[0:1, :], row_l[1:2, :]))
-        w = jnp.where(diag, 0.0, jnp.exp(s) * (inv + col_inv)) - jnp.where(hit, 2.0, 0.0)
-        ws = w * s
-        lanes = sum(ws[:, c * ROWS:(c + 1) * ROWS] for c in range(NCOL // ROWS))
-        projs.append(jnp.sum(lanes.T, axis=0, keepdims=True))
-        w_hi[j], w_lo[j] = split(w)
-    weights = (w_hi[...].reshape(NC * ROWS, NCOL), w_lo[...].reshape(NC * ROWS, NCOL))
+    s = s_ref[j * ROWS:(j + 1) * ROWS, :]
+    half = core ^ j
+    diag, hit = tile_masks(pos_ref, half, part_ref[...])
+    inv = column(1.0 / jnp.where(half == 0, row_l[0:1, :], row_l[1:2, :]))
+    w = jnp.where(diag, 0.0, jnp.exp(s) * (inv + col_inv)) - jnp.where(hit, 2.0, 0.0)
+    ws = w * s
+    lanes = sum(ws[:, c * ROWS:(c + 1) * ROWS] for c in range(NCOL // ROWS))
+    proj = jnp.sum(lanes.T, axis=0, keepdims=True)
+    weights = split(w)
     step = 4 * FEAT
-    tails = [jnp.concatenate([loss, proj, jnp.zeros((6, ROWS), jnp.float32)], axis=0) for proj in projs]
+    tail = jnp.concatenate([loss, proj, jnp.zeros((6, ROWS), jnp.float32)], axis=0)
     for c in range(WIDE // step):
         at = slice(c * step, (c + 1) * step)
-        g = INV_TAU * dot3(weights, split(cols_ref[:, at]), ((1,), (0,)))
-        for j, out in enumerate((mine_ref, theirs_ref)):
-            t = g[j * ROWS:(j + 1) * ROWS, :].T
-            for p in range(4):
-                out[4 * c + p, :FEAT, :] = t[p * FEAT:(p + 1) * FEAT, :]
-                out[4 * c + p, FEAT:, :] = tails[j]
+        t = (INV_TAU * dot3(weights, split(cols_ref[:, at]), ((1,), (0,)))).T
+        for p in range(4):
+            out_ref[4 * c + p, :FEAT, :] = t[p * FEAT:(p + 1) * FEAT, :]
+            out_ref[4 * c + p, FEAT:, :] = tail
 
 
 def last_kernel(piece_ref, scale_ref, view_ref, loss_ref, grad_ref):
@@ -197,9 +197,9 @@
 
     packed = CHUNK * FEAT // ROWS
     chunks, copy = call(chunk_kernel, "chunks", [f32(NYH * NF, packed, ROWS), f32(FEAT, ROWS)], [views.T])
-    chunk, copies = call(column_kernel, "columns", [f32(BLOCK, WIDE), f32(NF, FEAT, ROWS)],
-                         [trade(chunks, ("yh", "yl", "x")), copy])
+    chunk, = call(column_kernel, "columns", [f32(BLOCK, WIDE)], [trade(chunks, ("yh", "yl", "x"))])
     far = lax.all_gather(chunk, "z", axis=0, tiled=True)
+    copies, = call(copies_kernel, "copies", [f32(NF, FEAT, ROWS)], [copy, chunk], far=(1,))
     own, scale = call(norm_kernel, "norm", [f32(ROWS, WIDE), f32(1, ROWS)], [trade(copies, feat)])
     hi, lo = call(rows_kernel, "rows", [jax.ShapeDtypeStruct((NC * ROWS, WIDE), jnp.bfloat16)] * 2,
                   [own, swap(own, "core", NC, 1)])
@@ -214,11 +214,9 @@
     )
     rows_l = trade(row, ("core", "yl", "x"))
     cols_l = trade(col, ("z", "yh"))
-    mine, theirs = call(
-        grad_kernel, "gradient",
-        [f32(NF, PIECE, ROWS)] * 2,
-        [pos, s, cols, own_p, oth_p, rows_l, cols_l],
-        [pltpu.VMEM((NC, ROWS, NCOL), jnp.bfloat16)] * 2,
+    theirs, mine = (
+        call(functools.partial(grad_kernel, j), name, [f32(NF, PIECE, ROWS)], [pos, s, cols, part, rows_l, cols_l])[0]
+        for j, name, part in ((1, "theirs", oth_p), (0, "mine", own_p))
     )
     pieces = trade(mine + swap(theirs, "core", NC, 1), feat)
     loss, grad = call(last_kernel, "finish", [f32(1, 1), f32(FEAT, ROWS)], [pieces, scale, copy])

time: 150 us -> 150 us (level)
  waiting for transfers between devices: 29.6 us -> 27.6 us
    ppermute x3, waiting for transfers between devices: 2.83 us -> 0.9 us  [swap(): return lax.ppermute(x, axes, [(i, i ^ k) for i in range(size)])]
    pallas_call x7 -> x9, Pallas kernels: 10 us -> 11.4 us  [call(): pl.pallas_call(body, out_shape=outs, in_specs=[SMEM if a.shape == (3,) el...]
  transfers between devices with their start and end apart: 4 -> 4, of which waited for: 3 -> 2; matrix products, arithmetic and copies ran while one was open for 0% -> 0% of each run, Pallas kernels for 0% -> 2%
where the time goes in v13:
time: 150 us; the launch traced here: 149 us
  blocking collectives  83.3 us (56%)
  waiting for transfers between devices  27.6 us (18%)
  between operations  14.1 us (9%)
  starting transfers between devices  11.8 us (8%)
  Pallas kernels  11.4 us (8%)
    all_to_all x5, blocking collectives, trade(): return lax.all_to_all(x, axes, 0, 0, tiled=True)  83.3 us
    all_gather x1, waiting for transfers between devices, per_device(): far = lax.all_gather(chunk, 'z', axis=0, tiled=True)  26.7 us
    ppermute x3, starting transfers between devices, swap(): return lax.ppermute(x, axes, [(i, i ^ k) for i in range(size)])  11.7 us
    pallas_call x9, Pallas kernels, call(): pl.pallas_call(body, out_shape=outs, in_specs=[SMEM if a.shape == (3,) el...  11.4 us
  transfers between devices with their start and end apart: 4, of which 2 were waited for; matrix products, arithmetic and copies ran while one was open for 0% of the time, Pallas kernels for 2%

profile of v13, /device:TPU:1, one launch (start us, length us, event | category | flops | bytes accessed | tf_op | source)
XLA Modules:
  0.0 149.5 jit_solution(1551740053805122775)
XLA Ops:
  7.2 0.0 copy-start.1
  7.2 0.0 all-gather.2.cloned.1.call-start
  7.2 0.0 copy-start
  7.2 0.9 copy-done
  8.1 0.2 chunks.1
  8.3 24.1 %all_to_all.25.piece_ref = f32[32,24,128]{2,1,0:T(8,128)S(1)} all-to-all(f32[32,24,128]{2,1,0:T(8,128)S(1)} %get-tuple-element.15), channel_id=1, replica_groups=mesh['z'=8,'yh'=4,'core'=2,'yl'=2,'x'=4] {'yh','yl','x'}, dimensions={0} | all-to-all | bytes 786432 | tf_op jit(solution)/shard_map/all_to_all | solution.py:176
  32.4 1.0 columns.1.after_ref
  33.4 0.0 all-gather.2.cloned.1.call-update
  33.5 0.1 copies.1
  33.5 12.9 %all_to_all.26.piece_ref = f32[8,192,128]{2,1,0:T(8,128)S(1)} all-to-all(f32[8,192,128]{2,1,0:T(8,128)S(1)} %copies.1), channel_id=1, replica_groups=mesh['z'=8,'yh'=4,'core'=2,'yl'=2,'x'=4] {'yl','x'}, dimensions={0} | all-to-all | bytes 1572864 | tf_op jit(solution)/shard_map/all_to_all | solution.py:176
  46.4 0.5 norm.1
  46.9 5.9 %collective-permute-start = (f32[128,1536]{1,0:T(8,128)S(1)}, f32[128,1536]{1,0:T(8,128)S(1)}, u32[]{:S(2)}, u32[]{:S(2)}) collective-permute-start(f32[128,1536]{1,0:T(8,128)S(1)} %get-tuple-element.16.own_ref), channel_id=1, source_target_pairs={{0,8},{8,0},{1,9},{9,1},{2,10},{10,2},{3,11},{11,3},{4,12},{12,4},... | collective-permute-start | bytes 2359304 | tf_op jit(solution)/shard_map/ppermute | solution.py:172
  52.8 0.0 copy-done.1
  52.8 1.9 %collective-permute-start.1 = (s32[128]{0:T(128)S(1)}, s32[128]{0:T(128)S(1)}, u32[]{:S(2)}, u32[]{:S(2)}) collective-permute-start(s32[128]{0:T(128)S(1)} %copy-done.1), channel_id=1, source_target_pairs={{0,8},{8,0},{1,9},{9,1},{2,10},{10,2},{3,11},{11,3},{4,12},{12,4},... | collective-permute-start | bytes 1544 | tf_op jit(solution)/shard_map/ppermute | solution.py:172
  54.7 0.1 pad_add_fusion.pos_ref
  54.8 0.1 copy.4.ownp_ref.part_ref
  54.9 0.9 collective-permute-done.1
  55.8 0.1 copy.5.othp_ref.part_ref
  55.9 0.0 collective-permute-done.oth_ref
  55.9 0.2 rows.1
  56.2 26.7 %all-gather.2.cloned.1.call-done.far_ref = f32[512,1536]{1,0:T(8,128)} async-done(((f32[64,1536]{1,0:T(8,128)}), f32[512,1536]{1,0:T(8,128)}) %all-gather.2.cloned.1.call-update) | async-done | bytes 3145744 | tf_op jit(solution)/shard_map/all_gather | solution.py:201
  82.8 4.9 %scores.1 = (f32[256,512]{1,0:T(8,128)S(1)}, f32[16,8,128]{2,1,0:T(8,128)S(1)}, f32[32,8,128]{2,1,0:T(8,128)S(1)}, f32[512,1536]{1,0:T(8,128)S(1)}) custom-call(s32[3]{0:T(128)S(1)} %pad_add_fusion.pos_ref, bf16[256,1536]{1,0:T(8,128)(2,1)S(1)} %get-tuple-element.17.hi_ref, bf16[256,1536]{1,0:T(8,128)(2,1)S(1)} %get-tuple-element.18.lo_ref, ...), custom_call_target="tpu_custom_call" | custom-call | tf_op jit(solution)/shard_map/scores/pallas_call | solution.py:180
  87.7 11.5 %all_to_all.27.rows_ref = f32[16,8,128]{2,1,0:T(8,128)S(1)} all-to-all(f32[16,8,128]{2,1,0:T(8,128)S(1)} %get-tuple-element.21), channel_id=1, replica_groups=mesh['z'=8,'yh'=4,'core'=2,'yl'=2,'x'=4] {'core','yl','x'}, dimensions={0} | all-to-all | bytes 131072 | tf_op jit(solution)/shard_map/all_to_all | solution.py:176
  99.2 19.3 %all_to_all.28.cols_l_ref = f32[32,8,128]{2,1,0:T(8,128)S(1)} all-to-all(f32[32,8,128]{2,1,0:T(8,128)S(1)} %get-tuple-element.22), channel_id=1, replica_groups=mesh['z'=8,'yh'=4,'core'=2,'yl'=2,'x'=4] {'z','yh'}, dimensions={0} | all-to-all | bytes 262144 | tf_op jit(solution)/shard_map/all_to_all | solution.py:176
  118.5 1.9 %theirs.1 = f32[8,200,128]{2,1,0:T(8,128)S(1)} custom-call(s32[3]{0:T(128)S(1)} %pad_add_fusion.pos_ref, f32[256,512]{1,0:T(8,128)S(1)} %get-tuple-element.19.s_ref, f32[512,1536]{1,0:T(8,128)S(1)} %get-tuple-element.20.cols_ref, s32[128,1]{1,0:T(8,128)S(1)} %copy.5.othp_ref.part_ref, f32[16,8,128]{2,1,0:T(8,128)S(1)} %all_to_all.27.rows_ref, ...), custom_call_target="tpu_custom_call" | custom-call | tf_op jit(solution)/shard_map/theirs/pallas_call | solution.py:180
  120.5 3.9 %collective-permute-start.2 = (f32[8,200,128]{2,1,0:T(8,128)S(1)}, f32[8,200,128]{2,1,0:T(8,128)S(1)}, u32[]{:S(2)}, u32[]{:S(2)}) collective-permute-start(f32[8,200,128]{2,1,0:T(8,128)S(1)} %theirs.1), channel_id=1, source_target_pairs={{0,8},{8,0},{1,9},{9,1},{2,10},{10,2},{3,11},{11,3},{4,12},{12,4},... | collective-permute-start | bytes 2457608 | tf_op jit(solution)/shard_map/ppermute | solution.py:172
  124.4 1.9 %mine.1 = f32[8,200,128]{2,1,0:T(8,128)S(1)} custom-call(s32[3]{0:T(128)S(1)} %pad_add_fusion.pos_ref, f32[256,512]{1,0:T(8,128)S(1)} %get-tuple-element.19.s_ref, f32[512,1536]{1,0:T(8,128)S(1)} %get-tuple-element.20.cols_ref, s32[128,1]{1,0:T(8,128)S(1)} %copy.4.ownp_ref.part_ref, f32[16,8,128]{2,1,0:T(8,128)S(1)} %all_to_all.27.rows_ref, ...), custom_call_target="tpu_custom_call" | custom-call | tf_op jit(solution)/shard_map/mine/pallas_call | solution.py:180
  126.3 0.0 collective-permute-done.2
  126.3 0.1 add.11
  126.4 15.5 %all_to_all.29.piece_ref = f32[8,200,128]{2,1,0:T(8,128)S(1)} all-to-all(f32[8,200,128]{2,1,0:T(8,128)S(1)} %add.11), channel_id=1, replica_groups=mesh['z'=8,'yh'=4,'core'=2,'yl'=2,'x'=4] {'yl','x'}, dimensions={0} | all-to-all | bytes 1638400 | tf_op jit(solution)/shard_map/all_to_all | solution.py:176
  141.9 0.7 finish.1
Async XLA Ops:
  7.2 45.6 %copy-start.1 = (s32[128]{0:T(128)S(1)}, s32[128]{0:T(128)}, u32[]{:S(2)}) copy-start(s32[128]{0:T(128)} %param.3) | copy-start | bytes 1540
  7.2 75.7 %all-gather.2.cloned.1.call-start = ((), (), s32[]{:S(2)}) async-start(), calls=%async_computation.5 | async-start | bytes 3538944 | tf_op jit(solution)/shard_map/all_gather | solution.py:201
  7.2 0.9 copy-start
  46.9 9.1 %collective-permute-start = (f32[128,1536]{1,0:T(8,128)S(1)}, f32[128,1536]{1,0:T(8,128)S(1)}, u32[]{:S(2)}, u32[]{:S(2)}) collective-permute-start(f32[128,1536]{1,0:T(8,128)S(1)} %get-tuple-element.16.own_ref), channel_id=1, source_target_pairs={{0,8},{8,0},{1,9},{9,1},{2,10},{10,2},{3,11},{11,3},{4,12},{12,4},... | collective-permute-start | bytes 2359304 | tf_op jit(solution)/shard_map/ppermute | solution.py:172
  52.8 3.0 %collective-permute-start.1 = (s32[128]{0:T(128)S(1)}, s32[128]{0:T(128)S(1)}, u32[]{:S(2)}, u32[]{:S(2)}) collective-permute-start(s32[128]{0:T(128)S(1)} %copy-done.1), channel_id=1, source_target_pairs={{0,8},{8,0},{1,9},{9,1},{2,10},{10,2},{3,11},{11,3},{4,12},{12,4},... | collective-permute-start | bytes 1544 | tf_op jit(solution)/shard_map/ppermute | solution.py:172
  120.5 5.9 %collective-permute-start.2 = (f32[8,200,128]{2,1,0:T(8,128)S(1)}, f32[8,200,128]{2,1,0:T(8,128)S(1)}, u32[]{:S(2)}, u32[]{:S(2)}) collective-permute-start(f32[8,200,128]{2,1,0:T(8,128)S(1)} %theirs.1), channel_id=1, source_target_pairs={{0,8},{8,0},{1,9},{9,1},{2,10},{10,2},{3,11},{11,3},{4,12},{12,4},... | collective-permute-start | bytes 2457608 | tf_op jit(solution)/shard_map/ppermute | solution.py:172
Sparse Core Ops, SparseCore 0:
  33.6 49.2 all-gather.1

commit v14 on v11

--- a/solution.py
+++ b/solution.py
@@ -1,3 +1,5 @@
+import functools
+
 import jax
 import jax.numpy as jnp
 from jax import lax
@@ -152,35 +154,30 @@
         col_ref[k] = col
 
 
-def grad_kernel(pos_ref, s_ref, cols_ref, ownp_ref, othp_ref, rows_ref, cols_l_ref, mine_ref, theirs_ref, w_hi, w_lo):
+def grad_kernel(j, pos_ref, s_ref, cols_ref, part_ref, rows_ref, cols_l_ref, out_ref):
     core = pos_ref[1]
     row_l = jnp.sum(rows_ref[...], axis=0)
     col_l = jnp.sum(cols_l_ref[...], axis=0)
     nrow = NCOL // ROWS
     col_inv = jnp.concatenate([1.0 / col_l[c:c + 1, :] for c in range(nrow)], axis=1)
     loss = jnp.sum(jnp.log(col_l[:nrow, :]), axis=0, keepdims=True) - col_l[nrow:nrow + 1, :]
-    projs = []
-    for j, part in enumerate((ownp_ref, othp_ref)):
-        s = s_ref[j * ROWS:(j + 1) * ROWS, :]
-        half = core ^ j
-        diag, hit = tile_masks(pos_ref, half, part[...])
-        inv = column(1.0 / jnp.where(half == 0, row_l[0:1, :], row_l[1:2, :]))
-        w = jnp.where(diag, 0.0, jnp.exp(s) * (inv + col_inv)) - jnp.where(hit, 2.0, 0.0)
-        ws = w * s
-        lanes = sum(ws[:, c * ROWS:(c + 1) * ROWS] for c in range(NCOL // ROWS))
-        projs.append(jnp.sum(lanes.T, axis=0, keepdims=True))
-        w_hi[j], w_lo[j] = split(w)
-    weights = (w_hi[...].reshape(NC * ROWS, NCOL), w_lo[...].reshape(NC * ROWS, NCOL))
+    s = s_ref[j * ROWS:(j + 1) * ROWS, :]
+    half = core ^ j
+    diag, hit = tile_masks(pos_ref, half, part_ref[...])
+    inv = column(1.0 / jnp.where(half == 0, row_l[0:1, :], row_l[1:2, :]))
+    w = jnp.where(diag, 0.0, jnp.exp(s) * (inv + col_inv)) - jnp.where(hit, 2.0, 0.0)
+    ws = w * s
+    lanes = sum(ws[:, c * ROWS:(c + 1) * ROWS] for c in range(NCOL // ROWS))
+    proj = jnp.sum(lanes.T, axis=0, keepdims=True)
+    weights = split(w)
     step = 4 * FEAT
-    tails = [jnp.concatenate([loss, proj, jnp.zeros((6, ROWS), jnp.float32)], axis=0) for proj in projs]
+    tail = jnp.concatenate([loss, proj, jnp.zeros((6, ROWS), jnp.float32)], axis=0)
     for c in range(WIDE // step):
         at = slice(c * step, (c + 1) * step)
-        g = INV_TAU * dot3(weights, split(cols_ref[:, at]), ((1,), (0,)))
-        for j, out in enumerate((mine_ref, theirs_ref)):
-            t = g[j * ROWS:(j + 1) * ROWS, :].T
-            for p in range(4):
-                out[4 * c + p, :FEAT, :] = t[p * FEAT:(p + 1) * FEAT, :]
-                out[4 * c + p, FEAT:, :] = tails[j]
+        t = (INV_TAU * dot3(weights, split(cols_ref[:, at]), ((1,), (0,)))).T
+        for p in range(4):
+            out_ref[4 * c + p, :FEAT, :] = t[p * FEAT:(p + 1) * FEAT, :]
+            out_ref[4 * c + p, FEAT:, :] = tail
 
 
 def last_kernel(piece_ref, scale_ref, view_ref, loss_ref, grad_ref):
@@ -250,11 +247,9 @@
     )
     rows_l = trade(row, ("core", "yl", "x"))
     cols_l = trade(col, ("z", "yh"))
-    mine, theirs = call(
-        grad_kernel, "gradient",
-        [f32(NF, PIECE, ROWS)] * 2,
-        [pos, s, cols, own_p, oth_p, rows_l, cols_l],
-        [pltpu.VMEM((NC, ROWS, NCOL), jnp.bfloat16)] * 2,
+    theirs, mine = (
+        call(functools.partial(grad_kernel, j), name, [f32(NF, PIECE, ROWS)], [pos, s, cols, part, rows_l, cols_l])[0]
+        for j, name, part in ((1, "theirs", oth_p), (0, "mine", own_p))
     )
     pieces = trade(mine + swap(theirs, "core", NC, 1), feat)
     loss, grad = call(last_kernel, "finish", [f32(1, 1), f32(FEAT, ROWS)], [pieces, scale, copy])

time: 151 us -> 150 us (level)
  waiting for transfers between devices: 21.4 us -> 19.5 us
    ppermute x1, waiting for transfers between devices: 1.94 us -> 0.01 us  [swap(): return lax.ppermute(x, axes, [(i, i ^ k) for i in range(size)])]
    pallas_call x7 -> x8, Pallas kernels: 9.53 us -> 10.9 us  [call(): pl.pallas_call(body, out_shape=outs, in_specs=[SMEM if a.shape == (3,) el...]
  transfers between devices with their start and end apart: 10 -> 10, of which waited for: 5 -> 4; matrix products, arithmetic and copies ran while one was open for 1% -> 1% of each run, Pallas kernels for 2% -> 4%
where the time goes in v14:
time: 150 us; the launch traced here: 149 us
  blocking collectives  70.1 us (47%)
  starting transfers between devices  31 us (21%)
  waiting for transfers between devices  19.5 us (13%)
  between operations  14.2 us (9%)
  Pallas kernels  10.9 us (7%)
  local copies, waits for them, and re-layouts  3.67 us (2%)
    all_to_all x4, blocking collectives, trade(): return lax.all_to_all(x, axes, 0, 0, tiled=True)  70.1 us
    ppermute x6, starting transfers between devices, around(): got = (lax.ppermute(b[-1], 'z', pair), lax.ppermute(a[-1], 'z', between))  22.1 us
    ppermute x6, waiting for transfers between devices, around(): got = (lax.ppermute(b[-1], 'z', pair), lax.ppermute(a[-1], 'z', between))  19.5 us
    pallas_call x8, Pallas kernels, call(): pl.pallas_call(body, out_shape=outs, in_specs=[SMEM if a.shape == (3,) el...  10.9 us
    ppermute x1, starting transfers between devices, swap(): return lax.ppermute(x, axes, [(i, i ^ k) for i in range(size)])  3.92 us
    ppermute x1, starting transfers between devices, around(): lax.ppermute(a[-1][HALF:], 'z', between)  3.01 us
  transfers between devices with their start and end apart: 10, of which 4 were waited for; matrix products, arithmetic and copies ran while one was open for 1% of the time, Pallas kernels for 4%

profile of v14, /device:TPU:1, one launch (start us, length us, event | category | flops | bytes accessed | tf_op | source)
XLA Modules:
  0.0 149.5 jit_solution(11903093838919949957)
XLA Ops:
  7.2 0.0 all-gather.2.cloned.1.call-start
  7.2 0.0 copy-start.1
  7.2 0.9 copy-done.1
  8.1 0.2 chunks.1
  8.3 24.1 %all_to_all.20.piece_ref = f32[32,24,128]{2,1,0:T(8,128)S(1)} all-to-all(f32[32,24,128]{2,1,0:T(8,128)S(1)} %get-tuple-element.17), channel_id=1, replica_groups=mesh['z'=8,'yh'=4,'core'=2,'yl'=2,'x'=4] {'yh','yl','x'}, dimensions={0} | all-to-all | bytes 786432 | tf_op jit(solution)/shard_map/all_to_all | solution.py:207
  32.4 0.0 copy-start.2
  32.4 0.7 copy-done.2
  33.0 0.9 columns.1
  33.9 0.0 all-gather.2.cloned.1.call-update
  33.9 10.7 %collective-permute-start.1 = (f32[64,1536]{1,0:T(8,128)S(1)}, f32[64,1536]{1,0:T(8,128)S(1)}, u32[]{:S(2)}, u32[]{:S(2)}) collective-permute-start(f32[64,1536]{1,0:T(8,128)S(1)} %get-tuple-element.24.refs_0_), channel_id=1, source_target_pairs={{0,448},{64,128},{128,64},{192,256},{256,192},{320,384},{384,320},... | collective-permute-start | bytes 1179656 | tf_op jit(solution)/shard_map/ppermute | solution.py:199
  44.6 1.9 %collective-permute-start = (f32[64,1536]{1,0:T(8,128)S(1)}, f32[64,1536]{1,0:T(8,128)S(1)}, u32[]{:S(2)}, u32[]{:S(2)}) collective-permute-start(f32[64,1536]{1,0:T(8,128)S(1)} %get-tuple-element.24.refs_0_), channel_id=1, source_target_pairs={{0,64},{64,0},{128,192},{192,128},{256,320},{320,256},{384,448},{4... | collective-permute-start | bytes 1179656 | tf_op jit(solution)/shard_map/ppermute | solution.py:199
  46.5 5.0 %collective-permute-done.1.refs_4_ = f32[64,1536]{1,0:T(8,128)S(1)} collective-permute-done((f32[64,1536]{1,0:T(8,128)S(1)}, f32[64,1536]{1,0:T(8,128)S(1)}, u32[]{:S(2)}, u32[]{:S(2)}) %collective-permute-start.1) | collective-permute-done | bytes 393248 | tf_op jit(solution)/shard_map/ppermute | solution.py:199
  51.5 1.9 %collective-permute-start.2 = (f32[64,1536]{1,0:T(8,128)S(1)}, f32[64,1536]{1,0:T(8,128)S(1)}, u32[]{:S(2)}, u32[]{:S(2)}) collective-permute-start(f32[64,1536]{1,0:T(8,128)S(1)} %collective-permute-done.1.refs_4_), channel_id=1, source_target_pairs={{0,64},{64,0},{128,192},{192,128},{256,320},{320,256},{384,448},{4... | collective-permute-start | bytes 1179656 | tf_op jit(solution)/shard_map/ppermute | solution.py:199
  53.4 0.9 collective-permute-done.refs_1_
  54.3 3.4 %collective-permute-start.3 = (f32[64,1536]{1,0:T(8,128)S(1)}, f32[64,1536]{1,0:T(8,128)S(1)}, u32[]{:S(2)}, u32[]{:S(2)}) collective-permute-start(f32[64,1536]{1,0:T(8,128)S(1)} %collective-permute-done.refs_1_), channel_id=1, source_target_pairs={{0,448},{64,128},{128,64},{192,256},{256,192},{320,384},{384,320},... | collective-permute-start | bytes 1179656 | tf_op jit(solution)/shard_map/ppermute | solution.py:199
  57.7 6.2 %collective-permute-done.2.refs_2_ = f32[64,1536]{1,0:T(8,128)S(1)} collective-permute-done((f32[64,1536]{1,0:T(8,128)S(1)}, f32[64,1536]{1,0:T(8,128)S(1)}, u32[]{:S(2)}, u32[]{:S(2)}) %collective-permute-start.2) | collective-permute-done | bytes 393248 | tf_op jit(solution)/shard_map/ppermute | solution.py:199
  63.9 1.9 %collective-permute-start.5 = (f32[64,1536]{1,0:T(8,128)S(1)}, f32[64,1536]{1,0:T(8,128)S(1)}, u32[]{:S(2)}, u32[]{:S(2)}) collective-permute-start(f32[64,1536]{1,0:T(8,128)S(1)} %collective-permute-done.2.refs_2_), channel_id=1, source_target_pairs={{0,448},{64,128},{128,64},{192,256},{256,192},{320,384},{384,320},... | collective-permute-start | bytes 1179656 | tf_op jit(solution)/shard_map/ppermute | solution.py:199
  65.8 0.0 collective-permute-done.3.refs_5_
  65.8 2.3 %collective-permute-start.4 = (f32[64,1536]{1,0:T(8,128)S(1)}, f32[64,1536]{1,0:T(8,128)S(1)}, u32[]{:S(2)}, u32[]{:S(2)}) collective-permute-start(f32[64,1536]{1,0:T(8,128)S(1)} %collective-permute-done.3.refs_5_), channel_id=1, source_target_pairs={{0,64},{64,0},{128,192},{192,128},{256,320},{320,256},{384,448},{4... | collective-permute-start | bytes 1179656 | tf_op jit(solution)/shard_map/ppermute | solution.py:199
  68.1 7.4 %collective-permute-done.5.refs_6_ = f32[64,1536]{1,0:T(8,128)S(1)} collective-permute-done((f32[64,1536]{1,0:T(8,128)S(1)}, f32[64,1536]{1,0:T(8,128)S(1)}, u32[]{:S(2)}, u32[]{:S(2)}) %collective-permute-start.5) | collective-permute-done | bytes 393248 | tf_op jit(solution)/shard_map/ppermute | solution.py:199
  75.6 1.9 %collective-permute-start.6 = (f32[32,1536]{1,0:T(8,128)S(1)}, f32[32,1536]{1,0:T(8,128)S(1)}, u32[]{:S(2)}, u32[]{:S(2)}) collective-permute-start(f32[32,1536]{1,0:T(8,128)S(1)} %slice.8), channel_id=1, source_target_pairs={{0,64},{64,0},{128,192},{192,128},{256,320},{320,256},{384,448},{4... | collective-permute-start | bytes 589832 | tf_op jit(solution)/shard_map/ppermute | solution.py:202
  77.5 0.0 collective-permute-done.4.refs_3_
  77.5 0.7 slice.9
  78.2 3.0 %collective-permute-start.7 = (f32[32,1536]{1,0:T(8,128)}, f32[32,1536]{1,0:T(8,128)S(1)}, u32[]{:S(2)}, u32[]{:S(2)}) collective-permute-start(f32[32,1536]{1,0:T(8,128)} %slice.9), channel_id=1, source_target_pairs={{0,448},{64,128},{128,64},{192,256},{256,192},{320,384},{384,320},... | collective-permute-start | bytes 589832 | tf_op jit(solution)/shard_map/ppermute | solution.py:202
  81.2 0.1 pad_add_fusion.pos_ref
  81.3 0.0 all-gather.2.cloned.1.call-done
  81.3 0.0 copy-start
  81.3 1.4 copy-done
  82.7 1.3 norm.1
  84.0 2.2 %early.1.early_ref = f32[256,512]{1,0:T(8,128)S(1)} custom-call(s32[3]{0:T(128)S(1)} %pad_add_fusion.pos_ref, bf16[256,1536]{1,0:T(8,128)(2,1)S(1)} %get-tuple-element.20.hi_ref, bf16[256,1536]{1,0:T(8,128)(2,1)S(1)} %get-tuple-element.21.lo_ref, f32[64,1536]{1,0:T(8,128)S(1)} %get-tuple-element.24.refs_0_, f32[64,1536]{1,0:T(8,128)S(1)} %collective-permute-done.refs_1_, ...), custom_call_target="tpu_custom_call" | custom-call | tf_op jit(solution)/shard_map/early/pallas_call | solution.py:211
  86.2 0.0 collective-permute-done.6.refs_7_
  86.2 0.0 collective-permute-done.7.refs_8_
  86.3 1.8 %scores.1 = (f32[256,512]{1,0:T(8,128)S(1)}, f32[16,8,128]{2,1,0:T(8,128)S(1)}, f32[32,8,128]{2,1,0:T(8,128)S(1)}, f32[512,1536]{1,0:T(8,128)S(1)}) custom-call(s32[3]{0:T(128)S(1)} %pad_add_fusion.pos_ref, bf16[256,1536]{1,0:T(8,128)(2,1)S(1)} %get-tuple-element.20.hi_ref, bf16[256,1536]{1,0:T(8,128)(2,1)S(1)} %get-tuple-element.21.lo_ref, ...), custom_call_target="tpu_custom_call" | custom-call | tf_op jit(solution)/shard_map/scores/pallas_call | solution.py:211
  88.1 14.2 %all_to_all.21.rows_ref = f32[16,8,128]{2,1,0:T(8,128)S(1)} all-to-all(f32[16,8,128]{2,1,0:T(8,128)S(1)} %get-tuple-element.27), channel_id=1, replica_groups=mesh['z'=8,'yh'=4,'core'=2,'yl'=2,'x'=4] {'core','yl','x'}, dimensions={0} | all-to-all | bytes 131072 | tf_op jit(solution)/shard_map/all_to_all | solution.py:207
  102.3 16.3 %all_to_all.22.cols_l_ref = f32[32,8,128]{2,1,0:T(8,128)S(1)} all-to-all(f32[32,8,128]{2,1,0:T(8,128)S(1)} %get-tuple-element.28), channel_id=1, replica_groups=mesh['z'=8,'yh'=4,'core'=2,'yl'=2,'x'=4] {'z','yh'}, dimensions={0} | all-to-all | bytes 262144 | tf_op jit(solution)/shard_map/all_to_all | solution.py:207
  118.5 1.9 %theirs.1 = f32[8,200,128]{2,1,0:T(8,128)S(1)} custom-call(s32[3]{0:T(128)S(1)} %pad_add_fusion.pos_ref, f32[256,512]{1,0:T(8,128)S(1)} %get-tuple-element.25.s_ref, f32[512,1536]{1,0:T(8,128)S(1)} %get-tuple-element.26.cols_ref, s32[128,1]{1,0:T(8,128)S(1)} %get-tuple-element.23.othp_ref.part_ref, f32[16,8,128]{2,1,0:T(8,128)S(1)} %all_to_all.21.rows_ref, ...), custom_call_target="tpu_custom_call" | custom-call | tf_op jit(solution)/shard_map/theirs/pallas_call | solution.py:211
  120.5 3.9 %collective-permute-start.8 = (f32[8,200,128]{2,1,0:T(8,128)S(1)}, f32[8,200,128]{2,1,0:T(8,128)S(1)}, u32[]{:S(2)}, u32[]{:S(2)}) collective-permute-start(f32[8,200,128]{2,1,0:T(8,128)S(1)} %theirs.1), channel_id=1, source_target_pairs={{0,8},{8,0},{1,9},{9,1},{2,10},{10,2},{3,11},{11,3},{4,12},{12,4},... | collective-permute-start | bytes 2457608 | tf_op jit(solution)/shard_map/ppermute | solution.py:191
  124.4 1.9 %mine.1 = f32[8,200,128]{2,1,0:T(8,128)S(1)} custom-call(s32[3]{0:T(128)S(1)} %pad_add_fusion.pos_ref, f32[256,512]{1,0:T(8,128)S(1)} %get-tuple-element.25.s_ref, f32[512,1536]{1,0:T(8,128)S(1)} %get-tuple-element.26.cols_ref, s32[128,1]{1,0:T(8,128)S(1)} %get-tuple-element.22.ownp_ref.part_ref, f32[16,8,128]{2,1,0:T(8,128)S(1)} %all_to_all.21.rows_ref, ...), custom_call_target="tpu_custom_call" | custom-call | tf_op jit(solution)/shard_map/mine/pallas_call | solution.py:211
  126.3 0.0 collective-permute-done.8
  126.3 0.1 add.11
  126.4 15.5 %all_to_all.23.piece_ref = f32[8,200,128]{2,1,0:T(8,128)S(1)} all-to-all(f32[8,200,128]{2,1,0:T(8,128)S(1)} %add.11), channel_id=1, replica_groups=mesh['z'=8,'yh'=4,'core'=2,'yl'=2,'x'=4] {'yl','x'}, dimensions={0} | all-to-all | bytes 1638400 | tf_op jit(solution)/shard_map/all_to_all | solution.py:207
  141.9 0.7 finish.1
  (1 shorter events, 0.0 us)
Async XLA Ops:
  7.2 74.1 %all-gather.2.cloned.1.call-start = ((), (), s32[]{:S(2)}) async-start(), calls=%async_computation.4 | async-start | bytes 1740800 | tf_op jit(solution)/shard_map/all_gather | solution.py:233
  7.2 0.9 copy-start.1
  32.4 0.7 copy-start.2
  33.9 17.6 %collective-permute-start.1 = (f32[64,1536]{1,0:T(8,128)S(1)}, f32[64,1536]{1,0:T(8,128)S(1)}, u32[]{:S(2)}, u32[]{:S(2)}) collective-permute-start(f32[64,1536]{1,0:T(8,128)S(1)} %get-tuple-element.24.refs_0_), channel_id=1, source_target_pairs={{0,448},{64,128},{128,64},{192,256},{256,192},{320,384},{384,320},... | collective-permute-start | bytes 1179656 | tf_op jit(solution)/shard_map/ppermute | solution.py:199
  44.6 9.7 %collective-permute-start = (f32[64,1536]{1,0:T(8,128)S(1)}, f32[64,1536]{1,0:T(8,128)S(1)}, u32[]{:S(2)}, u32[]{:S(2)}) collective-permute-start(f32[64,1536]{1,0:T(8,128)S(1)} %get-tuple-element.24.refs_0_), channel_id=1, source_target_pairs={{0,64},{64,0},{128,192},{192,128},{256,320},{320,256},{384,448},{4... | collective-permute-start | bytes 1179656 | tf_op jit(solution)/shard_map/ppermute | solution.py:199
  51.5 12.4 %collective-permute-start.2 = (f32[64,1536]{1,0:T(8,128)S(1)}, f32[64,1536]{1,0:T(8,128)S(1)}, u32[]{:S(2)}, u32[]{:S(2)}) collective-permute-start(f32[64,1536]{1,0:T(8,128)S(1)} %collective-permute-done.1.refs_4_), channel_id=1, source_target_pairs={{0,64},{64,0},{128,192},{192,128},{256,320},{320,256},{384,448},{4... | collective-permute-start | bytes 1179656 | tf_op jit(solution)/shard_map/ppermute | solution.py:199
  54.3 11.5 %collective-permute-start.3 = (f32[64,1536]{1,0:T(8,128)S(1)}, f32[64,1536]{1,0:T(8,128)S(1)}, u32[]{:S(2)}, u32[]{:S(2)}) collective-permute-start(f32[64,1536]{1,0:T(8,128)S(1)} %collective-permute-done.refs_1_), channel_id=1, source_target_pairs={{0,448},{64,128},{128,64},{192,256},{256,192},{320,384},{384,320},... | collective-permute-start | bytes 1179656 | tf_op jit(solution)/shard_map/ppermute | solution.py:199
  63.9 11.6 %collective-permute-start.5 = (f32[64,1536]{1,0:T(8,128)S(1)}, f32[64,1536]{1,0:T(8,128)S(1)}, u32[]{:S(2)}, u32[]{:S(2)}) collective-permute-start(f32[64,1536]{1,0:T(8,128)S(1)} %collective-permute-done.2.refs_2_), channel_id=1, source_target_pairs={{0,448},{64,128},{128,64},{192,256},{256,192},{320,384},{384,320},... | collective-permute-start | bytes 1179656 | tf_op jit(solution)/shard_map/ppermute | solution.py:199
  65.8 11.7 %collective-permute-start.4 = (f32[64,1536]{1,0:T(8,128)S(1)}, f32[64,1536]{1,0:T(8,128)S(1)}, u32[]{:S(2)}, u32[]{:S(2)}) collective-permute-start(f32[64,1536]{1,0:T(8,128)S(1)} %collective-permute-done.3.refs_5_), channel_id=1, source_target_pairs={{0,64},{64,0},{128,192},{192,128},{256,320},{320,256},{384,448},{4... | collective-permute-start | bytes 1179656 | tf_op jit(solution)/shard_map/ppermute | solution.py:199
  75.6 10.7 %collective-permute-start.6 = (f32[32,1536]{1,0:T(8,128)S(1)}, f32[32,1536]{1,0:T(8,128)S(1)}, u32[]{:S(2)}, u32[]{:S(2)}) collective-permute-start(f32[32,1536]{1,0:T(8,128)S(1)} %slice.8), channel_id=1, source_target_pairs={{0,64},{64,0},{128,192},{192,128},{256,320},{320,256},{384,448},{4... | collective-permute-start | bytes 589832 | tf_op jit(solution)/shard_map/ppermute | solution.py:202
  78.2 8.1 %collective-permute-start.7 = (f32[32,1536]{1,0:T(8,128)}, f32[32,1536]{1,0:T(8,128)S(1)}, u32[]{:S(2)}, u32[]{:S(2)}) collective-permute-start(f32[32,1536]{1,0:T(8,128)} %slice.9), channel_id=1, source_target_pairs={{0,448},{64,128},{128,64},{192,256},{256,192},{320,384},{384,320},... | collective-permute-start | bytes 589832 | tf_op jit(solution)/shard_map/ppermute | solution.py:202
  81.3 1.4 copy-start
  120.5 5.9 %collective-permute-start.8 = (f32[8,200,128]{2,1,0:T(8,128)S(1)}, f32[8,200,128]{2,1,0:T(8,128)S(1)}, u32[]{:S(2)}, u32[]{:S(2)}) collective-permute-start(f32[8,200,128]{2,1,0:T(8,128)S(1)} %theirs.1), channel_id=1, source_target_pairs={{0,8},{8,0},{1,9},{9,1},{2,10},{10,2},{3,11},{11,3},{4,12},{12,4},... | collective-permute-start | bytes 2457608 | tf_op jit(solution)/shard_map/ppermute | solution.py:191
Sparse Core Ops, SparseCore 0:
  34.0 39.6 all-gather.1

commit v15 on v13

--- a/solution.py
+++ b/solution.py
@@ -98,7 +98,7 @@
 
 def score_kernel(pos_ref, hi_ref, lo_ref, ownp_ref, othp_ref, far_ref, s_ref, row_ref, col_ref, cols_ref, sems):
     core = pos_ref[1]
-    step = 256
+    step = 128
     copies = []
     for i in range(NCOL // step):
         at = pl.ds(i * step, step)
@@ -209,7 +209,7 @@
         score_kernel, "scores",
         [f32(NC * ROWS, NCOL), f32(NC * NF, 8, ROWS), f32(NZ * NYH, 8, ROWS), f32(NCOL, WIDE)],
         [pos, hi, lo, own_p, oth_p, far],
-        [pltpu.SemaphoreType.DMA((NCOL // 256,))],
+        [pltpu.SemaphoreType.DMA((NCOL // 128,))],
         far=(5,), limit=48,
     )
     rows_l = trade(row, ("core", "yl", "x"))

time: 150 us -> 152 us (1.013)
  Pallas kernels: 11.4 us -> 13.8 us
    pallas_call x9, Pallas kernels: 11.4 us -> 13.8 us  [call(): pl.pallas_call(body, out_shape=outs, in_specs=[SMEM if a.shape == (3,) el...]
where the time goes in v15:
time: 152 us
  blocking collectives  83.3 us (55%)
  waiting for transfers between devices  27.6 us (18%)
  between operations  14.1 us (9%)
  Pallas kernels  13.8 us (9%)
  starting transfers between devices  11.8 us (8%)
    all_to_all x5, blocking collectives, trade(): return lax.all_to_all(x, axes, 0, 0, tiled=True)  83.3 us
    all_gather x1, waiting for transfers between devices, per_device(): far = lax.all_gather(chunk, 'z', axis=0, tiled=True)  26.7 us
    pallas_call x9, Pallas kernels, call(): pl.pallas_call(body, out_shape=outs, in_specs=[SMEM if a.shape == (3,) el...  13.8 us
    ppermute x3, starting transfers between devices, swap(): return lax.ppermute(x, axes, [(i, i ^ k) for i in range(size)])  11.7 us
  transfers between devices with their start and end apart: 4, of which 2 were waited for; matrix products, arithmetic and copies ran while one was open for 0% of the time, Pallas kernels for 2%

profile of v15, /device:TPU:1, one launch (start us, length us, event | category | flops | bytes accessed | tf_op | source)
XLA Modules:
  0.0 151.9 jit_solution(18169419452112132133)
XLA Ops:
  7.2 0.0 copy-start.1
  7.2 0.0 all-gather.2.cloned.1.call-start
  7.2 0.0 copy-start
  7.2 0.9 copy-done
  8.1 0.2 chunks.1
  8.3 24.1 %all_to_all.25.piece_ref = f32[32,24,128]{2,1,0:T(8,128)S(1)} all-to-all(f32[32,24,128]{2,1,0:T(8,128)S(1)} %get-tuple-element.15), channel_id=1, replica_groups=mesh['z'=8,'yh'=4,'core'=2,'yl'=2,'x'=4] {'yh','yl','x'}, dimensions={0} | all-to-all | bytes 786432 | tf_op jit(solution)/shard_map/all_to_all | solution.py:176
  32.4 1.0 columns.1.after_ref
  33.4 0.0 all-gather.2.cloned.1.call-update
  33.5 0.1 copies.1
  33.5 12.9 %all_to_all.26.piece_ref = f32[8,192,128]{2,1,0:T(8,128)S(1)} all-to-all(f32[8,192,128]{2,1,0:T(8,128)S(1)} %copies.1), channel_id=1, replica_groups=mesh['z'=8,'yh'=4,'core'=2,'yl'=2,'x'=4] {'yl','x'}, dimensions={0} | all-to-all | bytes 1572864 | tf_op jit(solution)/shard_map/all_to_all | solution.py:176
  46.4 0.5 norm.1
  46.9 5.9 %collective-permute-start = (f32[128,1536]{1,0:T(8,128)S(1)}, f32[128,1536]{1,0:T(8,128)S(1)}, u32[]{:S(2)}, u32[]{:S(2)}) collective-permute-start(f32[128,1536]{1,0:T(8,128)S(1)} %get-tuple-element.16.own_ref), channel_id=1, source_target_pairs={{0,8},{8,0},{1,9},{9,1},{2,10},{10,2},{3,11},{11,3},{4,12},{12,4},... | collective-permute-start | bytes 2359304 | tf_op jit(solution)/shard_map/ppermute | solution.py:172
  52.8 0.0 copy-done.1
  52.8 1.9 %collective-permute-start.1 = (s32[128]{0:T(128)S(1)}, s32[128]{0:T(128)S(1)}, u32[]{:S(2)}, u32[]{:S(2)}) collective-permute-start(s32[128]{0:T(128)S(1)} %copy-done.1), channel_id=1, source_target_pairs={{0,8},{8,0},{1,9},{9,1},{2,10},{10,2},{3,11},{11,3},{4,12},{12,4},... | collective-permute-start | bytes 1544 | tf_op jit(solution)/shard_map/ppermute | solution.py:172
  54.7 0.1 pad_add_fusion.pos_ref
  54.8 0.1 copy.4.ownp_ref.part_ref
  54.9 0.9 collective-permute-done.1
  55.8 0.1 copy.5.othp_ref.part_ref
  55.9 0.0 collective-permute-done.oth_ref
  55.9 0.2 rows.1
  56.2 26.7 %all-gather.2.cloned.1.call-done.far_ref = f32[512,1536]{1,0:T(8,128)} async-done(((f32[64,1536]{1,0:T(8,128)}), f32[512,1536]{1,0:T(8,128)}) %all-gather.2.cloned.1.call-update) | async-done | bytes 3145744 | tf_op jit(solution)/shard_map/all_gather | solution.py:201
  82.8 7.3 %scores.1 = (f32[256,512]{1,0:T(8,128)S(1)}, f32[16,8,128]{2,1,0:T(8,128)S(1)}, f32[32,8,128]{2,1,0:T(8,128)S(1)}, f32[512,1536]{1,0:T(8,128)S(1)}) custom-call(s32[3]{0:T(128)S(1)} %pad_add_fusion.pos_ref, bf16[256,1536]{1,0:T(8,128)(2,1)S(1)} %get-tuple-element.17.hi_ref, bf16[256,1536]{1,0:T(8,128)(2,1)S(1)} %get-tuple-element.18.lo_ref, ...), custom_call_target="tpu_custom_call" | custom-call | tf_op jit(solution)/shard_map/scores/pallas_call | solution.py:180
  90.1 11.5 %all_to_all.27.rows_ref = f32[16,8,128]{2,1,0:T(8,128)S(1)} all-to-all(f32[16,8,128]{2,1,0:T(8,128)S(1)} %get-tuple-element.21), channel_id=1, replica_groups=mesh['z'=8,'yh'=4,'core'=2,'yl'=2,'x'=4] {'core','yl','x'}, dimensions={0} | all-to-all | bytes 131072 | tf_op jit(solution)/shard_map/all_to_all | solution.py:176
  101.6 19.3 %all_to_all.28.cols_l_ref = f32[32,8,128]{2,1,0:T(8,128)S(1)} all-to-all(f32[32,8,128]{2,1,0:T(8,128)S(1)} %get-tuple-element.22), channel_id=1, replica_groups=mesh['z'=8,'yh'=4,'core'=2,'yl'=2,'x'=4] {'z','yh'}, dimensions={0} | all-to-all | bytes 262144 | tf_op jit(solution)/shard_map/all_to_all | solution.py:176
  120.9 1.9 %theirs.1 = f32[8,200,128]{2,1,0:T(8,128)S(1)} custom-call(s32[3]{0:T(128)S(1)} %pad_add_fusion.pos_ref, f32[256,512]{1,0:T(8,128)S(1)} %get-tuple-element.19.s_ref, f32[512,1536]{1,0:T(8,128)S(1)} %get-tuple-element.20.cols_ref, s32[128,1]{1,0:T(8,128)S(1)} %copy.5.othp_ref.part_ref, f32[16,8,128]{2,1,0:T(8,128)S(1)} %all_to_all.27.rows_ref, ...), custom_call_target="tpu_custom_call" | custom-call | tf_op jit(solution)/shard_map/theirs/pallas_call | solution.py:180
  122.9 3.9 %collective-permute-start.2 = (f32[8,200,128]{2,1,0:T(8,128)S(1)}, f32[8,200,128]{2,1,0:T(8,128)S(1)}, u32[]{:S(2)}, u32[]{:S(2)}) collective-permute-start(f32[8,200,128]{2,1,0:T(8,128)S(1)} %theirs.1), channel_id=1, source_target_pairs={{0,8},{8,0},{1,9},{9,1},{2,10},{10,2},{3,11},{11,3},{4,12},{12,4},... | collective-permute-start | bytes 2457608 | tf_op jit(solution)/shard_map/ppermute | solution.py:172
  126.8 1.9 %mine.1 = f32[8,200,128]{2,1,0:T(8,128)S(1)} custom-call(s32[3]{0:T(128)S(1)} %pad_add_fusion.pos_ref, f32[256,512]{1,0:T(8,128)S(1)} %get-tuple-element.19.s_ref, f32[512,1536]{1,0:T(8,128)S(1)} %get-tuple-element.20.cols_ref, s32[128,1]{1,0:T(8,128)S(1)} %copy.4.ownp_ref.part_ref, f32[16,8,128]{2,1,0:T(8,128)S(1)} %all_to_all.27.rows_ref, ...), custom_call_target="tpu_custom_call" | custom-call | tf_op jit(solution)/shard_map/mine/pallas_call | solution.py:180
  128.7 0.0 collective-permute-done.2
  128.7 0.1 add.11
  128.8 15.5 %all_to_all.29.piece_ref = f32[8,200,128]{2,1,0:T(8,128)S(1)} all-to-all(f32[8,200,128]{2,1,0:T(8,128)S(1)} %add.11), channel_id=1, replica_groups=mesh['z'=8,'yh'=4,'core'=2,'yl'=2,'x'=4] {'yl','x'}, dimensions={0} | all-to-all | bytes 1638400 | tf_op jit(solution)/shard_map/all_to_all | solution.py:176
  144.3 0.7 finish.1
Async XLA Ops:
  7.2 45.6 %copy-start.1 = (s32[128]{0:T(128)S(1)}, s32[128]{0:T(128)}, u32[]{:S(2)}) copy-start(s32[128]{0:T(128)} %param.3) | copy-start | bytes 1540
  7.2 75.7 %all-gather.2.cloned.1.call-start = ((), (), s32[]{:S(2)}) async-start(), calls=%async_computation.5 | async-start | bytes 3538944 | tf_op jit(solution)/shard_map/all_gather | solution.py:201
  7.2 0.9 copy-start
  46.9 9.1 %collective-permute-start = (f32[128,1536]{1,0:T(8,128)S(1)}, f32[128,1536]{1,0:T(8,128)S(1)}, u32[]{:S(2)}, u32[]{:S(2)}) collective-permute-start(f32[128,1536]{1,0:T(8,128)S(1)} %get-tuple-element.16.own_ref), channel_id=1, source_target_pairs={{0,8},{8,0},{1,9},{9,1},{2,10},{10,2},{3,11},{11,3},{4,12},{12,4},... | collective-permute-start | bytes 2359304 | tf_op jit(solution)/shard_map/ppermute | solution.py:172
  52.8 3.0 %collective-permute-start.1 = (s32[128]{0:T(128)S(1)}, s32[128]{0:T(128)S(1)}, u32[]{:S(2)}, u32[]{:S(2)}) collective-permute-start(s32[128]{0:T(128)S(1)} %copy-done.1), channel_id=1, source_target_pairs={{0,8},{8,0},{1,9},{9,1},{2,10},{10,2},{3,11},{11,3},{4,12},{12,4},... | collective-permute-start | bytes 1544 | tf_op jit(solution)/shard_map/ppermute | solution.py:172
  122.9 5.9 %collective-permute-start.2 = (f32[8,200,128]{2,1,0:T(8,128)S(1)}, f32[8,200,128]{2,1,0:T(8,128)S(1)}, u32[]{:S(2)}, u32[]{:S(2)}) collective-permute-start(f32[8,200,128]{2,1,0:T(8,128)S(1)} %theirs.1), channel_id=1, source_target_pairs={{0,8},{8,0},{1,9},{9,1},{2,10},{10,2},{3,11},{11,3},{4,12},{12,4},... | collective-permute-start | bytes 2457608 | tf_op jit(solution)/shard_map/ppermute | solution.py:172
Sparse Core Ops, SparseCore 0:
  33.6 49.2 all-gather.1
